TPU v7x, 768 devices: a whole 4x8x12 slice. The times are simulated.
768 devices in a mesh: expert: 16 (over y, core), dp: 48 (over z, x).
Axes of the slice: x: 4, y: 8, z: 12, core: 2. Of those that a mesh axis runs over, the one named last changes fastest.
Arguments:
- routes: int32 [98304, 1], P(('expert', 'dp')), may hold values from 0 to 15; in each aligned block of 128 rows (0 to 127, 128 to 255, ...) at most 9 rows name the same one
- residual_grad: bfloat16 [98304, 2048], P(('expert', 'dp')), may hold values from -6 to 6
- saved_inputs: bfloat16 [16, 6912, 2048], P('expert', 'dp'), may hold values from -6 to 6
- saved_preact: bfloat16 [16, 6912, 288], P('expert', 'dp'), may hold values from -6 to 6
- expert_grad: bfloat16 [16, 6912, 2048], P('expert', 'dp'), may hold values from -6 to 6
- w_in: bfloat16 [16, 288, 2048], P('expert'), may hold values from -0.125 to 0.125
- w_out: bfloat16 [16, 288, 2048], P('expert'), may hold values from -0.375 to 0.375
Outputs:
- token_grad: bfloat16 [98304, 2048], P(('expert', 'dp'))
- grad_in: float32 [16, 288, 2048], P('expert', 'dp')
Inputs may be any that keep to these rules, and one draw needn't show every extreme that they name: `routes`: in each aligned block of 128 rows (the tokens of one device) no expert is named by more than 9 rows, and in every draw some block names some expert exactly 9 times.
All inputs are finite; a program needn't handle non-finite values.
Results may differ from a plain program's by a relative error of at most 0.0047.
Values may be sent and summed in bfloat16 or wider, within the bound.
No kernel may reach another device: no remote copies, remote signals or barrier semaphores. Data moves between devices by JAX's collectives and lax.ppermute only.
A program may use at most 32 MiB of HBM per device.

v0:
```python
import jax
import jax.numpy as jnp
from jax import lax
from jax.sharding import PartitionSpec as P


def column_product(left, right):
    return lax.dot_general(
        left, right, (((0,), (0,)), ((), ())), preferred_element_type=jnp.float32
    )


def weight_sum(hidden_grad, inputs):
    return lax.psum_scatter(
        column_product(hidden_grad, inputs), "dp", scatter_dimension=0, tiled=True
    )


def send_back(hidden_grad, weight_in, experts, cap, width):
    slot_grad = jnp.dot(hidden_grad, weight_in, preferred_element_type=jnp.float32).astype(
        jnp.bfloat16
    )
    return lax.all_to_all(
        slot_grad.reshape(experts, cap, width), "expert", split_axis=0, concat_axis=0, tiled=True
    )


def shards(routes, residual_grad, saved_inputs, saved_preact, expert_grad, w_in, w_out):
    experts = lax.axis_size("expert")
    groups = lax.axis_size("dp")
    ids = routes[:, 0]
    onehot = (ids[:, None] == jnp.arange(experts, dtype=jnp.int32)[None, :]).astype(jnp.int32)
    running = jnp.cumsum(onehot, axis=0, dtype=jnp.int32)
    counts = running[-1]
    slot_of = jnp.sum((running - onehot) * onehot, axis=1, dtype=jnp.int32)
    mine = lax.all_to_all(counts, "expert", split_axis=0, concat_axis=0, tiled=True)
    inputs = saved_inputs[0]
    preact = saved_preact[0]
    raw_grad = expert_grad[0]
    weight_in = w_in[0]
    weight_out = w_out[0]
    slots = inputs.shape[0]
    width = inputs.shape[1]
    cap = slots // experts
    position = jnp.arange(slots, dtype=jnp.int32) % cap
    live = position < jnp.repeat(mine, cap)
    gated = jnp.where(live[:, None], raw_grad, jnp.zeros_like(raw_grad))
    product = lax.dot_general(
        gated, weight_out, (((1,), (1,)), ((), ())), preferred_element_type=jnp.float32
    )
    hidden_grad = jnp.where(preact > 0, product, jnp.zeros_like(product)).astype(jnp.bfloat16)
    part_in = weight_sum(hidden_grad, inputs)
    returned = send_back(hidden_grad, weight_in, experts, cap, width)
    picked = returned.reshape(experts * cap, width)[ids * cap + slot_of]
    token_grad = (residual_grad.astype(jnp.float32) + picked.astype(jnp.float32)).astype(
        jnp.bfloat16
    )
    grad_in = (part_in / groups)[None]
    return (token_grad, grad_in)


def solution(mesh):
    in_specs = (
        P(("expert", "dp"), None),
        P(("expert", "dp"), None),
        P("expert", "dp", None),
        P("expert", "dp", None),
        P("expert", "dp", None),
        P("expert", None, None),
        P("expert", None, None),
    )
    out_specs = (P(("expert", "dp"), None), P("expert", "dp", None))
    return jax.shard_map(shards, mesh=mesh, in_specs=in_specs, out_specs=out_specs, check_vma=False)
```

profile of v0, /device:TPU:10, one launch (start us, length us, event | category | flops | bytes accessed | tf_op | source)
XLA Modules:
  0.0 218.7 jit_solution(14096777348737482462)
XLA Ops:
  0.6 0.0 copy-start
  0.6 0.8 fusion.17
  1.5 0.2 reduce_window_sum.11
  1.7 0.0 copy-start.3
  1.7 0.1 copy.13
  1.8 13.5 %all_to_all.17 = s32[16,1,1]{2,1,0:T(1,128)S(1)} all-to-all(s32[16,1,1]{2,1,0:T(1,128)S(1)} %copy.13), channel_id=1, replica_groups=mesh['expert'=16,'dp'=48] {'expert'}, dimensions={0} | all-to-all | bytes 128 | tf_op jit(solution)/shard_map/all_to_all | solution.py:36
  15.3 0.4 reduce
  15.7 0.1 broadcast_in_dim.23
  15.7 0.1 reshape.41
  15.9 0.0 copy-done.3
  15.9 0.0 copy-start.1
  15.9 2.1 fusion.7
  18.0 0.0 copy-done.1
  18.0 0.5 fusion.10
  18.5 0.0 copy-done
  18.5 1.3 convolution_convert_fusion
  19.9 2.3 %reshape.42 = bf16[16,9,2048]{2,1,0:T(8,128)(2,1)} reshape(bf16[144,2048]{1,0:T(8,128)(2,1)} %convolution_convert_fusion) | data formatting | bytes 1179648 | tf_op jit(solution)/shard_map/reshape | solution.py:24
  22.1 5.5 %all-to-all-start.1 = ((bf16[16,9,2048]{2,1,0:T(8,128)(2,1)}), bf16[16,9,2048]{2,1,0:T(8,128)(2,1)}, u32[]{:S(2)}, u32[]{:S(2)}) async-start(bf16[16,9,2048]{2,1,0:T(8,128)(2,1)} %reshape.42), calls=%async_computation.1 | async-start | bytes 2097152 | tf_op jit(solution)/shard_map/all_to_all | solution.py:23
  27.7 0.0 copy-start.4
  27.7 134.8 %fusion = f32[8,2048]{1,0:T(8,128)} fusion(f32[288,2048]{1,0:T(8,128)S(1)} %fusion.10), kind=kCustom, calls=%all-reduce-scatter | all-reduce-scatter fusion | flops 786433 | bytes 2428928
  162.5 0.8 slice.7
  163.4 1.9 collective-permute-start
  165.3 1.3 collective-permute-start.11
  166.6 0.0 copy-done.4
  166.6 1.0 select_reduce_fusion
  167.6 7.1 %collective-permute-start.1 = (f32[8,2048]{1,0:T(8,128)}, f32[8,2048]{1,0:T(8,128)S(1)}, u32[]{:S(2)}, u32[]{:S(2)}) collective-permute-start(f32[8,2048]{1,0:T(8,128)} %fusion), channel_id=1, source_target_pairs={{0,2},{1,3},{2,4},{3,5},{4,6},{5,7},{6,8},{7,9},{8,10},{9,11},{10,... | collective-permute-start | bytes 196616
  174.7 1.3 collective-permute-start.10
  176.0 6.3 %collective-permute-start.2 = (f32[8,2048]{1,0:T(8,128)}, f32[8,2048]{1,0:T(8,128)S(1)}, u32[]{:S(2)}, u32[]{:S(2)}) collective-permute-start(f32[8,2048]{1,0:T(8,128)} %fusion), channel_id=1, source_target_pairs={{0,3},{1,4},{2,5},{3,6},{4,7},{5,8},{6,9},{7,10},{8,11},{9,12},{10... | collective-permute-start | bytes 196616
  182.3 0.0 collective-permute-done.11
  182.3 7.7 %collective-permute-start.3 = (f32[8,2048]{1,0:T(8,128)}, f32[8,2048]{1,0:T(8,128)S(1)}, u32[]{:S(2)}, u32[]{:S(2)}) collective-permute-start(f32[8,2048]{1,0:T(8,128)} %fusion), channel_id=1, source_target_pairs={{0,4},{1,5},{2,6},{3,7},{4,8},{5,9},{6,10},{7,11},{8,12},{9,13},{1... | collective-permute-start | bytes 196616
  190.0 0.0 collective-permute-done
  190.0 2.2 %collective-permute-start.4 = (f32[8,2048]{1,0:T(8,128)}, f32[8,2048]{1,0:T(8,128)S(1)}, u32[]{:S(2)}, u32[]{:S(2)}) collective-permute-start(f32[8,2048]{1,0:T(8,128)} %fusion), channel_id=1, source_target_pairs={{0,5},{1,6},{2,7},{3,8},{4,9},{5,10},{6,11},{7,12},{8,13},{9,14},{... | collective-permute-start | bytes 196616
  192.2 1.3 dynamic-slice.4
  194.2 0.0 collective-permute-done.1
  194.2 4.0 %collective-permute-start.5 = (f32[8,2048]{1,0:T(8,128)}, f32[8,2048]{1,0:T(8,128)S(1)}, u32[]{:S(2)}, u32[]{:S(2)}) collective-permute-start(f32[8,2048]{1,0:T(8,128)} %fusion), channel_id=1, source_target_pairs={{0,6},{1,7},{2,8},{3,9},{4,10},{5,11},{6,12},{7,13},{8,14},{9,15},... | collective-permute-start | bytes 196616
  198.2 0.0 collective-permute-done.10
  198.2 1.9 collective-permute-start.6
  200.1 0.0 collective-permute-done.2
  200.1 2.5 %collective-permute-start.7 = (f32[8,2048]{1,0:T(8,128)}, f32[8,2048]{1,0:T(8,128)S(1)}, u32[]{:S(2)}, u32[]{:S(2)}) collective-permute-start(f32[8,2048]{1,0:T(8,128)} %fusion), channel_id=1, source_target_pairs={{0,8},{1,9},{2,10},{3,11},{4,12},{5,13},{6,14},{7,15},{8,16},{9,17... | collective-permute-start | bytes 196616
  202.6 0.0 collective-permute-done.3
  202.6 2.0 collective-permute-start.8
  204.6 0.0 collective-permute-done.4
  204.6 5.3 %collective-permute-start.9 = (f32[8,2048]{1,0:T(8,128)}, f32[8,2048]{1,0:T(8,128)S(1)}, u32[]{:S(2)}, u32[]{:S(2)}) collective-permute-start(f32[8,2048]{1,0:T(8,128)} %fusion), channel_id=1, source_target_pairs={{0,10},{1,11},{2,12},{3,13},{4,14},{5,15},{6,16},{7,17},{8,18},{9,... | collective-permute-start | bytes 196616
  209.9 0.0 collective-permute-done.5
  209.9 0.0 collective-permute-done.6
  209.9 0.0 collective-permute-done.7
  210.0 0.0 collective-permute-done.8
  210.0 2.1 collective-permute-done.9
  212.1 2.4 %concatenate = f32[102,2048]{1,0:T(8,128)S(1)} concatenate(f32[6,2048]{1,0:T(8,128)S(1)} %collective-permute-done.11, f32[8,2048]{1,0:T(8,128)S(1)} %collective-permute-done.10, f32[8,2048]{1,0:T(8,128)S(1)} %collective-permute-done.9, f32[8,2048]{1,0:T(8,128)S(1)} %collective-permute-done.8, f32[8,2048]{1,0:T(8,128)S(1)} %collective-permute-done.7, ...), dimensions={0} | concatenate | bytes 1671168
  214.5 0.7 copy.14
  215.2 0.0 all-to-all-done.1
  215.2 1.5 reshape.43
  216.7 0.0 copy-start.2
  216.7 0.9 gather_fusion
  217.6 0.1 copy-done.2
  217.7 0.9 add_convert_fusion
  (5 shorter events, 0.0 us)
Async XLA Ops:
  0.6 17.9 %copy-start = (bf16[1,288,2048]{2,1,0:T(8,128)(2,1)S(1)}, bf16[1,288,2048]{2,1,0:T(8,128)(2,1)}, u32[]{:S(2)}) copy-start(bf16[1,288,2048]{2,1,0:T(8,128)(2,1)} %param.12) | copy-start | bytes 3538948
  1.7 14.2 %copy-start.3 = (s32[128,16]{1,0:T(8,128)}, s32[128,16]{1,0:T(8,128)S(1)}, u32[]{:S(2)}) copy-start(s32[128,16]{1,0:T(8,128)S(1)} %reduce_window_sum.11) | copy-start | bytes 24580
  15.9 2.1 copy-start.1
  22.1 193.1 %all-to-all-start.1 = ((bf16[16,9,2048]{2,1,0:T(8,128)(2,1)}), bf16[16,9,2048]{2,1,0:T(8,128)(2,1)}, u32[]{:S(2)}, u32[]{:S(2)}) async-start(bf16[16,9,2048]{2,1,0:T(8,128)(2,1)} %reshape.42), calls=%async_computation.1 | async-start | bytes 2097152 | tf_op jit(solution)/shard_map/all_to_all | solution.py:23
  27.7 138.9 %copy-start.4 = (s32[128,1]{0,1:T(1,128)S(1)}, s32[128,1]{0,1:T(1,128)}, u32[]{:S(2)}) copy-start(s32[128,1]{0,1:T(1,128)} %param.7) | copy-start | bytes 1540
  163.4 26.6 %collective-permute-start = (f32[8,2048]{1,0:T(8,128)}, f32[8,2048]{1,0:T(8,128)S(1)}, u32[]{:S(2)}, u32[]{:S(2)}) collective-permute-start(f32[8,2048]{1,0:T(8,128)} %fusion), channel_id=1, source_target_pairs={{0,1},{1,2},{2,3},{3,4},{4,5},{5,6},{6,7},{7,8},{8,9},{9,10},{10,1... | collective-permute-start | bytes 196616
  165.3 17.0 %collective-permute-start.11 = (f32[6,2048]{1,0:T(8,128)S(1)}, f32[6,2048]{1,0:T(8,128)S(1)}, u32[]{:S(2)}, u32[]{:S(2)}) collective-permute-start(f32[6,2048]{1,0:T(8,128)S(1)} %slice.7), channel_id=1, source_target_pairs={{0,12},{1,13},{2,14},{3,15},{4,16},{5,17},{6,18},{7,19},{8,20},{9,... | collective-permute-start | bytes 147464
  167.6 26.5 %collective-permute-start.1 = (f32[8,2048]{1,0:T(8,128)}, f32[8,2048]{1,0:T(8,128)S(1)}, u32[]{:S(2)}, u32[]{:S(2)}) collective-permute-start(f32[8,2048]{1,0:T(8,128)} %fusion), channel_id=1, source_target_pairs={{0,2},{1,3},{2,4},{3,5},{4,6},{5,7},{6,8},{7,9},{8,10},{9,11},{10,... | collective-permute-start | bytes 196616
  174.7 23.5 %collective-permute-start.10 = (f32[8,2048]{1,0:T(8,128)}, f32[8,2048]{1,0:T(8,128)S(1)}, u32[]{:S(2)}, u32[]{:S(2)}) collective-permute-start(f32[8,2048]{1,0:T(8,128)} %fusion), channel_id=1, source_target_pairs={{0,11},{1,12},{2,13},{3,14},{4,15},{5,16},{6,17},{7,18},{8,19},{9,... | collective-permute-start | bytes 196616
  176.0 24.1 %collective-permute-start.2 = (f32[8,2048]{1,0:T(8,128)}, f32[8,2048]{1,0:T(8,128)S(1)}, u32[]{:S(2)}, u32[]{:S(2)}) collective-permute-start(f32[8,2048]{1,0:T(8,128)} %fusion), channel_id=1, source_target_pairs={{0,3},{1,4},{2,5},{3,6},{4,7},{5,8},{6,9},{7,10},{8,11},{9,12},{10... | collective-permute-start | bytes 196616
  182.3 20.3 %collective-permute-start.3 = (f32[8,2048]{1,0:T(8,128)}, f32[8,2048]{1,0:T(8,128)S(1)}, u32[]{:S(2)}, u32[]{:S(2)}) collective-permute-start(f32[8,2048]{1,0:T(8,128)} %fusion), channel_id=1, source_target_pairs={{0,4},{1,5},{2,6},{3,7},{4,8},{5,9},{6,10},{7,11},{8,12},{9,13},{1... | collective-permute-start | bytes 196616
  190.0 14.6 %collective-permute-start.4 = (f32[8,2048]{1,0:T(8,128)}, f32[8,2048]{1,0:T(8,128)S(1)}, u32[]{:S(2)}, u32[]{:S(2)}) collective-permute-start(f32[8,2048]{1,0:T(8,128)} %fusion), channel_id=1, source_target_pairs={{0,5},{1,6},{2,7},{3,8},{4,9},{5,10},{6,11},{7,12},{8,13},{9,14},{... | collective-permute-start | bytes 196616
  194.2 15.7 %collective-permute-start.5 = (f32[8,2048]{1,0:T(8,128)}, f32[8,2048]{1,0:T(8,128)S(1)}, u32[]{:S(2)}, u32[]{:S(2)}) collective-permute-start(f32[8,2048]{1,0:T(8,128)} %fusion), channel_id=1, source_target_pairs={{0,6},{1,7},{2,8},{3,9},{4,10},{5,11},{6,12},{7,13},{8,14},{9,15},... | collective-permute-start | bytes 196616
  198.2 11.8 %collective-permute-start.6 = (f32[8,2048]{1,0:T(8,128)}, f32[8,2048]{1,0:T(8,128)S(1)}, u32[]{:S(2)}, u32[]{:S(2)}) collective-permute-start(f32[8,2048]{1,0:T(8,128)} %fusion), channel_id=1, source_target_pairs={{0,7},{1,8},{2,9},{3,10},{4,11},{5,12},{6,13},{7,14},{8,15},{9,16}... | collective-permute-start | bytes 196616
  200.1 9.8 %collective-permute-start.7 = (f32[8,2048]{1,0:T(8,128)}, f32[8,2048]{1,0:T(8,128)S(1)}, u32[]{:S(2)}, u32[]{:S(2)}) collective-permute-start(f32[8,2048]{1,0:T(8,128)} %fusion), channel_id=1, source_target_pairs={{0,8},{1,9},{2,10},{3,11},{4,12},{5,13},{6,14},{7,15},{8,16},{9,17... | collective-permute-start | bytes 196616
  202.6 7.3 %collective-permute-start.8 = (f32[8,2048]{1,0:T(8,128)}, f32[8,2048]{1,0:T(8,128)S(1)}, u32[]{:S(2)}, u32[]{:S(2)}) collective-permute-start(f32[8,2048]{1,0:T(8,128)} %fusion), channel_id=1, source_target_pairs={{0,9},{1,10},{2,11},{3,12},{4,13},{5,14},{6,15},{7,16},{8,17},{9,1... | collective-permute-start | bytes 196616
  204.6 7.5 %collective-permute-start.9 = (f32[8,2048]{1,0:T(8,128)}, f32[8,2048]{1,0:T(8,128)S(1)}, u32[]{:S(2)}, u32[]{:S(2)}) collective-permute-start(f32[8,2048]{1,0:T(8,128)} %fusion), channel_id=1, source_target_pairs={{0,10},{1,11},{2,12},{3,13},{4,14},{5,15},{6,16},{7,17},{8,18},{9,... | collective-permute-start | bytes 196616
  216.7 1.0 copy-start.2
where the time goes:
time: 220 us; the launch traced here: 219 us
  blocking collectives  148 us (67%)
  starting transfers between devices  48.9 us (22%)
  local copies, waits for them, and re-layouts  10.2 us (5%)
  matrix products  3.96 us (2%)
  other arithmetic  3.36 us (2%)
    unnamed x1, blocking collectives  135 us
    unnamed x12, starting transfers between devices  43.4 us
    all_to_all x1, blocking collectives, shards(): lax.all_to_all(counts, 'expert', split_axis=0, concat_axis=0, tiled=True)  13.5 us
    all_to_all x1, starting transfers between devices, send_back(): lax.all_to_all(slot_grad.reshape(experts, cap, width), 'expert', split_ax...  5.55 us
    unnamed x14, local copies, waits for them, and re-layouts  5.3 us
  transfers between devices with their start and end apart: 13, of which 1 were waited for; matrix products, arithmetic and copies ran while one was open for 65% of the time, Pallas kernels for 0%

commit v1 on v0

v1 whole, which is shorter than its diff:
```python
import functools
import jax
import jax.numpy as jnp
from jax import lax
from jax.experimental import pallas as pl
from jax.experimental.pallas import tpu as pltpu
from jax.sharding import Mesh, PartitionSpec as P

BF = jnp.bfloat16
F32 = jnp.float32
CAP = 9
X_DEV = 4
VMEM = 48 * 1024 * 1024


def iota(shape, axis):
    return lax.broadcasted_iota(jnp.int32, shape, axis)


def dot(a, b, ca=1, cb=0):
    return lax.dot_general(a, b, (((ca,), (cb,)), ((), ())), preferred_element_type=F32)


def call(body, outs, *args, flops=0):
    size = sum(a.size * a.dtype.itemsize for a in args) + sum(o.size * o.dtype.itemsize for o in outs)
    return pl.pallas_call(
        body,
        out_shape=outs,
        compiler_params=pltpu.CompilerParams(vmem_limit_bytes=VMEM),
        cost_estimate=pl.CostEstimate(flops=flops, bytes_accessed=size, transcendentals=0),
    )(*args)


def count_body(routes, out):
    rows = out.shape[0]
    hit = (iota((rows, routes.shape[1]), 0) >> 2) == routes[...]
    total = jnp.sum(hit.astype(F32), axis=1, keepdims=True)
    out[...] = jnp.broadcast_to(total, out.shape).astype(jnp.int32)


def hidden_body(grad, w_out, preact, hidden, message):
    product = dot(grad[...], w_out[...], 1, 1)
    h = jnp.where(preact[...].astype(F32) > 0, product, 0.0).astype(BF)
    hidden[...] = h
    units, wide = h.shape[1], message.shape[1]
    col = iota((units, wide), 1)
    place = ((col & 7) < 6) & (iota((units, wide), 0) == 6 * (col >> 3) + (col & 7))
    spread = dot(h, place.astype(BF)).astype(BF)
    rows = h.shape[0]
    for i in range(X_DEV):
        message[i * rows : (i + 1) * rows, :] = spread


def slot_body(hidden, w_in, out):
    rows = hidden.shape[0]
    k = iota((256, rows), 0)
    j = k & 127
    i = iota((256, rows), 1)
    source = 9 * (j >> 3) + jnp.where(k < 128, j & 7, 8)
    picked = dot((i == source).astype(BF), hidden[...]).astype(BF)
    width = w_in.shape[1]
    product = dot(picked, w_in[...])
    out[:, :width] = product[:128].astype(BF)
    row = iota((128, 256), 0) & 7
    last = jnp.zeros((128, 256), F32)
    for r in range(8):
        last = jnp.where(row == r, product[128:, 256 * r : 256 * r + 256], last)
    out[:, width:] = last.astype(BF)


def weight_body(hidden, inputs, counts, out):
    rows = hidden.shape[0]
    n = counts.shape[0]
    eye = (iota((n, n), 0) == iota((n, n), 1)).astype(BF)
    lanes = dot(counts[...].astype(F32).astype(BF), eye, 0, 0)[0:1, :].astype(jnp.int32)
    k = iota((rows, n), 1)
    first = (k & 3) * (rows // X_DEV) + CAP * (k >> 2)
    g = iota((rows, n), 0)
    live = ((g >= first) & (g < first + lanes)).astype(BF)
    mask = dot(live, jnp.ones((n, 128), BF))
    mask = jnp.concatenate([mask] * 3, axis=1)
    h = jnp.where(mask > 0.5, hidden[...].astype(F32), 0.0).astype(BF)
    part = dot(h, inputs[...], 0, 0)
    last = part[:, 384:]
    sub = iota(last.shape, 0) & 7
    for w in range(3):
        tile = part[:, 128 * w : 128 * w + 128]
        tile = jnp.where(sub == 6, pltpu.roll(last, 6 - w, 0), tile)
        tile = jnp.where(sub == 7, pltpu.roll(last, 4 - w, 0), tile)
        out[:, 128 * w : 128 * w + 128] = tile.astype(BF)


def sum_body(scale, parts, out):
    step = 8 * X_DEV
    total = parts[0:step, :].astype(F32)
    for z in range(1, parts.shape[0] // step):
        total = total + parts[z * step : (z + 1) * step, :].astype(F32)
    total = total / scale
    for x in range(X_DEV):
        out[:, 512 * x : 512 * x + 384] = total[8 * x : 8 * x + 6, :]
        for u in range(6):
            v, w = u // 3, u % 3
            out[u : u + 1, 512 * x + 384 : 512 * x + 512] = total[
                8 * x + 6 + v : 8 * x + 7 + v, 128 * w : 128 * w + 128
            ]


def token_body(routes, residual, returned, out):
    ids = routes[...]
    n = ids.shape[1]
    onehot = (iota((16, n), 0) == ids).astype(F32)
    before = (iota((n, n), 0) < iota((n, n), 1)).astype(BF)
    prefix = dot(onehot.astype(BF), before)
    slot = jnp.sum(onehot * prefix, axis=0, keepdims=True).astype(jnp.int32)
    k = iota((n, n), 0)
    same = (k >> 3) == ids
    pick = (same & ((k & 7) == slot)).astype(BF)
    extra = returned[:, 2048:]
    for r in range(8):
        span = slice(256 * r, 256 * r + 256)
        pick_last = (same & (slot == 8) & ((k & 7) == r)).astype(BF)
        got = dot(pick, returned[:, span], 0, 0) + dot(pick_last, extra, 0, 0)
        out[:, span] = (residual[:, span].astype(F32) + got).astype(BF)


def shards(routes, residual_grad, saved_inputs, saved_preact, expert_grad, w_in, w_out):
    S = jax.ShapeDtypeStruct
    inputs = saved_inputs[0]
    slots, width = inputs.shape
    units = w_in.shape[1]
    groups = lax.axis_size("z") * lax.axis_size("x")
    ids = routes.reshape(1, 128)
    (counts,) = call(count_body, [S((64, 128), jnp.int32)], ids)
    counts = lax.all_to_all(
        counts.reshape(64, 1, 128), ("expert", "x"), split_axis=0, concat_axis=0, tiled=True
    ).reshape(64, 128)
    inputs = lax.all_to_all(inputs, "x", split_axis=1, concat_axis=0, tiled=True)
    hidden, message = call(
        hidden_body,
        [S((slots, units), BF), S((X_DEV * slots, 384), BF)],
        expert_grad[0], w_out[0], saved_preact[0],
        flops=2 * slots * units * width,
    )
    message = lax.all_to_all(message, "x", split_axis=0, concat_axis=0, tiled=True)
    (slot_grad,) = call(
        slot_body, [S((128, width + 256), BF)], hidden, w_in[0], flops=4 * 128 * units * width
    )
    returned = lax.all_to_all(slot_grad, "expert", split_axis=0, concat_axis=0, tiled=True)
    (part,) = call(
        weight_body, [S((8 * groups, 384), BF)], message, inputs, counts,
        flops=2 * 576 * 384 * 512,
    )
    part = lax.all_to_all(part, ("z", "x"), split_axis=0, concat_axis=0, tiled=True)
    (token_grad,) = call(
        token_body, [S((128, width), BF)], ids, residual_grad, returned,
        flops=4 * 128 * 128 * width,
    )
    (grad_in,) = call(
        functools.partial(sum_body, float(groups)), [S((6, width), F32)], part
    )
    return token_grad, grad_in[None]


def solution(mesh):
    fine = Mesh(mesh.devices.reshape(16, 12, X_DEV), ("expert", "z", "x"))
    tokens = P(("expert", "z", "x"), None)
    buffers = P("expert", ("z", "x"), None)
    weights = P("expert", None, None)
    return jax.shard_map(
        shards,
        mesh=fine,
        in_specs=(tokens, tokens, buffers, buffers, buffers, weights, weights),
        out_specs=(tokens, buffers),
        check_vma=False,
    )
```

time: 220 us -> 107 us (0.49)
  the two profiles are of different devices: /device:TPU:10 before, /device:TPU:1 now
where the time goes in v1:
time: 107 us; the launch traced here: 106 us
  waiting for transfers between devices  50.3 us (47%)
  starting transfers between devices  41.9 us (39%)
  Pallas kernels  7.13 us (7%)
  local copies, waits for them, and re-layouts  5.92 us (6%)
    all_to_all x1, waiting for transfers between devices, shards(): lax.all_to_all(slot_grad, 'expert', split_axis=0, concat_axis=0, tiled=True)  17 us
    all_to_all x1, waiting for transfers between devices, shards(): lax.all_to_all(part, ('z', 'x'), split_axis=0, concat_axis=0, tiled=True)  16.9 us
    all_to_all x1, starting transfers between devices, shards(): lax.all_to_all(counts.reshape(64, 1, 128), ('expert', 'x'), split_axis=0,...  14.6 us
    all_to_all x1, starting transfers between devices, shards(): lax.all_to_all(part, ('z', 'x'), split_axis=0, concat_axis=0, tiled=True)  13.1 us
    all_to_all x1, starting transfers between devices, shards(): lax.all_to_all(slot_grad, 'expert', split_axis=0, concat_axis=0, tiled=True)  7.26 us
    pallas_call x6, Pallas kernels, call(): pl.pallas_call(body, out_shape=outs, compiler_params=pltpu.CompilerParams...  7.13 us
    all_to_all x1, waiting for transfers between devices, shards(): lax.all_to_all(inputs, 'x', split_axis=1, concat_axis=0, tiled=True)  6.12 us
    all_to_all x1, waiting for transfers between devices, shards(): lax.all_to_all(message, 'x', split_axis=0, concat_axis=0, tiled=True)  6.04 us
  transfers between devices with their start and end apart: 5, of which 5 were waited for; matrix products, arithmetic and copies ran while one was open for 1% of the time, Pallas kernels for 6%

profile of v1, /device:TPU:1, one launch (start us, length us, event | category | flops | bytes accessed | tf_op | source)
XLA Modules:
  0.0 106.0 jit_solution(4534985849913116573)
XLA Ops:
  0.6 0.0 copy-start.5
  0.6 0.6 copy-done.5
  1.3 0.7 shard_map.89
  2.0 14.6 %all-to-all-start.3 = ((s32[64,1,128]{2,1,0:T(1,128)}), s32[64,1,128]{2,1,0:T(1,128)S(1)}, u32[]{:S(2)}, u32[]{:S(2)}) async-start(s32[64,1,128]{2,1,0:T(1,128)} %bitcast.12), calls=%async_computation.3 | async-start | bytes 65536 | tf_op jit(solution)/shard_map/all_to_all | solution.py:134
  16.6 0.0 copy-start
  16.6 1.3 %copy-done = bf16[1,288,2048]{2,1,0:T(8,128)(2,1)S(1)} copy-done((bf16[1,288,2048]{2,1,0:T(8,128)(2,1)S(1)}, bf16[1,288,2048]{2,1,0:T(8,128)(2,1)}, u32[]{:S(2)}) %copy-start) | copy-done | bytes 1179672
  17.8 0.0 copy-start.2
  17.8 1.1 %copy-done.2 = bf16[1,144,2048]{2,1,0:T(8,128)(2,1)S(1)} copy-done((bf16[1,144,2048]{2,1,0:T(8,128)(2,1)S(1)}, bf16[1,144,2048]{2,1,0:T(8,128)(2,1)}, u32[]{:S(2)}) %copy-start.2) | copy-done | bytes 589848
  18.9 0.0 copy-start.4
  18.9 0.9 copy-done.4
  19.8 0.0 copy-start.7
  19.8 1.7 %shard_map.86 = (bf16[144,288]{1,0:T(8,128)(2,1)S(1)}, bf16[576,384]{1,0:T(8,128)(2,1)}) custom-call(bf16[144,2048]{1,0:T(8,128)(2,1)S(1)} %bitcast.25, bf16[288,2048]{1,0:T(8,128)(2,1)S(1)} %bitcast.22, bf16[144,288]{1,0:T(8,128)(2,1)S(1)} %bitcast.28), custom_call_target="tpu_custom_call" | custom-call | flops 169869312 | bytes 2377728 | tf_op jit(solution)/shard_map/pallas_call | solution.py:26
  21.5 4.3 %all-to-all-done.3 = s32[64,1,128]{2,1,0:T(1,128)S(1)} async-done(((s32[64,1,128]{2,1,0:T(1,128)}), s32[64,1,128]{2,1,0:T(1,128)S(1)}, u32[]{:S(2)}, u32[]{:S(2)}) %all-to-all-start.3) | async-done | bytes 32800 | tf_op jit(solution)/shard_map/all_to_all | solution.py:134
  25.8 3.5 %all-to-all-start.1 = ((bf16[4,144,384]{2,1,0:T(8,128)(2,1)}), bf16[4,144,384]{2,1,0:T(8,128)(2,1)S(1)}, u32[]{:S(2)}, u32[]{:S(2)}) async-start(bf16[4,144,384]{2,1,0:T(8,128)(2,1)} %bitcast.7), calls=%async_computation.1 | async-start | bytes 884736 | tf_op jit(solution)/shard_map/all_to_all | solution.py:144
  29.2 0.0 copy-done.7
  29.2 0.4 all_to_all.44
  29.7 0.0 copy-start.1
  29.7 0.9 copy.11
  30.6 6.0 %all-to-all-done.1 = bf16[4,144,384]{2,1,0:T(8,128)(2,1)S(1)} async-done(((bf16[4,144,384]{2,1,0:T(8,128)(2,1)}), bf16[4,144,384]{2,1,0:T(8,128)(2,1)S(1)}, u32[]{:S(2)}, u32[]{:S(2)}) %all-to-all-start.1) | async-done | bytes 442400 | tf_op jit(solution)/shard_map/all_to_all | solution.py:144
  36.7 3.5 %all-to-all-start.2 = ((bf16[144,4,512]{2,0,1:T(8,128)(2,1)}), bf16[144,4,512]{2,0,1:T(8,128)(2,1)S(1)}, u32[]{:S(2)}, u32[]{:S(2)}) async-start(bf16[144,4,512]{2,0,1:T(8,128)(2,1)} %copy.11), calls=%async_computation.2 | async-start | bytes 1179648 | tf_op jit(solution)/shard_map/all_to_all | solution.py:137
  40.1 0.0 copy-done.1
  40.2 1.7 %shard_map.87 = bf16[128,2304]{1,0:T(8,128)(2,1)} custom-call(bf16[144,288]{1,0:T(8,128)(2,1)S(1)} %get-tuple-element.4.hidden, bf16[288,2048]{1,0:T(8,128)(2,1)S(1)} %bitcast.23), custom_call_target="tpu_custom_call" | custom-call | flops 301989888 | bytes 1852416 | tf_op jit(solution)/shard_map/pallas_call | solution.py:26
  41.8 6.1 %all-to-all-done.2 = bf16[144,4,512]{2,0,1:T(8,128)(2,1)S(1)} async-done(((bf16[144,4,512]{2,0,1:T(8,128)(2,1)}), bf16[144,4,512]{2,0,1:T(8,128)(2,1)S(1)}, u32[]{:S(2)}, u32[]{:S(2)}) %all-to-all-start.2) | async-done | bytes 589856 | tf_op jit(solution)/shard_map/all_to_all | solution.py:137
  47.9 7.3 %all-to-all-start = ((bf16[16,8,2304]{2,1,0:T(8,128)(2,1)}), bf16[16,8,2304]{2,1,0:T(8,128)(2,1)S(1)}, u32[]{:S(2)}, u32[]{:S(2)}) async-start(bf16[16,8,2304]{2,1,0:T(8,128)(2,1)} %bitcast.5), calls=%async_computation | async-start | bytes 1179648 | tf_op jit(solution)/shard_map/all_to_all | solution.py:148
  55.2 0.0 copy-start.3
  55.2 0.0 copy-start.6
  55.2 1.6 %shard_map.90 = bf16[384,384]{1,0:T(8,128)(2,1)} custom-call(bf16[576,384]{1,0:T(8,128)(2,1)S(1)} %bitcast.21, bf16[576,512]{1,0:T(8,128)(2,1)S(1)} %bitcast.20, s32[64,128]{1,0:T(8,128)S(1)} %bitcast.27), custom_call_target="tpu_custom_call" | custom-call | flops 226492416 | bytes 1359872 | tf_op jit(solution)/shard_map/pallas_call | solution.py:26
  56.8 17.0 %all-to-all-done = bf16[16,8,2304]{2,1,0:T(8,128)(2,1)S(1)} async-done(((bf16[16,8,2304]{2,1,0:T(8,128)(2,1)}), bf16[16,8,2304]{2,1,0:T(8,128)(2,1)S(1)}, u32[]{:S(2)}, u32[]{:S(2)}) %all-to-all-start) | async-done | bytes 589856 | tf_op jit(solution)/shard_map/all_to_all | solution.py:148
  73.8 13.1 %all-to-all-start.4 = ((bf16[48,8,384]{2,1,0:T(8,128)(2,1)}), bf16[48,8,384]{2,1,0:T(8,128)(2,1)S(1)}, u32[]{:S(2)}, u32[]{:S(2)}) async-start(bf16[48,8,384]{2,1,0:T(8,128)(2,1)} %bitcast.14), calls=%async_computation.4 | async-start | bytes 589824 | tf_op jit(solution)/shard_map/all_to_all | solution.py:153
  87.0 0.0 copy-done.3
  87.0 0.0 copy-done.6
  87.0 1.4 %shard_map.88 = bf16[128,2048]{1,0:T(8,128)(2,1)} custom-call(s32[1,128]{1,0:T(1,128)S(1)} %bitcast.30, bf16[128,2048]{1,0:T(8,128)(2,1)S(1)} %copy-done.3, bf16[128,2304]{1,0:T(8,128)(2,1)S(1)} %bitcast.19), custom_call_target="tpu_custom_call" | custom-call | flops 134217728 | bytes 1638912 | tf_op jit(solution)/shard_map/pallas_call | solution.py:26
  88.4 16.9 %all-to-all-done.4 = bf16[48,8,384]{2,1,0:T(8,128)(2,1)S(1)} async-done(((bf16[48,8,384]{2,1,0:T(8,128)(2,1)}), bf16[48,8,384]{2,1,0:T(8,128)(2,1)S(1)}, u32[]{:S(2)}, u32[]{:S(2)}) %all-to-all-start.4) | async-done | bytes 294944 | tf_op jit(solution)/shard_map/all_to_all | solution.py:153
  105.3 0.7 copy.13
  (1 shorter events, 0.0 us)
Async XLA Ops:
  0.6 0.7 copy-start.5
  2.0 23.8 %all-to-all-start.3 = ((s32[64,1,128]{2,1,0:T(1,128)}), s32[64,1,128]{2,1,0:T(1,128)S(1)}, u32[]{:S(2)}, u32[]{:S(2)}) async-start(s32[64,1,128]{2,1,0:T(1,128)} %bitcast.12), calls=%async_computation.3 | async-start | bytes 65536 | tf_op jit(solution)/shard_map/all_to_all | solution.py:134
  16.6 1.3 %copy-start = (bf16[1,288,2048]{2,1,0:T(8,128)(2,1)S(1)}, bf16[1,288,2048]{2,1,0:T(8,128)(2,1)}, u32[]{:S(2)}) copy-start(bf16[1,288,2048]{2,1,0:T(8,128)(2,1)} %param.13) | copy-start | bytes 3538948
  17.8 1.1 %copy-start.2 = (bf16[1,144,2048]{2,1,0:T(8,128)(2,1)S(1)}, bf16[1,144,2048]{2,1,0:T(8,128)(2,1)}, u32[]{:S(2)}) copy-start(bf16[1,144,2048]{2,1,0:T(8,128)(2,1)} %param.11) | copy-start | bytes 1769476
  18.9 0.9 copy-start.4
  19.8 9.4 %copy-start.7 = (bf16[1,144,2048]{2,1,0:T(8,128)(2,1)S(1)}, bf16[1,144,2048]{2,1,0:T(8,128)(2,1)}, u32[]{:S(2)}) copy-start(bf16[1,144,2048]{2,1,0:T(8,128)(2,1)} %param.9) | copy-start | bytes 1769476
  25.8 10.9 %all-to-all-start.1 = ((bf16[4,144,384]{2,1,0:T(8,128)(2,1)}), bf16[4,144,384]{2,1,0:T(8,128)(2,1)S(1)}, u32[]{:S(2)}, u32[]{:S(2)}) async-start(bf16[4,144,384]{2,1,0:T(8,128)(2,1)} %bitcast.7), calls=%async_computation.1 | async-start | bytes 884736 | tf_op jit(solution)/shard_map/all_to_all | solution.py:144
  29.7 10.5 %copy-start.1 = (bf16[1,288,2048]{2,1,0:T(8,128)(2,1)S(1)}, bf16[1,288,2048]{2,1,0:T(8,128)(2,1)}, u32[]{:S(2)}) copy-start(bf16[1,288,2048]{2,1,0:T(8,128)(2,1)} %param.12) | copy-start | bytes 3538948
  36.7 11.3 %all-to-all-start.2 = ((bf16[144,4,512]{2,0,1:T(8,128)(2,1)}), bf16[144,4,512]{2,0,1:T(8,128)(2,1)S(1)}, u32[]{:S(2)}, u32[]{:S(2)}) async-start(bf16[144,4,512]{2,0,1:T(8,128)(2,1)} %copy.11), calls=%async_computation.2 | async-start | bytes 1179648 | tf_op jit(solution)/shard_map/all_to_all | solution.py:137
  47.9 25.9 %all-to-all-start = ((bf16[16,8,2304]{2,1,0:T(8,128)(2,1)}), bf16[16,8,2304]{2,1,0:T(8,128)(2,1)S(1)}, u32[]{:S(2)}, u32[]{:S(2)}) async-start(bf16[16,8,2304]{2,1,0:T(8,128)(2,1)} %bitcast.5), calls=%async_computation | async-start | bytes 1179648 | tf_op jit(solution)/shard_map/all_to_all | solution.py:148
  55.2 31.8 %copy-start.3 = (bf16[128,2048]{1,0:T(8,128)(2,1)S(1)}, bf16[128,2048]{1,0:T(8,128)(2,1)}, u32[]{:S(2)}) copy-start(bf16[128,2048]{1,0:T(8,128)(2,1)} %residual.1) | copy-start | bytes 1572868
  55.2 31.8 %copy-start.6 = (s32[128,1]{0,1:T(1,128)S(1)}, s32[128,1]{0,1:T(1,128)}, u32[]{:S(2)}) copy-start(s32[128,1]{0,1:T(1,128)} %param.7) | copy-start | bytes 1540
  73.8 31.4 %all-to-all-start.4 = ((bf16[48,8,384]{2,1,0:T(8,128)(2,1)}), bf16[48,8,384]{2,1,0:T(8,128)(2,1)S(1)}, u32[]{:S(2)}, u32[]{:S(2)}) async-start(bf16[48,8,384]{2,1,0:T(8,128)(2,1)} %bitcast.14), calls=%async_computation.4 | async-start | bytes 589824 | tf_op jit(solution)/shard_map/all_to_all | solution.py:153

commit v2 on v1

v2 whole, which is shorter than its diff:
```python
import functools
import jax
import jax.numpy as jnp
from jax import lax
from jax.experimental import pallas as pl
from jax.experimental.pallas import tpu as pltpu
from jax.sharding import Mesh, PartitionSpec as P

BF = jnp.bfloat16
F32 = jnp.float32
CAP = 9
X_DEV = 4
PARTS = 4
MIB = 1024 * 1024


def iota(shape, axis):
    return lax.broadcasted_iota(jnp.int32, shape, axis)


def dot(a, b, ca=1, cb=0):
    return lax.dot_general(a, b, (((ca,), (cb,)), ((), ())), preferred_element_type=F32)


def call(body, outs, *args, flops=0, limit=32, **more):
    size = sum(a.size * a.dtype.itemsize for a in args) + sum(o.size * o.dtype.itemsize for o in outs)
    return pl.pallas_call(
        body,
        out_shape=outs,
        compiler_params=pltpu.CompilerParams(vmem_limit_bytes=limit * MIB),
        cost_estimate=pl.CostEstimate(flops=flops, bytes_accessed=size, transcendentals=0),
        **more,
    )(*args)


def front_body(
    me, grad, w_out, preact, w_in, inputs,
    send0, send1, send2, send3, slots,
    grad_v, w_out_v, preact_v, w_in_v, inputs_v, sems,
):
    width = grad.shape[1]
    part = width // PARTS
    copies = []
    for i in range(PARTS):
        span = pl.ds(i * part, part)
        copies.append(pltpu.make_async_copy(grad.at[:, span], grad_v.at[:, span], sems.at[2 * i]))
        copies.append(pltpu.make_async_copy(w_out.at[:, span], w_out_v.at[:, span], sems.at[2 * i + 1]))
    n = 2 * PARTS
    preact_copy = pltpu.make_async_copy(preact, preact_v, sems.at[n])
    w_in_copy = pltpu.make_async_copy(w_in, w_in_v, sems.at[n + 1])
    inputs_copy = pltpu.make_async_copy(inputs, inputs_v, sems.at[n + 2])
    for c in copies:
        c.start()
    preact_copy.start()
    w_in_copy.start()
    inputs_copy.start()
    rows, units = preact_v.shape
    product = jnp.zeros((rows, units), F32)
    for i in range(PARTS):
        copies[2 * i].wait()
        copies[2 * i + 1].wait()
        span = slice(i * part, i * part + part)
        product = product + dot(grad_v[:, span], w_out_v[:, span], 1, 1)
    preact_copy.wait()
    h = jnp.where(preact_v[...].astype(F32) > 0, product, 0.0).astype(BF)
    col = iota((units, 384), 1)
    place = ((col & 7) < 6) & (iota((units, 384), 0) == 6 * (col >> 3) + (col & 7))
    spread = dot(h, place.astype(BF)).astype(BF)
    k = iota((256, rows), 0)
    j = k & 127
    source = CAP * (j >> 3) + jnp.where(k < 128, j & 7, 8)
    picked = dot((iota((256, rows), 1) == source).astype(BF), h).astype(BF)
    w_in_copy.wait()
    slots[:, :width] = dot(picked[:128], w_in_v[...]).astype(BF)
    row = iota((128, 256), 0) & 7
    last = jnp.zeros((128, 256), F32)
    for r in range(8):
        got = dot(picked[128:], w_in_v[:, 256 * r : 256 * r + 256])
        last = jnp.where(row == r, got, last)
    slots[:, width:] = last.astype(BF)
    inputs_copy.wait()
    for i, send in enumerate((send0, send1, send2, send3)):
        send[:, :384] = spread
        first = pl.multiple_of(((me[0] + i) & 3) * 512, 512)
        send[:, 384:] = inputs_v[:, pl.ds(first, 512)]


def weight_body(me, own, one, two, three, routes, out):
    both = jnp.concatenate([own[...], one[...], two[...], three[...]], axis=0)
    rows, n = both.shape[0], routes.shape[0]
    hits = (routes[...] == me[1]).astype(F32).astype(BF)
    lanes = dot(jnp.ones((8, 128), BF), hits, 1, 1)[0:1, :].astype(jnp.int32)
    k = iota((rows, n), 1)
    first = ((me[0] - (k & 3)) & 3) * (rows // X_DEV) + CAP * (k >> 2)
    g = iota((rows, n), 0)
    live = ((g >= first) & (g < first + lanes)).astype(F32).astype(BF)
    mask = dot(live, jnp.ones((n, 128), BF))
    mask = jnp.concatenate([mask] * 3, axis=1)
    h = jnp.where(mask > 0.5, both[:, :384].astype(F32), 0.0).astype(BF)
    part = dot(h, both[:, 384:], 0, 0)
    last = part[:, 384:]
    sub = iota(last.shape, 0) & 7
    for w in range(3):
        tile = part[:, 128 * w : 128 * w + 128]
        tile = jnp.where(sub == 6, pltpu.roll(last, 6 - w, 0), tile)
        tile = jnp.where(sub == 7, pltpu.roll(last, 4 - w, 0), tile)
        out[:, 128 * w : 128 * w + 128] = tile.astype(BF)


def sum_body(scale, parts, out):
    step = 8 * X_DEV
    total = parts[0:step, :].astype(F32)
    for z in range(1, parts.shape[0] // step):
        total = total + parts[z * step : (z + 1) * step, :].astype(F32)
    total = total / scale
    for x in range(X_DEV):
        for u in range(6):
            v, w = u // 3, u % 3
            out[u, :, 512 * x : 512 * x + 384] = total[8 * x + u : 8 * x + u + 1, :]
            out[u, :, 512 * x + 384 : 512 * x + 512] = total[
                8 * x + 6 + v : 8 * x + 7 + v, 128 * w : 128 * w + 128
            ]


def token_body(routes, residual, returned, out):
    ids = routes[...]
    n = ids.shape[1]
    onehot = (iota((16, n), 0) == ids).astype(F32)
    before = (iota((n, n), 0) < iota((n, n), 1)).astype(BF)
    prefix = dot(onehot.astype(BF), before)
    slot = jnp.sum(onehot * prefix, axis=0, keepdims=True).astype(jnp.int32)
    k = iota((n, n), 0)
    same = (k >> 3) == ids
    pick = (same & ((k & 7) == slot)).astype(BF)
    extra = returned[:, 2048:]
    for r in range(8):
        span = slice(256 * r, 256 * r + 256)
        pick_last = (same & (slot == 8) & ((k & 7) == r)).astype(BF)
        got = dot(pick, returned[:, span], 0, 0) + dot(pick_last, extra, 0, 0)
        out[:, span] = (residual[:, span].astype(F32) + got).astype(BF)


def shards(routes, residual_grad, saved_inputs, saved_preact, expert_grad, w_in, w_out):
    S = jax.ShapeDtypeStruct
    slots, width = saved_inputs.shape[1:]
    units = w_in.shape[1]
    groups = lax.axis_size("z") * lax.axis_size("x")
    me = jnp.stack([lax.axis_index("x"), lax.axis_index("expert")]).astype(jnp.int32)
    ids = routes.reshape(1, 128)
    everyone = lax.all_gather(ids, ("expert", "x"), axis=0, tiled=True)
    hbm = pl.BlockSpec(memory_space=pl.ANY)
    smem = pl.BlockSpec(memory_space=pltpu.SMEM)
    vmem = pl.BlockSpec(memory_space=pltpu.VMEM)
    *sends, slot_grad = call(
        front_body,
        [S((slots, 896), BF)] * X_DEV + [S((128, width + 256), BF)],
        me, expert_grad[0], w_out[0], saved_preact[0], w_in[0], saved_inputs[0],
        flops=8 * slots * units * width,
        limit=63,
        in_specs=[smem] + [hbm] * 5,
        scratch_shapes=[
            pltpu.VMEM((slots, width), BF),
            pltpu.VMEM((units, width), BF),
            pltpu.VMEM((slots, units), BF),
            pltpu.VMEM((units, width), BF),
            pltpu.VMEM((slots, width), BF),
            pltpu.SemaphoreType.DMA((2 * PARTS + 3,)),
        ],
    )
    returned = lax.all_to_all(slot_grad, "expert", split_axis=0, concat_axis=0, tiled=True)
    got = [sends[0]]
    for i in range(1, X_DEV):
        got.append(lax.ppermute(sends[i], "x", [(j, (j + i) % X_DEV) for j in range(X_DEV)]))
    (part,) = call(
        weight_body, [S((8 * groups, 384), BF)], me, *got, everyone,
        flops=2 * 576 * 384 * 512,
        in_specs=[smem] + [vmem] * 5,
    )
    part = lax.all_to_all(part, ("z", "x"), split_axis=0, concat_axis=0, tiled=True)
    (token_grad,) = call(
        token_body, [S((128, width), BF)], ids, residual_grad, returned,
        flops=4 * 128 * 128 * width,
    )
    (grad_in,) = call(
        functools.partial(sum_body, float(groups)), [S((6, 1, width), F32)], part
    )
    return token_grad, jnp.transpose(grad_in, (1, 0, 2))


def solution(mesh):
    fine = Mesh(mesh.devices.reshape(16, 12, X_DEV), ("expert", "z", "x"))
    tokens = P(("expert", "z", "x"), None)
    buffers = P("expert", ("z", "x"), None)
    weights = P("expert", None, None)
    return jax.shard_map(
        shards,
        mesh=fine,
        in_specs=(tokens, tokens, buffers, buffers, buffers, weights, weights),
        out_specs=(tokens, buffers),
        check_vma=False,
    )
```

time: 107 us -> 126 us (1.18)
  the two profiles are of different devices: /device:TPU:1 before, /device:TPU:25 now
where the time goes in v2:
time: 126 us
  blocking collectives  65.3 us (52%)
  starting transfers between devices  33.7 us (27%)
  waiting for transfers between devices  16 us (13%)
  Pallas kernels  9.36 us (7%)
    all_gather x1, blocking collectives, shards(): everyone = lax.all_gather(ids, ('expert', 'x'), axis=0, tiled=True)  65.3 us
    all_to_all x1, waiting for transfers between devices, shards(): lax.all_to_all(part, ('z', 'x'), split_axis=0, concat_axis=0, tiled=True)  16 us
    all_to_all x1, starting transfers between devices, shards(): lax.all_to_all(slot_grad, 'expert', split_axis=0, concat_axis=0, tiled=True)  13.1 us
    all_to_all x1, starting transfers between devices, shards(): lax.all_to_all(part, ('z', 'x'), split_axis=0, concat_axis=0, tiled=True)  12.1 us
    pallas_call x4, Pallas kernels, call(): pl.pallas_call(body, out_shape=outs, compiler_params=pltpu.CompilerParams...  9.36 us
    ppermute x3, starting transfers between devices, shards(): lax.ppermute(sends[i], 'x', [(j, (j + i) % X_DEV) for j in range(X_DEV)])  8.55 us
  transfers between devices with their start and end apart: 5, of which 1 were waited for; matrix products, arithmetic and copies ran while one was open for 0% of the time, Pallas kernels for 3%

profile of v2, /device:TPU:25, one launch (start us, length us, event | category | flops | bytes accessed | tf_op | source)
XLA Modules:
  0.0 125.9 jit_solution(14381820737569322705)
XLA Ops:
  0.6 0.6 pad_add_fusion.me
  1.3 5.1 %shard_map.86 = (bf16[144,896]{1,0:T(8,128)(2,1)}, bf16[144,896]{1,0:T(8,128)(2,1)}, bf16[144,896]{1,0:T(8,128)(2,1)}, bf16[144,896]{1,0:T(8,128)(2,1)}, bf16[128,2304]{1,0:T(8,128)(2,1)}) custom-call(s32[2]{0:T(128)} %pad_add_fusion.me, bf16[144,2048]{1,0:T(8,128)(2,1)} %bitcast.21, bf16[288,2048]{1,0:T(8,128)(2,1)} %bitcast.18, bf16[144,288]{1,0:T(8,128)(2,1)} %bitcast.23, ...), custom_call_target="tpu_custom_call" | custom-call | flops 679477248 | bytes 5243912 | tf_op jit(solution)/shard_map/pallas_call | solution.py:27
  6.4 0.0 copy-start.6
  6.4 0.0 copy-start.5
  6.5 0.0 copy-start.4
  6.5 0.0 copy-start.3
  6.5 0.0 copy-start.1
  6.5 0.0 copy-start.2
  6.5 13.1 %all-to-all-start = ((bf16[16,8,2304]{2,1,0:T(8,128)(2,1)}), bf16[16,8,2304]{2,1,0:T(8,128)(2,1)S(1)}, u32[]{:S(2)}, u32[]{:S(2)}) async-start(bf16[16,8,2304]{2,1,0:T(8,128)(2,1)} %bitcast.20), calls=%async_computation | async-start | bytes 1179648 | tf_op jit(solution)/shard_map/all_to_all | solution.py:170
  19.6 0.0 copy-start
  19.6 0.0 copy-done.6
  19.6 2.1 %collective-permute-start = (bf16[144,896]{1,0:T(8,128)(2,1)S(1)}, bf16[144,896]{1,0:T(8,128)(2,1)S(1)}, u32[]{:S(2)}, u32[]{:S(2)}) collective-permute-start(bf16[144,896]{1,0:T(8,128)(2,1)S(1)} %copy-done.6), channel_id=1, source_target_pairs={{0,1},{1,2},{2,3},{3,0},{4,5},{5,6},{6,7},{7,4},{8,9},{9,10},{10,1... | collective-permute-start | bytes 774152 | tf_op jit(solution)/shard_map/ppermute | solution.py:173
  21.7 0.0 copy-done.5
  21.7 1.9 %collective-permute-start.1 = (bf16[144,896]{1,0:T(8,128)(2,1)S(1)}, bf16[144,896]{1,0:T(8,128)(2,1)S(1)}, u32[]{:S(2)}, u32[]{:S(2)}) collective-permute-start(bf16[144,896]{1,0:T(8,128)(2,1)S(1)} %copy-done.5), channel_id=1, source_target_pairs={{0,2},{1,3},{2,0},{3,1},{4,6},{5,7},{6,4},{7,5},{8,10},{9,11},{10,... | collective-permute-start | bytes 774152 | tf_op jit(solution)/shard_map/ppermute | solution.py:173
  23.6 0.0 copy-done.4
  23.6 4.6 %collective-permute-start.2 = (bf16[144,896]{1,0:T(8,128)(2,1)S(1)}, bf16[144,896]{1,0:T(8,128)(2,1)S(1)}, u32[]{:S(2)}, u32[]{:S(2)}) collective-permute-start(bf16[144,896]{1,0:T(8,128)(2,1)S(1)} %copy-done.4), channel_id=1, source_target_pairs={{0,3},{1,0},{2,1},{3,2},{4,7},{5,4},{6,5},{7,6},{8,11},{9,8},{10,9... | collective-permute-start | bytes 774152 | tf_op jit(solution)/shard_map/ppermute | solution.py:173
  28.2 0.0 copy-done.3
  28.2 65.3 %all-gather = s32[8192,1]{0,1:T(1,128)S(1)} all-gather(s32[128,1]{0,1:T(1,128)S(1)} %copy-done.3), channel_id=2, replica_groups=mesh['expert'=16,'z'=12,'x'=4] {'expert','x'}, dimensions={0}, use_global_device_ids=true | all-gather | bytes 33280 | tf_op jit(solution)/shard_map/all_gather | solution.py:150
  93.5 0.0 collective-permute-done.one
  93.5 0.0 collective-permute-done.1.two
  93.5 0.0 collective-permute-done.2.three
  93.5 0.0 copy-done.1
  93.6 0.0 copy-done.2
  93.6 2.1 %shard_map.88 = bf16[384,384]{1,0:T(8,128)(2,1)} custom-call(s32[2]{0:T(128)S(1)} %copy-done.2, bf16[144,896]{1,0:T(8,128)(2,1)S(1)} %copy-done.1, bf16[144,896]{1,0:T(8,128)(2,1)S(1)} %collective-permute-done.one, bf16[144,896]{1,0:T(8,128)(2,1)S(1)} %collective-permute-done.1.two, bf16[144,896]{1,0:T(8,128)(2,1)S(1)} %collective-permute-done.2.three, ...), custom_call_target="tpu_custom_call" | custom-call | flops 226492416 | bytes 1359880 | tf_op jit(solution)/shard_map/pallas_call | solution.py:27
  95.7 0.0 all-to-all-done
  95.7 12.1 %all-to-all-start.1 = ((bf16[48,8,384]{2,1,0:T(8,128)(2,1)}), bf16[48,8,384]{2,1,0:T(8,128)(2,1)S(1)}, u32[]{:S(2)}, u32[]{:S(2)}) async-start(bf16[48,8,384]{2,1,0:T(8,128)(2,1)} %bitcast.11), calls=%async_computation.1 | async-start | bytes 589824 | tf_op jit(solution)/shard_map/all_to_all | solution.py:179
  107.8 0.0 copy-done
  107.8 1.4 %shard_map.87 = bf16[128,2048]{1,0:T(8,128)(2,1)} custom-call(s32[1,128]{1,0:T(1,128)S(1)} %bitcast.17, bf16[128,2048]{1,0:T(8,128)(2,1)S(1)} %copy-done, bf16[128,2304]{1,0:T(8,128)(2,1)S(1)} %bitcast.14), custom_call_target="tpu_custom_call" | custom-call | flops 134217728 | bytes 1638912 | tf_op jit(solution)/shard_map/pallas_call | solution.py:27
  109.2 16.0 %all-to-all-done.1 = bf16[48,8,384]{2,1,0:T(8,128)(2,1)S(1)} async-done(((bf16[48,8,384]{2,1,0:T(8,128)(2,1)}), bf16[48,8,384]{2,1,0:T(8,128)(2,1)S(1)}, u32[]{:S(2)}, u32[]{:S(2)}) %all-to-all-start.1) | async-done | bytes 294944 | tf_op jit(solution)/shard_map/all_to_all | solution.py:179
  125.2 0.7 shard_map.89
Async XLA Ops:
  6.4 13.2 %copy-start.6 = (bf16[144,896]{1,0:T(8,128)(2,1)S(1)}, bf16[144,896]{1,0:T(8,128)(2,1)}, u32[]{:S(2)}) copy-start(bf16[144,896]{1,0:T(8,128)(2,1)} %get-tuple-element.9) | copy-start | bytes 774148
  6.4 15.2 %copy-start.5 = (bf16[144,896]{1,0:T(8,128)(2,1)S(1)}, bf16[144,896]{1,0:T(8,128)(2,1)}, u32[]{:S(2)}) copy-start(bf16[144,896]{1,0:T(8,128)(2,1)} %get-tuple-element.10) | copy-start | bytes 774148
  6.5 17.2 %copy-start.4 = (bf16[144,896]{1,0:T(8,128)(2,1)S(1)}, bf16[144,896]{1,0:T(8,128)(2,1)}, u32[]{:S(2)}) copy-start(bf16[144,896]{1,0:T(8,128)(2,1)} %get-tuple-element.11) | copy-start | bytes 774148
  6.5 21.7 %copy-start.3 = (s32[128,1]{0,1:T(1,128)S(1)}, s32[128,1]{0,1:T(1,128)}, u32[]{:S(2)}) copy-start(s32[128,1]{0,1:T(1,128)} %param.7) | copy-start | bytes 1540
  6.5 87.1 %copy-start.1 = (bf16[144,896]{1,0:T(8,128)(2,1)S(1)}, bf16[144,896]{1,0:T(8,128)(2,1)}, u32[]{:S(2)}) copy-start(bf16[144,896]{1,0:T(8,128)(2,1)} %get-tuple-element.8.own) | copy-start | bytes 774148
  6.5 87.1 %copy-start.2 = (s32[2]{0:T(128)S(1)}, s32[2]{0:T(128)}, u32[]{:S(2)}) copy-start(s32[2]{0:T(128)} %pad_add_fusion.me) | copy-start | bytes 28
  6.5 89.2 %all-to-all-start = ((bf16[16,8,2304]{2,1,0:T(8,128)(2,1)}), bf16[16,8,2304]{2,1,0:T(8,128)(2,1)S(1)}, u32[]{:S(2)}, u32[]{:S(2)}) async-start(bf16[16,8,2304]{2,1,0:T(8,128)(2,1)} %bitcast.20), calls=%async_computation | async-start | bytes 1179648 | tf_op jit(solution)/shard_map/all_to_all | solution.py:170
  19.6 88.2 %copy-start = (bf16[128,2048]{1,0:T(8,128)(2,1)S(1)}, bf16[128,2048]{1,0:T(8,128)(2,1)}, u32[]{:S(2)}) copy-start(bf16[128,2048]{1,0:T(8,128)(2,1)} %residual.1) | copy-start | bytes 1572868
  19.6 73.9 %collective-permute-start = (bf16[144,896]{1,0:T(8,128)(2,1)S(1)}, bf16[144,896]{1,0:T(8,128)(2,1)S(1)}, u32[]{:S(2)}, u32[]{:S(2)}) collective-permute-start(bf16[144,896]{1,0:T(8,128)(2,1)S(1)} %copy-done.6), channel_id=1, source_target_pairs={{0,1},{1,2},{2,3},{3,0},{4,5},{5,6},{6,7},{7,4},{8,9},{9,10},{10,1... | collective-permute-start | bytes 774152 | tf_op jit(solution)/shard_map/ppermute | solution.py:173
  21.7 71.9 %collective-permute-start.1 = (bf16[144,896]{1,0:T(8,128)(2,1)S(1)}, bf16[144,896]{1,0:T(8,128)(2,1)S(1)}, u32[]{:S(2)}, u32[]{:S(2)}) collective-permute-start(bf16[144,896]{1,0:T(8,128)(2,1)S(1)} %copy-done.5), channel_id=1, source_target_pairs={{0,2},{1,3},{2,0},{3,1},{4,6},{5,7},{6,4},{7,5},{8,10},{9,11},{10,... | collective-permute-start | bytes 774152 | tf_op jit(solution)/shard_map/ppermute | solution.py:173
  23.6 69.9 %collective-permute-start.2 = (bf16[144,896]{1,0:T(8,128)(2,1)S(1)}, bf16[144,896]{1,0:T(8,128)(2,1)S(1)}, u32[]{:S(2)}, u32[]{:S(2)}) collective-permute-start(bf16[144,896]{1,0:T(8,128)(2,1)S(1)} %copy-done.4), channel_id=1, source_target_pairs={{0,3},{1,0},{2,1},{3,2},{4,7},{5,4},{6,5},{7,6},{8,11},{9,8},{10,9... | collective-permute-start | bytes 774152 | tf_op jit(solution)/shard_map/ppermute | solution.py:173
  95.7 29.5 %all-to-all-start.1 = ((bf16[48,8,384]{2,1,0:T(8,128)(2,1)}), bf16[48,8,384]{2,1,0:T(8,128)(2,1)S(1)}, u32[]{:S(2)}, u32[]{:S(2)}) async-start(bf16[48,8,384]{2,1,0:T(8,128)(2,1)} %bitcast.11), calls=%async_computation.1 | async-start | bytes 589824 | tf_op jit(solution)/shard_map/all_to_all | solution.py:179

commit v3 on v2

--- a/solution.py
+++ b/solution.py
@@ -33,70 +33,97 @@
     )(*args)
 
 
+def count_body(routes, out):
+    rows = out.shape[0]
+    hit = (iota((rows, routes.shape[1]), 0) >> 2) == routes[...]
+    total = jnp.sum(hit.astype(F32), axis=1, keepdims=True)
+    out[...] = jnp.broadcast_to(total, out.shape).astype(jnp.int32)
+
+
 def front_body(
-    me, grad, w_out, preact, w_in, inputs,
+    grad, w_out, preact, w_in, inputs,
     send0, send1, send2, send3, slots,
-    grad_v, w_out_v, preact_v, w_in_v, inputs_v, sems,
+    grad_v, w_out_v, preact_v, w_in_v, spread_v, slots_v, sems,
 ):
+    sends = (send0, send1, send2, send3)
     width = grad.shape[1]
     part = width // PARTS
-    copies = []
+    loads = []
     for i in range(PARTS):
         span = pl.ds(i * part, part)
-        copies.append(pltpu.make_async_copy(grad.at[:, span], grad_v.at[:, span], sems.at[2 * i]))
-        copies.append(pltpu.make_async_copy(w_out.at[:, span], w_out_v.at[:, span], sems.at[2 * i + 1]))
+        loads.append(pltpu.make_async_copy(grad.at[:, span], grad_v.at[:, span], sems.at[2 * i]))
+        loads.append(pltpu.make_async_copy(w_out.at[:, span], w_out_v.at[:, span], sems.at[2 * i + 1]))
     n = 2 * PARTS
     preact_copy = pltpu.make_async_copy(preact, preact_v, sems.at[n])
     w_in_copy = pltpu.make_async_copy(w_in, w_in_v, sems.at[n + 1])
-    inputs_copy = pltpu.make_async_copy(inputs, inputs_v, sems.at[n + 2])
-    for c in copies:
+    me = lax.axis_index("x")
+    later = []
+    for i, send in enumerate(sends):
+        first = pl.multiple_of(((me + i) & 3) * 512, 512)
+        later.append(
+            pltpu.make_async_copy(
+                inputs.at[:, pl.ds(first, 512)], send.at[:, pl.ds(384, 512)], sems.at[n + 2 + i]
+            )
+        )
+    for c in loads:
         c.start()
     preact_copy.start()
     w_in_copy.start()
-    inputs_copy.start()
+    for c in later:
+        c.start()
     rows, units = preact_v.shape
     product = jnp.zeros((rows, units), F32)
     for i in range(PARTS):
-        copies[2 * i].wait()
-        copies[2 * i + 1].wait()
+        loads[2 * i].wait()
+        loads[2 * i + 1].wait()
         span = slice(i * part, i * part + part)
         product = product + dot(grad_v[:, span], w_out_v[:, span], 1, 1)
     preact_copy.wait()
     h = jnp.where(preact_v[...].astype(F32) > 0, product, 0.0).astype(BF)
     col = iota((units, 384), 1)
     place = ((col & 7) < 6) & (iota((units, 384), 0) == 6 * (col >> 3) + (col & 7))
-    spread = dot(h, place.astype(BF)).astype(BF)
+    spread_v[...] = dot(h, place.astype(BF)).astype(BF)
+    for i, send in enumerate(sends):
+        c = pltpu.make_async_copy(spread_v, send.at[:, pl.ds(0, 384)], sems.at[n + 6 + i])
+        c.start()
+        later.append(c)
     k = iota((256, rows), 0)
     j = k & 127
     source = CAP * (j >> 3) + jnp.where(k < 128, j & 7, 8)
     picked = dot((iota((256, rows), 1) == source).astype(BF), h).astype(BF)
     w_in_copy.wait()
-    slots[:, :width] = dot(picked[:128], w_in_v[...]).astype(BF)
     row = iota((128, 256), 0) & 7
     last = jnp.zeros((128, 256), F32)
     for r in range(8):
-        got = dot(picked[128:], w_in_v[:, 256 * r : 256 * r + 256])
-        last = jnp.where(row == r, got, last)
-    slots[:, width:] = last.astype(BF)
-    inputs_copy.wait()
-    for i, send in enumerate((send0, send1, send2, send3)):
-        send[:, :384] = spread
-        first = pl.multiple_of(((me[0] + i) & 3) * 512, 512)
-        send[:, 384:] = inputs_v[:, pl.ds(first, 512)]
-
-
-def weight_body(me, own, one, two, three, routes, out):
+        span = slice(256 * r, 256 * r + 256)
+        got = dot(picked, w_in_v[:, span])
+        slots_v[:, span] = got[:128].astype(BF)
+        last = jnp.where(row == r, got[128:], last)
+        if r % 4 == 3:
+            half = pl.ds(256 * (r - 3), 1024)
+            c = pltpu.make_async_copy(slots_v.at[:, half], slots.at[:, half], sems.at[n + 10 + r // 4])
+            c.start()
+            later.append(c)
+    slots_v[:, width:] = last.astype(BF)
+    tail = pl.ds(width, 256)
+    c = pltpu.make_async_copy(slots_v.at[:, tail], slots.at[:, tail], sems.at[n + 12])
+    c.start()
+    later.append(c)
+    for c in later:
+        c.wait()
+
+
+def weight_body(own, one, two, three, counts, out):
     both = jnp.concatenate([own[...], one[...], two[...], three[...]], axis=0)
-    rows, n = both.shape[0], routes.shape[0]
-    hits = (routes[...] == me[1]).astype(F32).astype(BF)
-    lanes = dot(jnp.ones((8, 128), BF), hits, 1, 1)[0:1, :].astype(jnp.int32)
+    rows, n = both.shape[0], counts.shape[0]
+    eye = (iota((n, n), 0) == iota((n, n), 1)).astype(F32).astype(BF)
+    lanes = dot(counts[...].astype(F32).astype(BF), eye, 0, 0)[0:1, :].astype(jnp.int32)
     k = iota((rows, n), 1)
-    first = ((me[0] - (k & 3)) & 3) * (rows // X_DEV) + CAP * (k >> 2)
+    first = ((lax.axis_index("x") - (k & 3)) & 3) * (rows // X_DEV) + CAP * (k >> 2)
     g = iota((rows, n), 0)
     live = ((g >= first) & (g < first + lanes)).astype(F32).astype(BF)
-    mask = dot(live, jnp.ones((n, 128), BF))
-    mask = jnp.concatenate([mask] * 3, axis=1)
-    h = jnp.where(mask > 0.5, both[:, :384].astype(F32), 0.0).astype(BF)
+    mask = dot(live, jnp.ones((n, 128), BF)).astype(BF)
+    h = both[:, :384] * jnp.concatenate([mask] * 3, axis=1)
     part = dot(h, both[:, 384:], 0, 0)
     last = part[:, 384:]
     sub = iota(last.shape, 0) & 7
@@ -145,26 +172,28 @@
     slots, width = saved_inputs.shape[1:]
     units = w_in.shape[1]
     groups = lax.axis_size("z") * lax.axis_size("x")
-    me = jnp.stack([lax.axis_index("x"), lax.axis_index("expert")]).astype(jnp.int32)
     ids = routes.reshape(1, 128)
-    everyone = lax.all_gather(ids, ("expert", "x"), axis=0, tiled=True)
     hbm = pl.BlockSpec(memory_space=pl.ANY)
-    smem = pl.BlockSpec(memory_space=pltpu.SMEM)
-    vmem = pl.BlockSpec(memory_space=pltpu.VMEM)
+    (counts,) = call(count_body, [S((64, 128), jnp.int32)], ids, limit=63)
+    counts = lax.all_to_all(
+        counts.reshape(64, 1, 128), ("expert", "x"), split_axis=0, concat_axis=0, tiled=True
+    ).reshape(64, 128)
     *sends, slot_grad = call(
         front_body,
         [S((slots, 896), BF)] * X_DEV + [S((128, width + 256), BF)],
-        me, expert_grad[0], w_out[0], saved_preact[0], w_in[0], saved_inputs[0],
+        expert_grad[0], w_out[0], saved_preact[0], w_in[0], saved_inputs[0],
         flops=8 * slots * units * width,
         limit=63,
-        in_specs=[smem] + [hbm] * 5,
+        in_specs=[hbm] * 5,
+        out_specs=[hbm] * 5,
         scratch_shapes=[
             pltpu.VMEM((slots, width), BF),
             pltpu.VMEM((units, width), BF),
             pltpu.VMEM((slots, units), BF),
             pltpu.VMEM((units, width), BF),
-            pltpu.VMEM((slots, width), BF),
-            pltpu.SemaphoreType.DMA((2 * PARTS + 3,)),
+            pltpu.VMEM((slots, 384), BF),
+            pltpu.VMEM((128, width + 256), BF),
+            pltpu.SemaphoreType.DMA((2 * PARTS + 13,)),
         ],
     )
     returned = lax.all_to_all(slot_grad, "expert", split_axis=0, concat_axis=0, tiled=True)
@@ -172,9 +201,8 @@
     for i in range(1, X_DEV):
         got.append(lax.ppermute(sends[i], "x", [(j, (j + i) % X_DEV) for j in range(X_DEV)]))
     (part,) = call(
-        weight_body, [S((8 * groups, 384), BF)], me, *got, everyone,
+        weight_body, [S((8 * groups, 384), BF)], *got, counts,
         flops=2 * 576 * 384 * 512,
-        in_specs=[smem] + [vmem] * 5,
     )
     part = lax.all_to_all(part, ("z", "x"), split_axis=0, concat_axis=0, tiled=True)
     (token_grad,) = call(

time: 126 us -> 98.2 us (0.78)
  the two profiles are of different devices: /device:TPU:25 before, /device:TPU:8 now
where the time goes in v3:
time: 98.2 us; the launch traced here: 97.8 us
  starting transfers between devices  47.8 us (49%)
  waiting for transfers between devices  24.9 us (25%)
  Pallas kernels  24.2 us (25%)
    pallas_call x5, Pallas kernels, call(): pl.pallas_call(body, out_shape=outs, compiler_params=pltpu.CompilerParams...  24.2 us
    all_to_all x1, waiting for transfers between devices, shards(): lax.all_to_all(part, ('z', 'x'), split_axis=0, concat_axis=0, tiled=True)  16.9 us
    all_to_all x1, starting transfers between devices, shards(): lax.all_to_all(part, ('z', 'x'), split_axis=0, concat_axis=0, tiled=True)  15.3 us
    all_to_all x1, starting transfers between devices, shards(): lax.all_to_all(counts.reshape(64, 1, 128), ('expert', 'x'), split_axis=0,...  13.5 us
    ppermute x3, starting transfers between devices, shards(): lax.ppermute(sends[i], 'x', [(j, (j + i) % X_DEV) for j in range(X_DEV)])  11.5 us
    ppermute x3, waiting for transfers between devices, shards(): lax.ppermute(sends[i], 'x', [(j, (j + i) % X_DEV) for j in range(X_DEV)])  8.02 us
    all_to_all x1, starting transfers between devices, shards(): lax.all_to_all(slot_grad, 'expert', split_axis=0, concat_axis=0, tiled=True)  7.53 us
  transfers between devices with their start and end apart: 6, of which 3 were waited for; matrix products, arithmetic and copies ran while one was open for 0% of the time, Pallas kernels for 23%

profile of v3, /device:TPU:8, one launch (start us, length us, event | category | flops | bytes accessed | tf_op | source)
XLA Modules:
  0.0 97.8 jit_solution(14269732229323965148)
XLA Ops:
  0.6 1.4 %shard_map.88 = s32[64,128]{1,0:T(8,128)} custom-call(s32[1,128]{1,0:T(1,128)} %bitcast.18), custom_call_target="tpu_custom_call" | custom-call | bytes 33280 | tf_op jit(solution)/shard_map/pallas_call | solution.py:27
  2.0 13.5 %all-to-all-start.1 = ((s32[64,1,128]{2,1,0:T(1,128)}), s32[64,1,128]{2,1,0:T(1,128)S(1)}, u32[]{:S(2)}, u32[]{:S(2)}) async-start(s32[64,1,128]{2,1,0:T(1,128)} %bitcast.25), calls=%async_computation.1 | async-start | bytes 65536 | tf_op jit(solution)/shard_map/all_to_all | solution.py:178
  15.5 19.2 %shard_map.86 = (bf16[144,896]{1,0:T(8,128)(2,1)}, bf16[144,896]{1,0:T(8,128)(2,1)}, bf16[144,896]{1,0:T(8,128)(2,1)}, bf16[144,896]{1,0:T(8,128)(2,1)}, bf16[128,2304]{1,0:T(8,128)(2,1)}) custom-call(bf16[144,2048]{1,0:T(8,128)(2,1)} %bitcast.23, bf16[288,2048]{1,0:T(8,128)(2,1)} %bitcast.20, bf16[144,288]{1,0:T(8,128)(2,1)} %bitcast.26, ...), custom_call_target="tpu_custom_call" | custom-call | flops 679477248 | bytes 5243904 | tf_op jit(solution)/shard_map/pallas_call | solution.py:27
  34.7 0.0 copy-start.5
  34.7 0.0 copy-start.4
  34.8 0.0 copy-start.3
  34.8 0.0 copy-start.1
  34.8 0.0 all-to-all-done.1
  34.8 7.5 %all-to-all-start = ((bf16[16,8,2304]{2,1,0:T(8,128)(2,1)}), bf16[16,8,2304]{2,1,0:T(8,128)(2,1)S(1)}, u32[]{:S(2)}, u32[]{:S(2)}) async-start(bf16[16,8,2304]{2,1,0:T(8,128)(2,1)} %bitcast.22), calls=%async_computation | async-start | bytes 1179648 | tf_op jit(solution)/shard_map/all_to_all | solution.py:199
  42.3 0.0 copy-start
  42.3 0.0 copy-start.2
  42.3 0.0 copy-done.5
  42.3 3.5 %collective-permute-start = (bf16[144,896]{1,0:T(8,128)(2,1)S(1)}, bf16[144,896]{1,0:T(8,128)(2,1)S(1)}, u32[]{:S(2)}, u32[]{:S(2)}) collective-permute-start(bf16[144,896]{1,0:T(8,128)(2,1)S(1)} %copy-done.5), channel_id=1, source_target_pairs={{0,1},{1,2},{2,3},{3,0},{4,5},{5,6},{6,7},{7,4},{8,9},{9,10},{10,1... | collective-permute-start | bytes 774152 | tf_op jit(solution)/shard_map/ppermute | solution.py:202
  45.9 0.0 copy-done.4
  45.9 4.6 %collective-permute-start.1 = (bf16[144,896]{1,0:T(8,128)(2,1)S(1)}, bf16[144,896]{1,0:T(8,128)(2,1)S(1)}, u32[]{:S(2)}, u32[]{:S(2)}) collective-permute-start(bf16[144,896]{1,0:T(8,128)(2,1)S(1)} %copy-done.4), channel_id=1, source_target_pairs={{0,2},{1,3},{2,0},{3,1},{4,6},{5,7},{6,4},{7,5},{8,10},{9,11},{10,... | collective-permute-start | bytes 774152 | tf_op jit(solution)/shard_map/ppermute | solution.py:202
  50.5 0.0 copy-done.3
  50.5 3.4 %collective-permute-start.2 = (bf16[144,896]{1,0:T(8,128)(2,1)S(1)}, bf16[144,896]{1,0:T(8,128)(2,1)S(1)}, u32[]{:S(2)}, u32[]{:S(2)}) collective-permute-start(bf16[144,896]{1,0:T(8,128)(2,1)S(1)} %copy-done.3), channel_id=1, source_target_pairs={{0,3},{1,0},{2,1},{3,2},{4,7},{5,4},{6,5},{7,6},{8,11},{9,8},{10,9... | collective-permute-start | bytes 774152 | tf_op jit(solution)/shard_map/ppermute | solution.py:202
  53.9 0.0 collective-permute-done.one
  53.9 6.4 %collective-permute-done.1.two = bf16[144,896]{1,0:T(8,128)(2,1)S(1)} collective-permute-done((bf16[144,896]{1,0:T(8,128)(2,1)S(1)}, bf16[144,896]{1,0:T(8,128)(2,1)S(1)}, u32[]{:S(2)}, u32[]{:S(2)}) %collective-permute-start.1) | collective-permute-done | bytes 258080 | tf_op jit(solution)/shard_map/ppermute | solution.py:202
  60.3 1.6 %collective-permute-done.2.three = bf16[144,896]{1,0:T(8,128)(2,1)S(1)} collective-permute-done((bf16[144,896]{1,0:T(8,128)(2,1)S(1)}, bf16[144,896]{1,0:T(8,128)(2,1)S(1)}, u32[]{:S(2)}, u32[]{:S(2)}) %collective-permute-start.2) | collective-permute-done | bytes 258080 | tf_op jit(solution)/shard_map/ppermute | solution.py:202
  61.9 0.0 copy-done.1
  61.9 1.6 %shard_map.89 = bf16[384,384]{1,0:T(8,128)(2,1)} custom-call(bf16[144,896]{1,0:T(8,128)(2,1)S(1)} %copy-done.1, bf16[144,896]{1,0:T(8,128)(2,1)S(1)} %collective-permute-done.one, bf16[144,896]{1,0:T(8,128)(2,1)S(1)} %collective-permute-done.1.two, bf16[144,896]{1,0:T(8,128)(2,1)S(1)} %collective-permute-done.2.three, s32[64,128]{1,0:T(8,128)S(1)} %bitcast.17), custom_call_target="tpu_custom_call" | custom-call | flops 226492416 | bytes 1359872 | tf_op jit(solution)/shard_map/pallas_call | solution.py:27
  63.5 0.0 all-to-all-done
  63.5 15.3 %all-to-all-start.2 = ((bf16[48,8,384]{2,1,0:T(8,128)(2,1)}), bf16[48,8,384]{2,1,0:T(8,128)(2,1)S(1)}, u32[]{:S(2)}, u32[]{:S(2)}) async-start(bf16[48,8,384]{2,1,0:T(8,128)(2,1)} %bitcast.11), calls=%async_computation.2 | async-start | bytes 589824 | tf_op jit(solution)/shard_map/all_to_all | solution.py:207
  78.8 0.0 copy-done
  78.8 0.0 copy-done.2
  78.8 1.4 %shard_map.87 = bf16[128,2048]{1,0:T(8,128)(2,1)} custom-call(s32[1,128]{1,0:T(1,128)S(1)} %bitcast.19, bf16[128,2048]{1,0:T(8,128)(2,1)S(1)} %copy-done, bf16[128,2304]{1,0:T(8,128)(2,1)S(1)} %bitcast.15), custom_call_target="tpu_custom_call" | custom-call | flops 134217728 | bytes 1638912 | tf_op jit(solution)/shard_map/pallas_call | solution.py:27
  80.2 16.9 %all-to-all-done.2 = bf16[48,8,384]{2,1,0:T(8,128)(2,1)S(1)} async-done(((bf16[48,8,384]{2,1,0:T(8,128)(2,1)}), bf16[48,8,384]{2,1,0:T(8,128)(2,1)S(1)}, u32[]{:S(2)}, u32[]{:S(2)}) %all-to-all-start.2) | async-done | bytes 294944 | tf_op jit(solution)/shard_map/all_to_all | solution.py:207
  97.1 0.7 shard_map.90
Async XLA Ops:
  2.0 32.8 %all-to-all-start.1 = ((s32[64,1,128]{2,1,0:T(1,128)}), s32[64,1,128]{2,1,0:T(1,128)S(1)}, u32[]{:S(2)}, u32[]{:S(2)}) async-start(s32[64,1,128]{2,1,0:T(1,128)} %bitcast.25), calls=%async_computation.1 | async-start | bytes 65536 | tf_op jit(solution)/shard_map/all_to_all | solution.py:178
  34.7 7.6 %copy-start.5 = (bf16[144,896]{1,0:T(8,128)(2,1)S(1)}, bf16[144,896]{1,0:T(8,128)(2,1)}, u32[]{:S(2)}) copy-start(bf16[144,896]{1,0:T(8,128)(2,1)} %get-tuple-element.9) | copy-start | bytes 774148
  34.7 11.1 %copy-start.4 = (bf16[144,896]{1,0:T(8,128)(2,1)S(1)}, bf16[144,896]{1,0:T(8,128)(2,1)}, u32[]{:S(2)}) copy-start(bf16[144,896]{1,0:T(8,128)(2,1)} %get-tuple-element.10) | copy-start | bytes 774148
  34.8 15.7 %copy-start.3 = (bf16[144,896]{1,0:T(8,128)(2,1)S(1)}, bf16[144,896]{1,0:T(8,128)(2,1)}, u32[]{:S(2)}) copy-start(bf16[144,896]{1,0:T(8,128)(2,1)} %get-tuple-element.11) | copy-start | bytes 774148
  34.8 27.1 %copy-start.1 = (bf16[144,896]{1,0:T(8,128)(2,1)S(1)}, bf16[144,896]{1,0:T(8,128)(2,1)}, u32[]{:S(2)}) copy-start(bf16[144,896]{1,0:T(8,128)(2,1)} %get-tuple-element.8.own) | copy-start | bytes 774148
  34.8 28.7 %all-to-all-start = ((bf16[16,8,2304]{2,1,0:T(8,128)(2,1)}), bf16[16,8,2304]{2,1,0:T(8,128)(2,1)S(1)}, u32[]{:S(2)}, u32[]{:S(2)}) async-start(bf16[16,8,2304]{2,1,0:T(8,128)(2,1)} %bitcast.22), calls=%async_computation | async-start | bytes 1179648 | tf_op jit(solution)/shard_map/all_to_all | solution.py:199
  42.3 36.4 %copy-start = (bf16[128,2048]{1,0:T(8,128)(2,1)S(1)}, bf16[128,2048]{1,0:T(8,128)(2,1)}, u32[]{:S(2)}) copy-start(bf16[128,2048]{1,0:T(8,128)(2,1)} %residual.1) | copy-start | bytes 1572868
  42.3 36.4 %copy-start.2 = (s32[128,1]{0,1:T(1,128)S(1)}, s32[128,1]{0,1:T(1,128)}, u32[]{:S(2)}) copy-start(s32[128,1]{0,1:T(1,128)} %param.7) | copy-start | bytes 1540
  42.3 11.5 %collective-permute-start = (bf16[144,896]{1,0:T(8,128)(2,1)S(1)}, bf16[144,896]{1,0:T(8,128)(2,1)S(1)}, u32[]{:S(2)}, u32[]{:S(2)}) collective-permute-start(bf16[144,896]{1,0:T(8,128)(2,1)S(1)} %copy-done.5), channel_id=1, source_target_pairs={{0,1},{1,2},{2,3},{3,0},{4,5},{5,6},{6,7},{7,4},{8,9},{9,10},{10,1... | collective-permute-start | bytes 774152 | tf_op jit(solution)/shard_map/ppermute | solution.py:202
  45.9 14.4 %collective-permute-start.1 = (bf16[144,896]{1,0:T(8,128)(2,1)S(1)}, bf16[144,896]{1,0:T(8,128)(2,1)S(1)}, u32[]{:S(2)}, u32[]{:S(2)}) collective-permute-start(bf16[144,896]{1,0:T(8,128)(2,1)S(1)} %copy-done.4), channel_id=1, source_target_pairs={{0,2},{1,3},{2,0},{3,1},{4,6},{5,7},{6,4},{7,5},{8,10},{9,11},{10,... | collective-permute-start | bytes 774152 | tf_op jit(solution)/shard_map/ppermute | solution.py:202
  50.5 11.4 %collective-permute-start.2 = (bf16[144,896]{1,0:T(8,128)(2,1)S(1)}, bf16[144,896]{1,0:T(8,128)(2,1)S(1)}, u32[]{:S(2)}, u32[]{:S(2)}) collective-permute-start(bf16[144,896]{1,0:T(8,128)(2,1)S(1)} %copy-done.3), channel_id=1, source_target_pairs={{0,3},{1,0},{2,1},{3,2},{4,7},{5,4},{6,5},{7,6},{8,11},{9,8},{10,9... | collective-permute-start | bytes 774152 | tf_op jit(solution)/shard_map/ppermute | solution.py:202
  63.5 33.6 %all-to-all-start.2 = ((bf16[48,8,384]{2,1,0:T(8,128)(2,1)}), bf16[48,8,384]{2,1,0:T(8,128)(2,1)S(1)}, u32[]{:S(2)}, u32[]{:S(2)}) async-start(bf16[48,8,384]{2,1,0:T(8,128)(2,1)} %bitcast.11), calls=%async_computation.2 | async-start | bytes 589824 | tf_op jit(solution)/shard_map/all_to_all | solution.py:207

commit v4 on v3

v4 whole, which is shorter than its diff:
```python
import functools
import jax
import jax.numpy as jnp
from jax import lax
from jax.experimental import pallas as pl
from jax.experimental.pallas import tpu as pltpu
from jax.sharding import Mesh, PartitionSpec as P

BF = jnp.bfloat16
F32 = jnp.float32
CAP = 9
X_DEV = 4
Z_DEV = 12
PARTS = 4
MIB = 1024 * 1024


def iota(shape, axis):
    return lax.broadcasted_iota(jnp.int32, shape, axis)


def as_bf(mask):
    return mask.astype(F32).astype(BF)


def dot(a, b, ca=1, cb=0):
    return lax.dot_general(a, b, (((ca,), (cb,)), ((), ())), preferred_element_type=F32)


def call(body, outs, *args, flops=0, limit=32, **more):
    size = sum(a.size * a.dtype.itemsize for a in args) + sum(o.size * o.dtype.itemsize for o in outs)
    return pl.pallas_call(
        body,
        out_shape=outs,
        compiler_params=pltpu.CompilerParams(vmem_limit_bytes=limit * MIB),
        cost_estimate=pl.CostEstimate(flops=flops, bytes_accessed=size, transcendentals=0),
        **more,
    )(*args)


def count_body(routes, out):
    hit = iota((out.shape[0], routes.shape[1]), 0) == routes[...]
    total = jnp.sum(hit.astype(F32), axis=1, keepdims=True)
    out[...] = jnp.broadcast_to(total, out.shape).astype(jnp.int32)


def front_body(
    grad, w_out, preact, w_in, hidden, slots,
    grad_v, w_out_v, preact_v, w_in_v, slots_v, sems,
):
    width = grad.shape[1]
    part = width // PARTS
    loads = []
    for i in range(PARTS):
        span = pl.ds(i * part, part)
        loads.append(pltpu.make_async_copy(grad.at[:, span], grad_v.at[:, span], sems.at[2 * i]))
        loads.append(pltpu.make_async_copy(w_out.at[:, span], w_out_v.at[:, span], sems.at[2 * i + 1]))
    n = 2 * PARTS
    preact_copy = pltpu.make_async_copy(preact, preact_v, sems.at[n])
    w_in_copy = pltpu.make_async_copy(w_in, w_in_v, sems.at[n + 1])
    for c in loads:
        c.start()
    preact_copy.start()
    w_in_copy.start()
    rows, units = preact_v.shape
    product = jnp.zeros((rows, units), F32)
    for i in range(PARTS):
        loads[2 * i].wait()
        loads[2 * i + 1].wait()
        span = slice(i * part, i * part + part)
        product = product + dot(grad_v[:, span], w_out_v[:, span], 1, 1)
    preact_copy.wait()
    h = jnp.where(preact_v[...].astype(F32) > 0, product, 0.0).astype(BF)
    hidden[...] = h
    k = iota((256, rows), 0)
    j = k & 127
    source = CAP * (j >> 3) + jnp.where(k < 128, j & 7, 8)
    picked = dot(as_bf(iota((256, rows), 1) == source), h).astype(BF)
    w_in_copy.wait()
    row = iota((128, 256), 0) & 7
    last = jnp.zeros((128, 256), F32)
    stores = []
    for r in range(8):
        span = slice(256 * r, 256 * r + 256)
        got = dot(picked, w_in_v[:, span])
        slots_v[:, span] = got[:128].astype(BF)
        last = jnp.where(row == r, got[128:], last)
        if r % 4 == 3:
            half = pl.ds(256 * (r - 3), 1024)
            stores.append(
                pltpu.make_async_copy(slots_v.at[:, half], slots.at[:, half], sems.at[n + 2 + r // 4])
            )
            stores[-1].start()
    slots_v[:, width:] = last.astype(BF)
    tail = pl.ds(width, 256)
    stores.append(pltpu.make_async_copy(slots_v.at[:, tail], slots.at[:, tail], sems.at[n + 4]))
    stores[-1].start()
    for c in stores:
        c.wait()


def weight_body(hidden, inputs, counts, *outs):
    rows, units = hidden.shape
    j = iota((96, units), 0)
    unit = iota((96, units), 1)
    n = counts.shape[0]
    g = iota((n, rows), 1)
    first = CAP * iota((n, rows), 0)
    live = (g >= first) & (g < first + counts[:, :1])
    mask = as_bf(jnp.sum(live.astype(F32), axis=0, keepdims=True) > 0.5)
    me = lax.axis_index("x")
    for k, out in enumerate(outs):
        owner = X_DEV * (j >> 3) + ((me + k) & 3)
        place = ((j & 7) < 6) & (unit == 6 * owner + (j & 7))
        spread = dot(as_bf(place), hidden[...], 1, 1).astype(BF) * mask
        last = dot(spread, inputs[:, 1536:])
        sub = iota(last.shape, 0) & 7
        for w in range(3):
            span = slice(512 * w, 512 * w + 512)
            tile = dot(spread, inputs[:, span])
            tile = jnp.where(sub == 6, pltpu.roll(last, 6 - w, 0), tile)
            tile = jnp.where(sub == 7, pltpu.roll(last, 4 - w, 0), tile)
            out[:, span] = tile.astype(BF)


def add_body(own, one, two, three, out):
    total = (own[...].astype(F32) + one[...].astype(F32)) + (two[...].astype(F32) + three[...].astype(F32))
    out[...] = total.astype(BF)


def sum_body(scale, parts, out):
    total = parts[0:8, :].astype(F32)
    for z in range(1, parts.shape[0] // 8):
        total = total + parts[8 * z : 8 * z + 8, :].astype(F32)
    total = total / scale
    for u in range(6):
        v, w = u // 3, u % 3
        out[u, :, :1536] = total[u : u + 1, :]
        out[u, :, 1536:] = total[6 + v : 7 + v, 512 * w : 512 * w + 512]


def token_body(routes, residual, returned, out):
    ids = routes[...]
    n = ids.shape[1]
    onehot = (iota((16, n), 0) == ids).astype(F32)
    before = as_bf(iota((n, n), 0) < iota((n, n), 1))
    prefix = dot(onehot.astype(BF), before)
    slot = jnp.sum(onehot * prefix, axis=0, keepdims=True).astype(jnp.int32)
    k = iota((n, n), 0)
    same = (k >> 3) == ids
    pick = as_bf(same & ((k & 7) == slot))
    extra = returned[:, 2048:]
    for r in range(8):
        span = slice(256 * r, 256 * r + 256)
        pick_last = as_bf(same & (slot == 8) & ((k & 7) == r))
        got = dot(pick, returned[:, span], 0, 0) + dot(pick_last, extra, 0, 0)
        out[:, span] = (residual[:, span].astype(F32) + got).astype(BF)


def shards(routes, residual_grad, saved_inputs, saved_preact, expert_grad, w_in, w_out):
    S = jax.ShapeDtypeStruct
    slots, width = saved_inputs.shape[1:]
    units = w_in.shape[1]
    groups = lax.axis_size("z") * lax.axis_size("x")
    ids = routes.reshape(1, 128)
    hbm = pl.BlockSpec(memory_space=pl.ANY)
    vmem = pl.BlockSpec(memory_space=pltpu.VMEM)
    (counts,) = call(count_body, [S((16, 128), jnp.int32)], ids, limit=63)
    counts = lax.all_to_all(
        counts.reshape(16, 1, 128), "expert", split_axis=0, concat_axis=0, tiled=True
    ).reshape(16, 128)
    hidden, slot_grad = call(
        front_body,
        [S((slots, units), BF), S((128, width + 256), BF)],
        expert_grad[0], w_out[0], saved_preact[0], w_in[0],
        flops=6 * slots * units * width,
        limit=63,
        in_specs=[hbm] * 4,
        out_specs=[vmem, hbm],
        scratch_shapes=[
            pltpu.VMEM((slots, width), BF),
            pltpu.VMEM((units, width), BF),
            pltpu.VMEM((slots, units), BF),
            pltpu.VMEM((units, width), BF),
            pltpu.VMEM((128, width + 256), BF),
            pltpu.SemaphoreType.DMA((2 * PARTS + 5,)),
        ],
    )
    returned = lax.all_to_all(slot_grad, "expert", split_axis=0, concat_axis=0, tiled=True)
    sends = call(
        weight_body, [S((8 * Z_DEV, 1536), BF)] * X_DEV, hidden, saved_inputs[0], counts,
        flops=2 * slots * 384 * width,
    )
    got = [sends[0]]
    for i in range(1, X_DEV):
        got.append(lax.ppermute(sends[i], "x", [(j, (j + i) % X_DEV) for j in range(X_DEV)]))
    (part,) = call(add_body, [S((8 * Z_DEV, 1536), BF)], *got)
    part = lax.all_to_all(part, "z", split_axis=0, concat_axis=0, tiled=True)
    (token_grad,) = call(
        token_body, [S((128, width), BF)], ids, residual_grad, returned,
        flops=4 * 128 * 128 * width,
    )
    (grad_in,) = call(
        functools.partial(sum_body, float(groups)), [S((6, 1, width), F32)], part
    )
    return token_grad, jnp.transpose(grad_in, (1, 0, 2))


def solution(mesh):
    fine = Mesh(mesh.devices.reshape(16, Z_DEV, X_DEV), ("expert", "z", "x"))
    tokens = P(("expert", "z", "x"), None)
    buffers = P("expert", ("z", "x"), None)
    weights = P("expert", None, None)
    return jax.shard_map(
        shards,
        mesh=fine,
        in_specs=(tokens, tokens, buffers, buffers, buffers, weights, weights),
        out_specs=(tokens, buffers),
        check_vma=False,
    )
```

time: 98.2 us -> 79.5 us (0.81)
  the two profiles are of different devices: /device:TPU:8 before, /device:TPU:10 now
where the time goes in v4:
time: 79.5 us; the launch traced here: 79 us
  starting transfers between devices  39.1 us (49%)
  waiting for transfers between devices  28.8 us (36%)
  Pallas kernels  10.4 us (13%)
    all_to_all x1, waiting for transfers between devices, shards(): part = lax.all_to_all(part, 'z', split_axis=0, concat_axis=0, tiled=True)  15.8 us
    ppermute x3, starting transfers between devices, shards(): lax.ppermute(sends[i], 'x', [(j, (j + i) % X_DEV) for j in range(X_DEV)])  13.7 us
    all_to_all x1, starting transfers between devices, shards(): part = lax.all_to_all(part, 'z', split_axis=0, concat_axis=0, tiled=True)  12.1 us
    ppermute x3, waiting for transfers between devices, shards(): lax.ppermute(sends[i], 'x', [(j, (j + i) % X_DEV) for j in range(X_DEV)])  11.4 us
    pallas_call x6, Pallas kernels, call(): pl.pallas_call(body, out_shape=outs, compiler_params=pltpu.CompilerParams...  10.4 us
    all_to_all x1, starting transfers between devices, shards(): lax.all_to_all(counts.reshape(16, 1, 128), 'expert', split_axis=0, concat...  7.56 us
    all_to_all x1, starting transfers between devices, shards(): lax.all_to_all(slot_grad, 'expert', split_axis=0, concat_axis=0, tiled=True)  5.75 us
    all_to_all x1, waiting for transfers between devices, shards(): lax.all_to_all(counts.reshape(16, 1, 128), 'expert', split_axis=0, concat...  1.63 us
  transfers between devices with their start and end apart: 6, of which 5 were waited for; matrix products, arithmetic and copies ran while one was open for 0% of the time, Pallas kernels for 11%

profile of v4, /device:TPU:10, one launch (start us, length us, event | category | flops | bytes accessed | tf_op | source)
XLA Modules:
  0.0 79.0 jit_solution(15381927274430281997)
XLA Ops:
  0.6 1.3 %shard_map.88 = s32[16,128]{1,0:T(8,128)} custom-call(s32[1,128]{1,0:T(1,128)} %bitcast.18), custom_call_target="tpu_custom_call" | custom-call | bytes 8704 | tf_op jit(solution)/shard_map/pallas_call | solution.py:32
  2.0 7.6 %all-to-all-start.1 = ((s32[16,1,128]{2,1,0:T(1,128)}), s32[16,1,128]{2,1,0:T(1,128)S(1)}, u32[]{:S(2)}, u32[]{:S(2)}) async-start(s32[16,1,128]{2,1,0:T(1,128)} %bitcast.27), calls=%async_computation.1 | async-start | bytes 16384 | tf_op jit(solution)/shard_map/all_to_all | solution.py:169
  9.5 4.5 %shard_map.86 = (bf16[144,288]{1,0:T(8,128)(2,1)}, bf16[128,2304]{1,0:T(8,128)(2,1)}) custom-call(bf16[144,2048]{1,0:T(8,128)(2,1)} %bitcast.24, bf16[288,2048]{1,0:T(8,128)(2,1)} %bitcast.21, bf16[144,288]{1,0:T(8,128)(2,1)} %bitcast.25, bf16[288,2048]{1,0:T(8,128)(2,1)} %bitcast.22), custom_call_target="tpu_custom_call" | custom-call | flops 509607936 | bytes 3704832 | tf_op jit(solution)/shard_map/pallas_call | solution.py:32
  14.0 0.0 copy-start.2
  14.0 0.0 copy-start.3
  14.0 1.6 %all-to-all-done.1 = s32[16,1,128]{2,1,0:T(1,128)S(1)} async-done(((s32[16,1,128]{2,1,0:T(1,128)}), s32[16,1,128]{2,1,0:T(1,128)S(1)}, u32[]{:S(2)}, u32[]{:S(2)}) %all-to-all-start.1) | async-done | bytes 8224 | tf_op jit(solution)/shard_map/all_to_all | solution.py:169
  15.7 5.8 %all-to-all-start = ((bf16[16,8,2304]{2,1,0:T(8,128)(2,1)}), bf16[16,8,2304]{2,1,0:T(8,128)(2,1)S(1)}, u32[]{:S(2)}, u32[]{:S(2)}) async-start(bf16[16,8,2304]{2,1,0:T(8,128)(2,1)} %bitcast.23), calls=%async_computation | async-start | bytes 1179648 | tf_op jit(solution)/shard_map/all_to_all | solution.py:189
  21.4 0.0 copy-done.2
  21.4 0.0 copy-done.3
  21.4 1.6 %shard_map.89 = (bf16[96,1536]{1,0:T(8,128)(2,1)S(1)}, bf16[96,1536]{1,0:T(8,128)(2,1)S(1)}, bf16[96,1536]{1,0:T(8,128)(2,1)S(1)}, bf16[96,1536]{1,0:T(8,128)(2,1)S(1)}) custom-call(bf16[144,288]{1,0:T(8,128)(2,1)S(1)} %copy-done.3, bf16[144,2048]{1,0:T(8,128)(2,1)S(1)} %bitcast.20, s32[16,128]{1,0:T(8,128)S(1)} %bitcast.17), custom_call_target="tpu_custom_call" | custom-call | flops 226492416 | bytes 1860608 | tf_op jit(solution)/shard_map/pallas_call | solution.py:32
  23.0 0.0 copy-start
  23.1 0.0 copy-start.1
  23.1 3.5 %collective-permute-start = (bf16[96,1536]{1,0:T(8,128)(2,1)S(1)}, bf16[96,1536]{1,0:T(8,128)(2,1)S(1)}, u32[]{:S(2)}, u32[]{:S(2)}) collective-permute-start(bf16[96,1536]{1,0:T(8,128)(2,1)S(1)} %get-tuple-element.11), channel_id=1, source_target_pairs={{0,1},{1,2},{2,3},{3,0},{4,5},{5,6},{6,7},{7,4},{8,9},{9,10},{10,1... | collective-permute-start | bytes 884744 | tf_op jit(solution)/shard_map/ppermute | solution.py:196
  26.6 8.2 %collective-permute-start.1 = (bf16[96,1536]{1,0:T(8,128)(2,1)S(1)}, bf16[96,1536]{1,0:T(8,128)(2,1)S(1)}, u32[]{:S(2)}, u32[]{:S(2)}) collective-permute-start(bf16[96,1536]{1,0:T(8,128)(2,1)S(1)} %get-tuple-element.12), channel_id=1, source_target_pairs={{0,2},{1,3},{2,0},{3,1},{4,6},{5,7},{6,4},{7,5},{8,10},{9,11},{10,... | collective-permute-start | bytes 884744 | tf_op jit(solution)/shard_map/ppermute | solution.py:196
  34.8 1.9 %collective-permute-start.2 = (bf16[96,1536]{1,0:T(8,128)(2,1)S(1)}, bf16[96,1536]{1,0:T(8,128)(2,1)S(1)}, u32[]{:S(2)}, u32[]{:S(2)}) collective-permute-start(bf16[96,1536]{1,0:T(8,128)(2,1)S(1)} %get-tuple-element.13), channel_id=1, source_target_pairs={{0,3},{1,0},{2,1},{3,2},{4,7},{5,4},{6,5},{7,6},{8,11},{9,8},{10,9... | collective-permute-start | bytes 884744 | tf_op jit(solution)/shard_map/ppermute | solution.py:196
  36.8 1.9 %collective-permute-done.one = bf16[96,1536]{1,0:T(8,128)(2,1)S(1)} collective-permute-done((bf16[96,1536]{1,0:T(8,128)(2,1)S(1)}, bf16[96,1536]{1,0:T(8,128)(2,1)S(1)}, u32[]{:S(2)}, u32[]{:S(2)}) %collective-permute-start) | collective-permute-done | bytes 294944 | tf_op jit(solution)/shard_map/ppermute | solution.py:196
  38.6 4.1 %collective-permute-done.1.two = bf16[96,1536]{1,0:T(8,128)(2,1)S(1)} collective-permute-done((bf16[96,1536]{1,0:T(8,128)(2,1)S(1)}, bf16[96,1536]{1,0:T(8,128)(2,1)S(1)}, u32[]{:S(2)}, u32[]{:S(2)}) %collective-permute-start.1) | collective-permute-done | bytes 294944 | tf_op jit(solution)/shard_map/ppermute | solution.py:196
  42.7 5.5 %collective-permute-done.2.three = bf16[96,1536]{1,0:T(8,128)(2,1)S(1)} collective-permute-done((bf16[96,1536]{1,0:T(8,128)(2,1)S(1)}, bf16[96,1536]{1,0:T(8,128)(2,1)S(1)}, u32[]{:S(2)}, u32[]{:S(2)}) %collective-permute-start.2) | collective-permute-done | bytes 294944 | tf_op jit(solution)/shard_map/ppermute | solution.py:196
  48.2 0.9 %shard_map.90 = bf16[96,1536]{1,0:T(8,128)(2,1)} custom-call(bf16[96,1536]{1,0:T(8,128)(2,1)S(1)} %get-tuple-element.10.own, bf16[96,1536]{1,0:T(8,128)(2,1)S(1)} %collective-permute-done.one, bf16[96,1536]{1,0:T(8,128)(2,1)S(1)} %collective-permute-done.1.two, bf16[96,1536]{1,0:T(8,128)(2,1)S(1)} %collective-permute-done.2.three), custom_call_target="tpu_custom_call" | custom-call | bytes 1474560 | tf_op jit(solution)/shard_map/pallas_call | solution.py:32
  49.0 0.0 all-to-all-done
  49.1 12.1 %all-to-all-start.2 = ((bf16[12,8,1536]{2,1,0:T(8,128)(2,1)}), bf16[12,8,1536]{2,1,0:T(8,128)(2,1)S(1)}, u32[]{:S(2)}, u32[]{:S(2)}) async-start(bf16[12,8,1536]{2,1,0:T(8,128)(2,1)} %bitcast.11), calls=%async_computation.2 | async-start | bytes 589824 | tf_op jit(solution)/shard_map/all_to_all | solution.py:198
  61.1 0.0 copy-done
  61.2 0.0 copy-done.1
  61.2 1.4 %shard_map.87 = bf16[128,2048]{1,0:T(8,128)(2,1)} custom-call(s32[1,128]{1,0:T(1,128)S(1)} %bitcast.19, bf16[128,2048]{1,0:T(8,128)(2,1)S(1)} %copy-done, bf16[128,2304]{1,0:T(8,128)(2,1)S(1)} %bitcast.15), custom_call_target="tpu_custom_call" | custom-call | flops 134217728 | bytes 1638912 | tf_op jit(solution)/shard_map/pallas_call | solution.py:32
  62.6 15.8 %all-to-all-done.2 = bf16[12,8,1536]{2,1,0:T(8,128)(2,1)S(1)} async-done(((bf16[12,8,1536]{2,1,0:T(8,128)(2,1)}), bf16[12,8,1536]{2,1,0:T(8,128)(2,1)S(1)}, u32[]{:S(2)}, u32[]{:S(2)}) %all-to-all-start.2) | async-done | bytes 294944 | tf_op jit(solution)/shard_map/all_to_all | solution.py:198
  78.4 0.7 shard_map.91
Async XLA Ops:
  2.0 13.7 %all-to-all-start.1 = ((s32[16,1,128]{2,1,0:T(1,128)}), s32[16,1,128]{2,1,0:T(1,128)S(1)}, u32[]{:S(2)}, u32[]{:S(2)}) async-start(s32[16,1,128]{2,1,0:T(1,128)} %bitcast.27), calls=%async_computation.1 | async-start | bytes 16384 | tf_op jit(solution)/shard_map/all_to_all | solution.py:169
  14.0 7.4 %copy-start.2 = (bf16[1,144,2048]{2,1,0:T(8,128)(2,1)S(1)}, bf16[1,144,2048]{2,1,0:T(8,128)(2,1)}, u32[]{:S(2)}) copy-start(bf16[1,144,2048]{2,1,0:T(8,128)(2,1)} %param.9) | copy-start | bytes 1769476
  14.0 7.4 %copy-start.3 = (bf16[144,288]{1,0:T(8,128)(2,1)S(1)}, bf16[144,288]{1,0:T(8,128)(2,1)}, u32[]{:S(2)}) copy-start(bf16[144,288]{1,0:T(8,128)(2,1)} %get-tuple-element.9.hidden) | copy-start | bytes 248836
  15.7 33.4 %all-to-all-start = ((bf16[16,8,2304]{2,1,0:T(8,128)(2,1)}), bf16[16,8,2304]{2,1,0:T(8,128)(2,1)S(1)}, u32[]{:S(2)}, u32[]{:S(2)}) async-start(bf16[16,8,2304]{2,1,0:T(8,128)(2,1)} %bitcast.23), calls=%async_computation | async-start | bytes 1179648 | tf_op jit(solution)/shard_map/all_to_all | solution.py:189
  23.0 38.1 %copy-start = (bf16[128,2048]{1,0:T(8,128)(2,1)S(1)}, bf16[128,2048]{1,0:T(8,128)(2,1)}, u32[]{:S(2)}) copy-start(bf16[128,2048]{1,0:T(8,128)(2,1)} %residual.1) | copy-start | bytes 1572868
  23.1 38.1 %copy-start.1 = (s32[128,1]{0,1:T(1,128)S(1)}, s32[128,1]{0,1:T(1,128)}, u32[]{:S(2)}) copy-start(s32[128,1]{0,1:T(1,128)} %param.7) | copy-start | bytes 1540
  23.1 15.6 %collective-permute-start = (bf16[96,1536]{1,0:T(8,128)(2,1)S(1)}, bf16[96,1536]{1,0:T(8,128)(2,1)S(1)}, u32[]{:S(2)}, u32[]{:S(2)}) collective-permute-start(bf16[96,1536]{1,0:T(8,128)(2,1)S(1)} %get-tuple-element.11), channel_id=1, source_target_pairs={{0,1},{1,2},{2,3},{3,0},{4,5},{5,6},{6,7},{7,4},{8,9},{9,10},{10,1... | collective-permute-start | bytes 884744 | tf_op jit(solution)/shard_map/ppermute | solution.py:196
  26.6 16.1 %collective-permute-start.1 = (bf16[96,1536]{1,0:T(8,128)(2,1)S(1)}, bf16[96,1536]{1,0:T(8,128)(2,1)S(1)}, u32[]{:S(2)}, u32[]{:S(2)}) collective-permute-start(bf16[96,1536]{1,0:T(8,128)(2,1)S(1)} %get-tuple-element.12), channel_id=1, source_target_pairs={{0,2},{1,3},{2,0},{3,1},{4,6},{5,7},{6,4},{7,5},{8,10},{9,11},{10,... | collective-permute-start | bytes 884744 | tf_op jit(solution)/shard_map/ppermute | solution.py:196
  34.8 13.3 %collective-permute-start.2 = (bf16[96,1536]{1,0:T(8,128)(2,1)S(1)}, bf16[96,1536]{1,0:T(8,128)(2,1)S(1)}, u32[]{:S(2)}, u32[]{:S(2)}) collective-permute-start(bf16[96,1536]{1,0:T(8,128)(2,1)S(1)} %get-tuple-element.13), channel_id=1, source_target_pairs={{0,3},{1,0},{2,1},{3,2},{4,7},{5,4},{6,5},{7,6},{8,11},{9,8},{10,9... | collective-permute-start | bytes 884744 | tf_op jit(solution)/shard_map/ppermute | solution.py:196
  49.1 29.3 %all-to-all-start.2 = ((bf16[12,8,1536]{2,1,0:T(8,128)(2,1)}), bf16[12,8,1536]{2,1,0:T(8,128)(2,1)S(1)}, u32[]{:S(2)}, u32[]{:S(2)}) async-start(bf16[12,8,1536]{2,1,0:T(8,128)(2,1)} %bitcast.11), calls=%async_computation.2 | async-start | bytes 589824 | tf_op jit(solution)/shard_map/all_to_all | solution.py:198

commit v5 on v4

--- a/solution.py
+++ b/solution.py
@@ -36,12 +36,6 @@
         cost_estimate=pl.CostEstimate(flops=flops, bytes_accessed=size, transcendentals=0),
         **more,
     )(*args)
-
-
-def count_body(routes, out):
-    hit = iota((out.shape[0], routes.shape[1]), 0) == routes[...]
-    total = jnp.sum(hit.astype(F32), axis=1, keepdims=True)
-    out[...] = jnp.broadcast_to(total, out.shape).astype(jnp.int32)
 
 
 def front_body(
@@ -74,7 +68,8 @@
     hidden[...] = h
     k = iota((256, rows), 0)
     j = k & 127
-    source = CAP * (j >> 3) + jnp.where(k < 128, j & 7, 8)
+    block = 2 * (j >> 4) + (((j >> 3) & 1) ^ lax.axis_index("core"))
+    source = CAP * block + jnp.where(k < 128, j & 7, 8)
     picked = dot(as_bf(iota((256, rows), 1) == source), h).astype(BF)
     w_in_copy.wait()
     row = iota((128, 256), 0) & 7
@@ -99,14 +94,16 @@
         c.wait()
 
 
-def weight_body(hidden, inputs, counts, *outs):
+def weight_body(hidden, inputs, routes, *outs):
     rows, units = hidden.shape
+    expert = 2 * lax.axis_index("y") + lax.axis_index("core")
+    counts = jnp.sum((routes[...] == expert).astype(F32), axis=1, keepdims=True).astype(jnp.int32)
     j = iota((96, units), 0)
     unit = iota((96, units), 1)
-    n = counts.shape[0]
+    n = routes.shape[0]
     g = iota((n, rows), 1)
     first = CAP * iota((n, rows), 0)
-    live = (g >= first) & (g < first + counts[:, :1])
+    live = (g >= first) & (g < first + counts)
     mask = as_bf(jnp.sum(live.astype(F32), axis=0, keepdims=True) > 0.5)
     me = lax.axis_index("x")
     for k, out in enumerate(outs):
@@ -139,21 +136,30 @@
         out[u, :, 1536:] = total[6 + v : 7 + v, 512 * w : 512 * w + 512]
 
 
-def token_body(routes, residual, returned, out):
+def token_body(routes, residual, near, far, out):
     ids = routes[...]
     n = ids.shape[1]
     onehot = (iota((16, n), 0) == ids).astype(F32)
     before = as_bf(iota((n, n), 0) < iota((n, n), 1))
     prefix = dot(onehot.astype(BF), before)
     slot = jnp.sum(onehot * prefix, axis=0, keepdims=True).astype(jnp.int32)
-    k = iota((n, n), 0)
-    same = (k >> 3) == ids
-    pick = as_bf(same & ((k & 7) == slot))
-    extra = returned[:, 2048:]
+    here = (ids & 1) == lax.axis_index("core")
+    k = iota((near.shape[0], n), 0)
+    same_near = here & ((k >> 3) == 2 * (ids >> 1))
+    c_near = k & 7
+    k = iota((far.shape[0], n), 0)
+    same_far = jnp.logical_not(here) & ((k >> 3) == (ids >> 1))
+    c_far = k & 7
+    pick_near = as_bf(same_near & (c_near == slot))
+    pick_far = as_bf(same_far & (c_far == slot))
+    last_near = near[:, 2048:]
+    last_far = far[:, 2048:]
     for r in range(8):
         span = slice(256 * r, 256 * r + 256)
-        pick_last = as_bf(same & (slot == 8) & ((k & 7) == r))
-        got = dot(pick, returned[:, span], 0, 0) + dot(pick_last, extra, 0, 0)
+        tail_near = as_bf(same_near & (slot == 8) & (c_near == r))
+        tail_far = as_bf(same_far & (slot == 8) & (c_far == r))
+        got = dot(pick_near, near[:, span], 0, 0) + dot(pick_far, far[:, span], 0, 0)
+        got = got + dot(tail_near, last_near, 0, 0) + dot(tail_far, last_far, 0, 0)
         out[:, span] = (residual[:, span].astype(F32) + got).astype(BF)
 
 
@@ -165,9 +171,9 @@
     ids = routes.reshape(1, 128)
     hbm = pl.BlockSpec(memory_space=pl.ANY)
     vmem = pl.BlockSpec(memory_space=pltpu.VMEM)
-    (counts,) = call(count_body, [S((16, 128), jnp.int32)], ids, limit=63)
-    counts = lax.all_to_all(
-        counts.reshape(16, 1, 128), "expert", split_axis=0, concat_axis=0, tiled=True
+    experts = ("y", "core")
+    everyone = lax.all_to_all(
+        jnp.broadcast_to(ids[:, None], (16, 1, 128)), experts, split_axis=0, concat_axis=0, tiled=True
     ).reshape(16, 128)
     hidden, slot_grad = call(
         front_body,
@@ -186,20 +192,24 @@
             pltpu.SemaphoreType.DMA((2 * PARTS + 5,)),
         ],
     )
-    returned = lax.all_to_all(slot_grad, "expert", split_axis=0, concat_axis=0, tiled=True)
     sends = call(
-        weight_body, [S((8 * Z_DEV, 1536), BF)] * X_DEV, hidden, saved_inputs[0], counts,
+        weight_body, [S((8 * Z_DEV, 1536), BF)] * X_DEV, hidden, saved_inputs[0], everyone,
         flops=2 * slots * 384 * width,
     )
+    *sends, slot_grad = lax.optimization_barrier((*sends, slot_grad))
+    near = lax.all_to_all(slot_grad, "y", split_axis=0, concat_axis=0, tiled=True)
+    far = near.reshape(8, 2, 8, width + 256)[:, 1].reshape(64, width + 256)
+    far = lax.ppermute(far, "core", [(0, 1), (1, 0)])
     got = [sends[0]]
-    for i in range(1, X_DEV):
+    for i in (2, 1, 3):
         got.append(lax.ppermute(sends[i], "x", [(j, (j + i) % X_DEV) for j in range(X_DEV)]))
     (part,) = call(add_body, [S((8 * Z_DEV, 1536), BF)], *got)
     part = lax.all_to_all(part, "z", split_axis=0, concat_axis=0, tiled=True)
     (token_grad,) = call(
-        token_body, [S((128, width), BF)], ids, residual_grad, returned,
-        flops=4 * 128 * 128 * width,
-    )
+        token_body, [S((128, width), BF)], ids, residual_grad, near, far,
+        flops=6 * 128 * 128 * width,
+    )
+    token_grad, part = lax.optimization_barrier((token_grad, part))
     (grad_in,) = call(
         functools.partial(sum_body, float(groups)), [S((6, 1, width), F32)], part
     )
@@ -207,10 +217,10 @@
 
 
 def solution(mesh):
-    fine = Mesh(mesh.devices.reshape(16, Z_DEV, X_DEV), ("expert", "z", "x"))
-    tokens = P(("expert", "z", "x"), None)
-    buffers = P("expert", ("z", "x"), None)
-    weights = P("expert", None, None)
+    fine = Mesh(mesh.devices.reshape(8, 2, Z_DEV, X_DEV), ("y", "core", "z", "x"))
+    tokens = P(("y", "core", "z", "x"), None)
+    buffers = P(("y", "core"), ("z", "x"), None)
+    weights = P(("y", "core"), None, None)
     return jax.shard_map(
         shards,
         mesh=fine,

time: 79.5 us -> 76.4 us (0.961)
  the two profiles are of different devices: /device:TPU:10 before, /device:TPU:12 now
where the time goes in v5:
time: 76.4 us; the launch traced here: 76 us
  starting transfers between devices  41.4 us (54%)
  waiting for transfers between devices  22.4 us (29%)
  Pallas kernels  9.34 us (12%)
  local copies, waits for them, and re-layouts  2.19 us (3%)
    ppermute x3, starting transfers between devices, shards(): lax.ppermute(sends[i], 'x', [(j, (j + i) % X_DEV) for j in range(X_DEV)])  13.6 us
    all_to_all x1, starting transfers between devices, shards(): part = lax.all_to_all(part, 'z', split_axis=0, concat_axis=0, tiled=True)  12.7 us
    all_to_all x1, waiting for transfers between devices, shards(): part = lax.all_to_all(part, 'z', split_axis=0, concat_axis=0, tiled=True)  12 us
    pallas_call x5, Pallas kernels, call(): pl.pallas_call(body, out_shape=outs, compiler_params=pltpu.CompilerParams...  9.34 us
    all_to_all x1, starting transfers between devices, shards(): lax.all_to_all(jnp.broadcast_to(ids[:, None], (16, 1, 128)), experts, spl...  7.56 us
    ppermute x3, waiting for transfers between devices, shards(): lax.ppermute(sends[i], 'x', [(j, (j + i) % X_DEV) for j in range(X_DEV)])  7.21 us
    all_to_all x1, starting transfers between devices, shards(): lax.all_to_all(slot_grad, 'y', split_axis=0, concat_axis=0, tiled=True)  5.61 us
    ppermute x1, starting transfers between devices, shards(): far = lax.ppermute(far, 'core', [(0, 1), (1, 0)])  1.92 us
  transfers between devices with their start and end apart: 7, of which 5 were waited for; matrix products, arithmetic and copies ran while one was open for 0% of the time, Pallas kernels for 9%

profile of v5, /device:TPU:12, one launch (start us, length us, event | category | flops | bytes accessed | tf_op | source)
XLA Modules:
  0.0 76.0 jit_solution(12856132414120544381)
XLA Ops:
  0.6 1.3 %broadcast_in_dim.8 = s32[16,1,128]{2,1,0:T(1,128)} broadcast(s32[128]{0:T(128)} %bitcast.20), dimensions={2} | broadcast | bytes 8704 | tf_op jit(solution)/shard_map/broadcast_in_dim | solution.py:176
  1.9 7.6 %all-to-all-start = ((s32[16,1,128]{2,1,0:T(1,128)}), s32[16,1,128]{2,1,0:T(1,128)S(1)}, u32[]{:S(2)}, u32[]{:S(2)}) async-start(s32[16,1,128]{2,1,0:T(1,128)} %broadcast_in_dim.8), calls=%async_computation | async-start | bytes 16384 | tf_op jit(solution)/shard_map/all_to_all | solution.py:175
  9.5 0.0 copy-start.2
  9.5 4.5 %shard_map.86 = (bf16[144,288]{1,0:T(8,128)(2,1)}, bf16[128,2304]{1,0:T(8,128)(2,1)}) custom-call(bf16[144,2048]{1,0:T(8,128)(2,1)} %bitcast.26, bf16[288,2048]{1,0:T(8,128)(2,1)} %bitcast.23, bf16[144,288]{1,0:T(8,128)(2,1)} %bitcast.27, bf16[288,2048]{1,0:T(8,128)(2,1)} %bitcast.24), custom_call_target="tpu_custom_call" | custom-call | flops 509607936 | bytes 3704832 | tf_op jit(solution)/shard_map/pallas_call | solution.py:32
  13.9 1.6 %all-to-all-done = s32[16,1,128]{2,1,0:T(1,128)S(1)} async-done(((s32[16,1,128]{2,1,0:T(1,128)}), s32[16,1,128]{2,1,0:T(1,128)S(1)}, u32[]{:S(2)}, u32[]{:S(2)}) %all-to-all-start) | async-done | bytes 8224 | tf_op jit(solution)/shard_map/all_to_all | solution.py:175
  15.6 0.0 copy-done.2
  15.6 0.0 copy-start.3
  15.6 0.9 %copy-done.3 = bf16[144,288]{1,0:T(8,128)(2,1)S(1)} copy-done((bf16[144,288]{1,0:T(8,128)(2,1)S(1)}, bf16[144,288]{1,0:T(8,128)(2,1)}, u32[]{:S(2)}) %copy-start.3) | copy-done | bytes 82968
  16.5 1.6 %shard_map.87 = (bf16[96,1536]{1,0:T(8,128)(2,1)S(1)}, bf16[96,1536]{1,0:T(8,128)(2,1)S(1)}, bf16[96,1536]{1,0:T(8,128)(2,1)S(1)}, bf16[96,1536]{1,0:T(8,128)(2,1)S(1)}) custom-call(bf16[144,288]{1,0:T(8,128)(2,1)S(1)} %copy-done.3, bf16[144,2048]{1,0:T(8,128)(2,1)S(1)} %bitcast.22, s32[16,128]{1,0:T(8,128)S(1)} %bitcast.19), custom_call_target="tpu_custom_call" | custom-call | flops 226492416 | bytes 1860608 | tf_op jit(solution)/shard_map/pallas_call | solution.py:32
  18.1 5.6 %all-to-all-start.1 = ((bf16[8,16,2304]{2,1,0:T(8,128)(2,1)}), bf16[8,16,2304]{2,1,0:T(8,128)(2,1)S(1)}, u32[]{:S(2)}, u32[]{:S(2)}) async-start(bf16[8,16,2304]{2,1,0:T(8,128)(2,1)} %bitcast.25), calls=%async_computation.1 | async-start | bytes 1179648 | tf_op jit(solution)/shard_map/all_to_all | solution.py:200
  23.7 0.0 copy-start
  23.7 0.0 copy-start.1
  23.7 7.7 %collective-permute-start.1 = (bf16[96,1536]{1,0:T(8,128)(2,1)S(1)}, bf16[96,1536]{1,0:T(8,128)(2,1)S(1)}, u32[]{:S(2)}, u32[]{:S(2)}) collective-permute-start(bf16[96,1536]{1,0:T(8,128)(2,1)S(1)} %get-tuple-element.23), channel_id=1, source_target_pairs={{0,2},{1,3},{2,0},{3,1},{4,6},{5,7},{6,4},{7,5},{8,10},{9,11},{10,... | collective-permute-start | bytes 884744 | tf_op jit(solution)/shard_map/ppermute | solution.py:205
  31.5 1.9 %collective-permute-start.2 = (bf16[96,1536]{1,0:T(8,128)(2,1)S(1)}, bf16[96,1536]{1,0:T(8,128)(2,1)S(1)}, u32[]{:S(2)}, u32[]{:S(2)}) collective-permute-start(bf16[96,1536]{1,0:T(8,128)(2,1)S(1)} %get-tuple-element.24), channel_id=1, source_target_pairs={{0,1},{1,2},{2,3},{3,0},{4,5},{5,6},{6,7},{7,4},{8,9},{9,10},{10,1... | collective-permute-start | bytes 884744 | tf_op jit(solution)/shard_map/ppermute | solution.py:205
  33.4 3.9 %collective-permute-start.3 = (bf16[96,1536]{1,0:T(8,128)(2,1)S(1)}, bf16[96,1536]{1,0:T(8,128)(2,1)S(1)}, u32[]{:S(2)}, u32[]{:S(2)}) collective-permute-start(bf16[96,1536]{1,0:T(8,128)(2,1)S(1)} %get-tuple-element.25), channel_id=1, source_target_pairs={{0,3},{1,0},{2,1},{3,2},{4,7},{5,4},{6,5},{7,6},{8,11},{9,8},{10,9... | collective-permute-start | bytes 884744 | tf_op jit(solution)/shard_map/ppermute | solution.py:205
  37.3 2.0 %collective-permute-done.1.one = bf16[96,1536]{1,0:T(8,128)(2,1)S(1)} collective-permute-done((bf16[96,1536]{1,0:T(8,128)(2,1)S(1)}, bf16[96,1536]{1,0:T(8,128)(2,1)S(1)}, u32[]{:S(2)}, u32[]{:S(2)}) %collective-permute-start.1) | collective-permute-done | bytes 294944 | tf_op jit(solution)/shard_map/ppermute | solution.py:205
  39.4 5.2 %collective-permute-done.2.two = bf16[96,1536]{1,0:T(8,128)(2,1)S(1)} collective-permute-done((bf16[96,1536]{1,0:T(8,128)(2,1)S(1)}, bf16[96,1536]{1,0:T(8,128)(2,1)S(1)}, u32[]{:S(2)}, u32[]{:S(2)}) %collective-permute-start.2) | collective-permute-done | bytes 294944 | tf_op jit(solution)/shard_map/ppermute | solution.py:205
  44.5 0.0 collective-permute-done.3.three
  44.5 0.9 %shard_map.89 = bf16[96,1536]{1,0:T(8,128)(2,1)} custom-call(bf16[96,1536]{1,0:T(8,128)(2,1)S(1)} %get-tuple-element.22.own, bf16[96,1536]{1,0:T(8,128)(2,1)S(1)} %collective-permute-done.1.one, bf16[96,1536]{1,0:T(8,128)(2,1)S(1)} %collective-permute-done.2.two, bf16[96,1536]{1,0:T(8,128)(2,1)S(1)} %collective-permute-done.3.three), custom_call_target="tpu_custom_call" | custom-call | bytes 1474560 | tf_op jit(solution)/shard_map/pallas_call | solution.py:32
  45.4 0.0 all-to-all-done.1
  45.4 12.7 %all-to-all-start.2 = ((bf16[12,8,1536]{2,1,0:T(8,128)(2,1)}), bf16[12,8,1536]{2,1,0:T(8,128)(2,1)S(1)}, u32[]{:S(2)}, u32[]{:S(2)}) async-start(bf16[12,8,1536]{2,1,0:T(8,128)(2,1)} %bitcast.12), calls=%async_computation.2 | async-start | bytes 589824 | tf_op jit(solution)/shard_map/all_to_all | solution.py:207
  58.1 1.9 %collective-permute-start = (bf16[64,2304]{1,0:T(8,128)(2,1)S(1)}, bf16[64,2304]{1,0:T(8,128)(2,1)S(1)}, u32[]{:S(2)}, u32[]{:S(2)}) collective-permute-start(bf16[64,2304]{1,0:T(8,128)(2,1)S(1)} %slice_bitcast_fusion), channel_id=1, source_target_pairs={{0,48},{48,0},{1,49},{49,1},{2,50},{50,2},{3,51},{51,3},{4,52},{52... | collective-permute-start | bytes 884744 | tf_op jit(solution)/shard_map/ppermute | solution.py:202
  60.0 1.5 %collective-permute-done.far = bf16[64,2304]{1,0:T(8,128)(2,1)S(1)} collective-permute-done((bf16[64,2304]{1,0:T(8,128)(2,1)S(1)}, bf16[64,2304]{1,0:T(8,128)(2,1)S(1)}, u32[]{:S(2)}, u32[]{:S(2)}) %collective-permute-start) | collective-permute-done | bytes 294944 | tf_op jit(solution)/shard_map/ppermute | solution.py:202
  61.6 0.0 copy-done
  61.6 0.0 copy-done.1
  61.6 1.7 %shard_map.88 = bf16[128,2048]{1,0:T(8,128)(2,1)} custom-call(s32[1,128]{1,0:T(1,128)S(1)} %bitcast.21, bf16[128,2048]{1,0:T(8,128)(2,1)S(1)} %copy-done, bf16[128,2304]{1,0:T(8,128)(2,1)S(1)} %bitcast.17, bf16[64,2304]{1,0:T(8,128)(2,1)S(1)} %collective-permute-done.far), custom_call_target="tpu_custom_call" | custom-call | flops 201326592 | bytes 1933824 | tf_op jit(solution)/shard_map/pallas_call | solution.py:32
  63.3 12.0 %all-to-all-done.2 = bf16[12,8,1536]{2,1,0:T(8,128)(2,1)S(1)} async-done(((bf16[12,8,1536]{2,1,0:T(8,128)(2,1)}), bf16[12,8,1536]{2,1,0:T(8,128)(2,1)S(1)}, u32[]{:S(2)}, u32[]{:S(2)}) %all-to-all-start.2) | async-done | bytes 294944 | tf_op jit(solution)/shard_map/all_to_all | solution.py:207
  75.3 0.7 shard_map.90
  (1 shorter events, 0.0 us)
Async XLA Ops:
  1.9 13.7 %all-to-all-start = ((s32[16,1,128]{2,1,0:T(1,128)}), s32[16,1,128]{2,1,0:T(1,128)S(1)}, u32[]{:S(2)}, u32[]{:S(2)}) async-start(s32[16,1,128]{2,1,0:T(1,128)} %broadcast_in_dim.8), calls=%async_computation | async-start | bytes 16384 | tf_op jit(solution)/shard_map/all_to_all | solution.py:175
  9.5 6.1 %copy-start.2 = (bf16[1,144,2048]{2,1,0:T(8,128)(2,1)S(1)}, bf16[1,144,2048]{2,1,0:T(8,128)(2,1)}, u32[]{:S(2)}) copy-start(bf16[1,144,2048]{2,1,0:T(8,128)(2,1)} %param.9) | copy-start | bytes 1769476
  15.6 0.9 %copy-start.3 = (bf16[144,288]{1,0:T(8,128)(2,1)S(1)}, bf16[144,288]{1,0:T(8,128)(2,1)}, u32[]{:S(2)}) copy-start(bf16[144,288]{1,0:T(8,128)(2,1)} %get-tuple-element.15.hidden) | copy-start | bytes 248836
  18.1 27.3 %all-to-all-start.1 = ((bf16[8,16,2304]{2,1,0:T(8,128)(2,1)}), bf16[8,16,2304]{2,1,0:T(8,128)(2,1)S(1)}, u32[]{:S(2)}, u32[]{:S(2)}) async-start(bf16[8,16,2304]{2,1,0:T(8,128)(2,1)} %bitcast.25), calls=%async_computation.1 | async-start | bytes 1179648 | tf_op jit(solution)/shard_map/all_to_all | solution.py:200
  23.7 37.9 %copy-start = (bf16[128,2048]{1,0:T(8,128)(2,1)S(1)}, bf16[128,2048]{1,0:T(8,128)(2,1)}, u32[]{:S(2)}) copy-start(bf16[128,2048]{1,0:T(8,128)(2,1)} %residual.1) | copy-start | bytes 1572868
  23.7 37.9 %copy-start.1 = (s32[128,1]{0,1:T(1,128)S(1)}, s32[128,1]{0,1:T(1,128)}, u32[]{:S(2)}) copy-start(s32[128,1]{0,1:T(1,128)} %param.7) | copy-start | bytes 1540
  23.7 15.6 %collective-permute-start.1 = (bf16[96,1536]{1,0:T(8,128)(2,1)S(1)}, bf16[96,1536]{1,0:T(8,128)(2,1)S(1)}, u32[]{:S(2)}, u32[]{:S(2)}) collective-permute-start(bf16[96,1536]{1,0:T(8,128)(2,1)S(1)} %get-tuple-element.23), channel_id=1, source_target_pairs={{0,2},{1,3},{2,0},{3,1},{4,6},{5,7},{6,4},{7,5},{8,10},{9,11},{10,... | collective-permute-start | bytes 884744 | tf_op jit(solution)/shard_map/ppermute | solution.py:205
  31.5 13.1 %collective-permute-start.2 = (bf16[96,1536]{1,0:T(8,128)(2,1)S(1)}, bf16[96,1536]{1,0:T(8,128)(2,1)S(1)}, u32[]{:S(2)}, u32[]{:S(2)}) collective-permute-start(bf16[96,1536]{1,0:T(8,128)(2,1)S(1)} %get-tuple-element.24), channel_id=1, source_target_pairs={{0,1},{1,2},{2,3},{3,0},{4,5},{5,6},{6,7},{7,4},{8,9},{9,10},{10,1... | collective-permute-start | bytes 884744 | tf_op jit(solution)/shard_map/ppermute | solution.py:205
  33.4 11.1 %collective-permute-start.3 = (bf16[96,1536]{1,0:T(8,128)(2,1)S(1)}, bf16[96,1536]{1,0:T(8,128)(2,1)S(1)}, u32[]{:S(2)}, u32[]{:S(2)}) collective-permute-start(bf16[96,1536]{1,0:T(8,128)(2,1)S(1)} %get-tuple-element.25), channel_id=1, source_target_pairs={{0,3},{1,0},{2,1},{3,2},{4,7},{5,4},{6,5},{7,6},{8,11},{9,8},{10,9... | collective-permute-start | bytes 884744 | tf_op jit(solution)/shard_map/ppermute | solution.py:205
  45.4 29.9 %all-to-all-start.2 = ((bf16[12,8,1536]{2,1,0:T(8,128)(2,1)}), bf16[12,8,1536]{2,1,0:T(8,128)(2,1)S(1)}, u32[]{:S(2)}, u32[]{:S(2)}) async-start(bf16[12,8,1536]{2,1,0:T(8,128)(2,1)} %bitcast.12), calls=%async_computation.2 | async-start | bytes 589824 | tf_op jit(solution)/shard_map/all_to_all | solution.py:207
  58.1 3.5 %collective-permute-start = (bf16[64,2304]{1,0:T(8,128)(2,1)S(1)}, bf16[64,2304]{1,0:T(8,128)(2,1)S(1)}, u32[]{:S(2)}, u32[]{:S(2)}) collective-permute-start(bf16[64,2304]{1,0:T(8,128)(2,1)S(1)} %slice_bitcast_fusion), channel_id=1, source_target_pairs={{0,48},{48,0},{1,49},{49,1},{2,50},{50,2},{3,51},{51,3},{4,52},{52... | collective-permute-start | bytes 884744 | tf_op jit(solution)/shard_map/ppermute | solution.py:202

commit v6 on v5

--- a/solution.py
+++ b/solution.py
@@ -105,9 +105,10 @@
     first = CAP * iota((n, rows), 0)
     live = (g >= first) & (g < first + counts)
     mask = as_bf(jnp.sum(live.astype(F32), axis=0, keepdims=True) > 0.5)
-    me = lax.axis_index("x")
     for k, out in enumerate(outs):
-        owner = X_DEV * (j >> 3) + ((me + k) & 3)
+        z = 2 * (j >> 4) + (lax.axis_index("zl") ^ (k >> 1))
+        x = 2 * ((j >> 3) & 1) + (lax.axis_index("xl") ^ (k & 1))
+        owner = X_DEV * z + x
         place = ((j & 7) < 6) & (unit == 6 * owner + (j & 7))
         spread = dot(as_bf(place), hidden[...], 1, 1).astype(BF) * mask
         last = dot(spread, inputs[:, 1536:])
@@ -167,7 +168,7 @@
     S = jax.ShapeDtypeStruct
     slots, width = saved_inputs.shape[1:]
     units = w_in.shape[1]
-    groups = lax.axis_size("z") * lax.axis_size("x")
+    groups = Z_DEV * X_DEV
     ids = routes.reshape(1, 128)
     hbm = pl.BlockSpec(memory_space=pl.ANY)
     vmem = pl.BlockSpec(memory_space=pltpu.VMEM)
@@ -193,18 +194,19 @@
         ],
     )
     sends = call(
-        weight_body, [S((8 * Z_DEV, 1536), BF)] * X_DEV, hidden, saved_inputs[0], everyone,
+        weight_body, [S((96, 1536), BF)] * 4, hidden, saved_inputs[0], everyone,
         flops=2 * slots * 384 * width,
     )
     *sends, slot_grad = lax.optimization_barrier((*sends, slot_grad))
     near = lax.all_to_all(slot_grad, "y", split_axis=0, concat_axis=0, tiled=True)
     far = near.reshape(8, 2, 8, width + 256)[:, 1].reshape(64, width + 256)
     far = lax.ppermute(far, "core", [(0, 1), (1, 0)])
-    got = [sends[0]]
-    for i in (2, 1, 3):
-        got.append(lax.ppermute(sends[i], "x", [(j, (j + i) % X_DEV) for j in range(X_DEV)]))
-    (part,) = call(add_body, [S((8 * Z_DEV, 1536), BF)], *got)
-    part = lax.all_to_all(part, "z", split_axis=0, concat_axis=0, tiled=True)
+    both = ("zl", "xl")
+    got = [lax.ppermute(sends[3], both, [(0, 3), (1, 2), (2, 1), (3, 0)])]
+    got.append(lax.ppermute(sends[2], "zl", [(0, 1), (1, 0)]))
+    got.append(lax.ppermute(sends[1], "xl", [(0, 1), (1, 0)]))
+    (part,) = call(add_body, [S((96, 1536), BF)], sends[0], *got)
+    part = lax.all_to_all(part, ("zh", "xh"), split_axis=0, concat_axis=0, tiled=True)
     (token_grad,) = call(
         token_body, [S((128, width), BF)], ids, residual_grad, near, far,
         flops=6 * 128 * 128 * width,
@@ -217,9 +219,10 @@
 
 
 def solution(mesh):
-    fine = Mesh(mesh.devices.reshape(8, 2, Z_DEV, X_DEV), ("y", "core", "z", "x"))
-    tokens = P(("y", "core", "z", "x"), None)
-    buffers = P(("y", "core"), ("z", "x"), None)
+    fine = Mesh(mesh.devices.reshape(8, 2, 6, 2, 2, 2), ("y", "core", "zh", "zl", "xh", "xl"))
+    dp = ("zh", "zl", "xh", "xl")
+    tokens = P(("y", "core", *dp), None)
+    buffers = P(("y", "core"), dp, None)
     weights = P(("y", "core"), None, None)
     return jax.shard_map(
         shards,

time: 76.4 us -> 78.7 us (1.030)
  the two profiles are of different devices: /device:TPU:12 before, /device:TPU:64 now
where the time goes in v6:
time: 78.7 us; the launch traced here: 78.2 us
  starting transfers between devices  39.6 us (50%)
  waiting for transfers between devices  26.3 us (33%)
  Pallas kernels  9.31 us (12%)
  local copies, waits for them, and re-layouts  2.19 us (3%)
    all_to_all x1, starting transfers between devices, shards(): lax.all_to_all(part, ('zh', 'xh'), split_axis=0, concat_axis=0, tiled=True)  14.2 us
    all_to_all x1, waiting for transfers between devices, shards(): lax.all_to_all(part, ('zh', 'xh'), split_axis=0, concat_axis=0, tiled=True)  13.7 us
    pallas_call x5, Pallas kernels, call(): pl.pallas_call(body, out_shape=outs, compiler_params=pltpu.CompilerParams...  9.31 us
    ppermute x1, waiting for transfers between devices, shards(): got.append(lax.ppermute(sends[2], 'zl', [(0, 1), (1, 0)]))  8.03 us
    all_to_all x1, starting transfers between devices, shards(): lax.all_to_all(jnp.broadcast_to(ids[:, None], (16, 1, 128)), experts, spl...  7.21 us
    ppermute x1, starting transfers between devices, shards(): got.append(lax.ppermute(sends[2], 'zl', [(0, 1), (1, 0)]))  6.21 us
    all_to_all x1, starting transfers between devices, shards(): lax.all_to_all(slot_grad, 'y', split_axis=0, concat_axis=0, tiled=True)  4.15 us
    ppermute x1, starting transfers between devices, shards(): got.append(lax.ppermute(sends[1], 'xl', [(0, 1), (1, 0)]))  3.37 us
  transfers between devices with their start and end apart: 7, of which 4 were waited for; matrix products, arithmetic and copies ran while one was open for 0% of the time, Pallas kernels for 9%

profile of v6, /device:TPU:64, one launch (start us, length us, event | category | flops | bytes accessed | tf_op | source)
XLA Modules:
  0.0 78.2 jit_solution(17444161935657317883)
XLA Ops:
  0.6 1.3 %broadcast_in_dim.8 = s32[16,1,128]{2,1,0:T(1,128)} broadcast(s32[128]{0:T(128)} %bitcast.20), dimensions={2} | broadcast | bytes 8704 | tf_op jit(solution)/shard_map/broadcast_in_dim | solution.py:177
  1.9 7.2 %all-to-all-start = ((s32[16,1,128]{2,1,0:T(1,128)}), s32[16,1,128]{2,1,0:T(1,128)S(1)}, u32[]{:S(2)}, u32[]{:S(2)}) async-start(s32[16,1,128]{2,1,0:T(1,128)} %broadcast_in_dim.8), calls=%async_computation | async-start | bytes 16384 | tf_op jit(solution)/shard_map/all_to_all | solution.py:176
  9.1 0.0 copy-start.2
  9.1 4.5 %shard_map.86 = (bf16[144,288]{1,0:T(8,128)(2,1)}, bf16[128,2304]{1,0:T(8,128)(2,1)}) custom-call(bf16[144,2048]{1,0:T(8,128)(2,1)} %bitcast.26, bf16[288,2048]{1,0:T(8,128)(2,1)} %bitcast.23, bf16[144,288]{1,0:T(8,128)(2,1)} %bitcast.27, bf16[288,2048]{1,0:T(8,128)(2,1)} %bitcast.24), custom_call_target="tpu_custom_call" | custom-call | flops 509607936 | bytes 3704832 | tf_op jit(solution)/shard_map/pallas_call | solution.py:32
  13.6 3.0 %all-to-all-done = s32[16,1,128]{2,1,0:T(1,128)S(1)} async-done(((s32[16,1,128]{2,1,0:T(1,128)}), s32[16,1,128]{2,1,0:T(1,128)S(1)}, u32[]{:S(2)}, u32[]{:S(2)}) %all-to-all-start) | async-done | bytes 8224 | tf_op jit(solution)/shard_map/all_to_all | solution.py:176
  16.6 0.0 copy-done.2
  16.6 0.0 copy-start.3
  16.6 0.9 %copy-done.3 = bf16[144,288]{1,0:T(8,128)(2,1)S(1)} copy-done((bf16[144,288]{1,0:T(8,128)(2,1)S(1)}, bf16[144,288]{1,0:T(8,128)(2,1)}, u32[]{:S(2)}) %copy-start.3) | copy-done | bytes 82968
  17.5 1.6 %shard_map.87 = (bf16[96,1536]{1,0:T(8,128)(2,1)S(1)}, bf16[96,1536]{1,0:T(8,128)(2,1)S(1)}, bf16[96,1536]{1,0:T(8,128)(2,1)S(1)}, bf16[96,1536]{1,0:T(8,128)(2,1)S(1)}) custom-call(bf16[144,288]{1,0:T(8,128)(2,1)S(1)} %copy-done.3, bf16[144,2048]{1,0:T(8,128)(2,1)S(1)} %bitcast.22, s32[16,128]{1,0:T(8,128)S(1)} %bitcast.19), custom_call_target="tpu_custom_call" | custom-call | flops 226492416 | bytes 1860608 | tf_op jit(solution)/shard_map/pallas_call | solution.py:32
  19.1 4.2 %all-to-all-start.1 = ((bf16[8,16,2304]{2,1,0:T(8,128)(2,1)}), bf16[8,16,2304]{2,1,0:T(8,128)(2,1)S(1)}, u32[]{:S(2)}, u32[]{:S(2)}) async-start(bf16[8,16,2304]{2,1,0:T(8,128)(2,1)} %bitcast.25), calls=%async_computation.1 | async-start | bytes 1179648 | tf_op jit(solution)/shard_map/all_to_all | solution.py:201
  23.3 0.0 copy-start
  23.3 0.0 copy-start.1
  23.3 2.6 %collective-permute-start.1 = (bf16[96,1536]{1,0:T(8,128)(2,1)S(1)}, bf16[96,1536]{1,0:T(8,128)(2,1)S(1)}, u32[]{:S(2)}, u32[]{:S(2)}) collective-permute-start(bf16[96,1536]{1,0:T(8,128)(2,1)S(1)} %get-tuple-element.23), channel_id=1, source_target_pairs={{0,5},{1,4},{4,1},{5,0},{2,7},{3,6},{6,3},{7,2},{8,13},{9,12},{12,... | collective-permute-start | bytes 884744 | tf_op jit(solution)/shard_map/ppermute | solution.py:205
  25.9 6.2 %collective-permute-start.2 = (bf16[96,1536]{1,0:T(8,128)(2,1)S(1)}, bf16[96,1536]{1,0:T(8,128)(2,1)S(1)}, u32[]{:S(2)}, u32[]{:S(2)}) collective-permute-start(bf16[96,1536]{1,0:T(8,128)(2,1)S(1)} %get-tuple-element.24), channel_id=1, source_target_pairs={{0,4},{4,0},{1,5},{5,1},{2,6},{6,2},{3,7},{7,3},{8,12},{12,8},{9,1... | collective-permute-start | bytes 884744 | tf_op jit(solution)/shard_map/ppermute | solution.py:206
  32.1 3.4 %collective-permute-start.3 = (bf16[96,1536]{1,0:T(8,128)(2,1)S(1)}, bf16[96,1536]{1,0:T(8,128)(2,1)S(1)}, u32[]{:S(2)}, u32[]{:S(2)}) collective-permute-start(bf16[96,1536]{1,0:T(8,128)(2,1)S(1)} %get-tuple-element.25), channel_id=1, source_target_pairs={{0,1},{1,0},{2,3},{3,2},{4,5},{5,4},{6,7},{7,6},{8,9},{9,8},{10,11... | collective-permute-start | bytes 884744 | tf_op jit(solution)/shard_map/ppermute | solution.py:207
  35.5 0.0 collective-permute-done.1.one
  35.5 8.0 %collective-permute-done.2.two = bf16[96,1536]{1,0:T(8,128)(2,1)S(1)} collective-permute-done((bf16[96,1536]{1,0:T(8,128)(2,1)S(1)}, bf16[96,1536]{1,0:T(8,128)(2,1)S(1)}, u32[]{:S(2)}, u32[]{:S(2)}) %collective-permute-start.2) | collective-permute-done | bytes 294944 | tf_op jit(solution)/shard_map/ppermute | solution.py:206
  43.5 0.0 collective-permute-done.3.three
  43.5 0.9 %shard_map.89 = bf16[96,1536]{1,0:T(8,128)(2,1)} custom-call(bf16[96,1536]{1,0:T(8,128)(2,1)S(1)} %get-tuple-element.22.own, bf16[96,1536]{1,0:T(8,128)(2,1)S(1)} %collective-permute-done.1.one, bf16[96,1536]{1,0:T(8,128)(2,1)S(1)} %collective-permute-done.2.two, bf16[96,1536]{1,0:T(8,128)(2,1)S(1)} %collective-permute-done.3.three), custom_call_target="tpu_custom_call" | custom-call | bytes 1474560 | tf_op jit(solution)/shard_map/pallas_call | solution.py:32
  44.4 0.0 all-to-all-done.1
  44.4 14.2 %all-to-all-start.2 = ((bf16[12,8,1536]{2,1,0:T(8,128)(2,1)}), bf16[12,8,1536]{2,1,0:T(8,128)(2,1)S(1)}, u32[]{:S(2)}, u32[]{:S(2)}) async-start(bf16[12,8,1536]{2,1,0:T(8,128)(2,1)} %bitcast.12), calls=%async_computation.2 | async-start | bytes 589824 | tf_op jit(solution)/shard_map/all_to_all | solution.py:209
  58.6 1.9 %collective-permute-start = (bf16[64,2304]{1,0:T(8,128)(2,1)S(1)}, bf16[64,2304]{1,0:T(8,128)(2,1)S(1)}, u32[]{:S(2)}, u32[]{:S(2)}) collective-permute-start(bf16[64,2304]{1,0:T(8,128)(2,1)S(1)} %slice_bitcast_fusion), channel_id=1, source_target_pairs={{0,48},{48,0},{1,49},{49,1},{2,50},{50,2},{3,51},{51,3},{4,52},{52... | collective-permute-start | bytes 884744 | tf_op jit(solution)/shard_map/ppermute | solution.py:203
  60.5 1.5 %collective-permute-done.far = bf16[64,2304]{1,0:T(8,128)(2,1)S(1)} collective-permute-done((bf16[64,2304]{1,0:T(8,128)(2,1)S(1)}, bf16[64,2304]{1,0:T(8,128)(2,1)S(1)}, u32[]{:S(2)}, u32[]{:S(2)}) %collective-permute-start) | collective-permute-done | bytes 294944 | tf_op jit(solution)/shard_map/ppermute | solution.py:203
  62.1 0.0 copy-done
  62.1 0.0 copy-done.1
  62.1 1.7 %shard_map.88 = bf16[128,2048]{1,0:T(8,128)(2,1)} custom-call(s32[1,128]{1,0:T(1,128)S(1)} %bitcast.21, bf16[128,2048]{1,0:T(8,128)(2,1)S(1)} %copy-done, bf16[128,2304]{1,0:T(8,128)(2,1)S(1)} %bitcast.17, bf16[64,2304]{1,0:T(8,128)(2,1)S(1)} %collective-permute-done.far), custom_call_target="tpu_custom_call" | custom-call | flops 201326592 | bytes 1933824 | tf_op jit(solution)/shard_map/pallas_call | solution.py:32
  63.8 13.7 %all-to-all-done.2 = bf16[12,8,1536]{2,1,0:T(8,128)(2,1)S(1)} async-done(((bf16[12,8,1536]{2,1,0:T(8,128)(2,1)}), bf16[12,8,1536]{2,1,0:T(8,128)(2,1)S(1)}, u32[]{:S(2)}, u32[]{:S(2)}) %all-to-all-start.2) | async-done | bytes 294944 | tf_op jit(solution)/shard_map/all_to_all | solution.py:209
  77.5 0.7 shard_map.90
  (1 shorter events, 0.0 us)
Async XLA Ops:
  1.9 14.7 %all-to-all-start = ((s32[16,1,128]{2,1,0:T(1,128)}), s32[16,1,128]{2,1,0:T(1,128)S(1)}, u32[]{:S(2)}, u32[]{:S(2)}) async-start(s32[16,1,128]{2,1,0:T(1,128)} %broadcast_in_dim.8), calls=%async_computation | async-start | bytes 16384 | tf_op jit(solution)/shard_map/all_to_all | solution.py:176
  9.1 7.5 %copy-start.2 = (bf16[1,144,2048]{2,1,0:T(8,128)(2,1)S(1)}, bf16[1,144,2048]{2,1,0:T(8,128)(2,1)}, u32[]{:S(2)}) copy-start(bf16[1,144,2048]{2,1,0:T(8,128)(2,1)} %param.9) | copy-start | bytes 1769476
  16.6 0.9 %copy-start.3 = (bf16[144,288]{1,0:T(8,128)(2,1)S(1)}, bf16[144,288]{1,0:T(8,128)(2,1)}, u32[]{:S(2)}) copy-start(bf16[144,288]{1,0:T(8,128)(2,1)} %get-tuple-element.15.hidden) | copy-start | bytes 248836
  19.1 25.3 %all-to-all-start.1 = ((bf16[8,16,2304]{2,1,0:T(8,128)(2,1)}), bf16[8,16,2304]{2,1,0:T(8,128)(2,1)S(1)}, u32[]{:S(2)}, u32[]{:S(2)}) async-start(bf16[8,16,2304]{2,1,0:T(8,128)(2,1)} %bitcast.25), calls=%async_computation.1 | async-start | bytes 1179648 | tf_op jit(solution)/shard_map/all_to_all | solution.py:201
  23.3 38.8 %copy-start = (bf16[128,2048]{1,0:T(8,128)(2,1)S(1)}, bf16[128,2048]{1,0:T(8,128)(2,1)}, u32[]{:S(2)}) copy-start(bf16[128,2048]{1,0:T(8,128)(2,1)} %residual.1) | copy-start | bytes 1572868
  23.3 38.8 %copy-start.1 = (s32[128,1]{0,1:T(1,128)S(1)}, s32[128,1]{0,1:T(1,128)}, u32[]{:S(2)}) copy-start(s32[128,1]{0,1:T(1,128)} %param.7) | copy-start | bytes 1540
  23.3 12.2 %collective-permute-start.1 = (bf16[96,1536]{1,0:T(8,128)(2,1)S(1)}, bf16[96,1536]{1,0:T(8,128)(2,1)S(1)}, u32[]{:S(2)}, u32[]{:S(2)}) collective-permute-start(bf16[96,1536]{1,0:T(8,128)(2,1)S(1)} %get-tuple-element.23), channel_id=1, source_target_pairs={{0,5},{1,4},{4,1},{5,0},{2,7},{3,6},{6,3},{7,2},{8,13},{9,12},{12,... | collective-permute-start | bytes 884744 | tf_op jit(solution)/shard_map/ppermute | solution.py:205
  25.9 17.6 %collective-permute-start.2 = (bf16[96,1536]{1,0:T(8,128)(2,1)S(1)}, bf16[96,1536]{1,0:T(8,128)(2,1)S(1)}, u32[]{:S(2)}, u32[]{:S(2)}) collective-permute-start(bf16[96,1536]{1,0:T(8,128)(2,1)S(1)} %get-tuple-element.24), channel_id=1, source_target_pairs={{0,4},{4,0},{1,5},{5,1},{2,6},{6,2},{3,7},{7,3},{8,12},{12,8},{9,1... | collective-permute-start | bytes 884744 | tf_op jit(solution)/shard_map/ppermute | solution.py:206
  32.1 11.4 %collective-permute-start.3 = (bf16[96,1536]{1,0:T(8,128)(2,1)S(1)}, bf16[96,1536]{1,0:T(8,128)(2,1)S(1)}, u32[]{:S(2)}, u32[]{:S(2)}) collective-permute-start(bf16[96,1536]{1,0:T(8,128)(2,1)S(1)} %get-tuple-element.25), channel_id=1, source_target_pairs={{0,1},{1,0},{2,3},{3,2},{4,5},{5,4},{6,7},{7,6},{8,9},{9,8},{10,11... | collective-permute-start | bytes 884744 | tf_op jit(solution)/shard_map/ppermute | solution.py:207
  44.4 33.1 %all-to-all-start.2 = ((bf16[12,8,1536]{2,1,0:T(8,128)(2,1)}), bf16[12,8,1536]{2,1,0:T(8,128)(2,1)S(1)}, u32[]{:S(2)}, u32[]{:S(2)}) async-start(bf16[12,8,1536]{2,1,0:T(8,128)(2,1)} %bitcast.12), calls=%async_computation.2 | async-start | bytes 589824 | tf_op jit(solution)/shard_map/all_to_all | solution.py:209
  58.6 3.5 %collective-permute-start = (bf16[64,2304]{1,0:T(8,128)(2,1)S(1)}, bf16[64,2304]{1,0:T(8,128)(2,1)S(1)}, u32[]{:S(2)}, u32[]{:S(2)}) collective-permute-start(bf16[64,2304]{1,0:T(8,128)(2,1)S(1)} %slice_bitcast_fusion), channel_id=1, source_target_pairs={{0,48},{48,0},{1,49},{49,1},{2,50},{50,2},{3,51},{51,3},{4,52},{52... | collective-permute-start | bytes 884744 | tf_op jit(solution)/shard_map/ppermute | solution.py:203

commit v7 on v5

v7 whole, which is shorter than its diff:
```python
import functools
import jax
import jax.numpy as jnp
from jax import lax
from jax.experimental import pallas as pl
from jax.experimental.pallas import tpu as pltpu
from jax.sharding import Mesh, PartitionSpec as P

BF = jnp.bfloat16
F32 = jnp.float32
CAP = 9
X_DEV = 4
Z_DEV = 12
PARTS = 4
MIB = 1024 * 1024


def iota(shape, axis):
    return lax.broadcasted_iota(jnp.int32, shape, axis)


def as_bf(mask):
    return mask.astype(F32).astype(BF)


def dot(a, b, ca=1, cb=0):
    return lax.dot_general(a, b, (((ca,), (cb,)), ((), ())), preferred_element_type=F32)


def call(body, outs, *args, flops=0, limit=32, **more):
    size = sum(a.size * a.dtype.itemsize for a in args) + sum(o.size * o.dtype.itemsize for o in outs)
    return pl.pallas_call(
        body,
        out_shape=outs,
        compiler_params=pltpu.CompilerParams(vmem_limit_bytes=limit * MIB),
        cost_estimate=pl.CostEstimate(flops=flops, bytes_accessed=size, transcendentals=0),
        **more,
    )(*args)


def hidden_body(grad, w_out, preact, hidden, grad_v, w_out_v, preact_v, sems):
    width = grad.shape[1]
    part = width // PARTS
    loads = []
    for i in range(PARTS):
        span = pl.ds(i * part, part)
        loads.append(pltpu.make_async_copy(grad.at[:, span], grad_v.at[:, span], sems.at[2 * i]))
        loads.append(pltpu.make_async_copy(w_out.at[:, span], w_out_v.at[:, span], sems.at[2 * i + 1]))
    preact_copy = pltpu.make_async_copy(preact, preact_v, sems.at[2 * PARTS])
    for c in loads:
        c.start()
    preact_copy.start()
    product = jnp.zeros(hidden.shape, F32)
    for i in range(PARTS):
        loads[2 * i].wait()
        loads[2 * i + 1].wait()
        span = slice(i * part, i * part + part)
        product = product + dot(grad_v[:, span], w_out_v[:, span], 1, 1)
    preact_copy.wait()
    hidden[...] = jnp.where(preact_v[...].astype(F32) > 0, product, 0.0).astype(BF)


def slot_body(hidden, w_in, *outs):
    rows = hidden.shape[0]
    width = w_in.shape[1]
    k = iota((256, rows), 0)
    j = k & 127
    block = 2 * ((lax.axis_index("y") + (j >> 4)) & 7) + (((j >> 3) & 1) ^ lax.axis_index("core"))
    source = CAP * block + jnp.where(k < 128, j & 7, 8)
    picked = dot(as_bf(iota((256, rows), 1) == source), hidden[...]).astype(BF)
    row = iota((128, 256), 0) & 7
    last = jnp.zeros((128, 256), F32)
    for r in range(8):
        span = slice(256 * r, 256 * r + 256)
        got = dot(picked, w_in[:, span])
        main = got[:128].astype(BF)
        for i, out in enumerate(outs):
            out[:, span] = main[16 * i : 16 * i + 16]
        last = jnp.where(row == r, got[128:], last)
    last = last.astype(BF)
    for i, out in enumerate(outs):
        out[:, width:] = last[16 * i : 16 * i + 16]


def weight_body(hidden, inputs, routes, out):
    rows, units = hidden.shape
    expert = 2 * lax.axis_index("y") + lax.axis_index("core")
    counts = jnp.sum((routes[...] == expert).astype(F32), axis=1, keepdims=True).astype(jnp.int32)
    n = routes.shape[0]
    g = iota((n, rows), 1)
    first = CAP * iota((n, rows), 0)
    live = (g >= first) & (g < first + counts)
    mask = as_bf(jnp.sum(live.astype(F32), axis=0, keepdims=True) > 0.5)
    j = iota((96, units), 0)
    unit = iota((96, units), 1)
    for k in range(4):
        place = ((j & 7) < 6) & (unit == 6 * (12 * k + (j >> 3)) + (j & 7))
        spread = dot(as_bf(place), hidden[...], 1, 1).astype(BF) * mask
        last = dot(spread, inputs[:, 1536:])
        sub = iota(last.shape, 0) & 7
        for w in range(3):
            span = slice(512 * w, 512 * w + 512)
            tile = dot(spread, inputs[:, span])
            tile = jnp.where(sub == 6, pltpu.roll(last, 6 - w, 0), tile)
            tile = jnp.where(sub == 7, pltpu.roll(last, 4 - w, 0), tile)
            out[96 * k : 96 * k + 96, span] = tile.astype(BF)


def sum_body(scale, parts, out):
    total = parts[0:8, :].astype(F32)
    for z in range(1, parts.shape[0] // 8):
        total = total + parts[8 * z : 8 * z + 8, :].astype(F32)
    total = total / scale
    for u in range(6):
        v, w = u // 3, u % 3
        out[u, :, :1536] = total[u : u + 1, :]
        out[u, :, 1536:] = total[6 + v : 7 + v, 512 * w : 512 * w + 512]


def token_body(routes, residual, far, *rest):
    near = jnp.concatenate([p[...] for p in rest[:-1]], axis=0)
    out = rest[-1]
    ids = routes[...]
    n = ids.shape[1]
    onehot = (iota((16, n), 0) == ids).astype(F32)
    before = as_bf(iota((n, n), 0) < iota((n, n), 1))
    prefix = dot(onehot.astype(BF), before)
    slot = jnp.sum(onehot * prefix, axis=0, keepdims=True).astype(jnp.int32)
    back = (lax.axis_index("y") - (ids >> 1)) & 7
    here = (ids & 1) == lax.axis_index("core")
    k = iota((near.shape[0], n), 0)
    same_near = here & ((k >> 3) == 2 * back)
    c_near = k & 7
    k = iota((far.shape[0], n), 0)
    same_far = jnp.logical_not(here) & ((k >> 3) == back)
    c_far = k & 7
    pick_near = as_bf(same_near & (c_near == slot))
    pick_far = as_bf(same_far & (c_far == slot))
    last_near = near[:, 2048:]
    last_far = far[:, 2048:]
    for r in range(8):
        span = slice(256 * r, 256 * r + 256)
        tail_near = as_bf(same_near & (slot == 8) & (c_near == r))
        tail_far = as_bf(same_far & (slot == 8) & (c_far == r))
        got = dot(pick_near, near[:, span], 0, 0) + dot(pick_far, far[:, span], 0, 0)
        got = got + dot(tail_near, last_near, 0, 0) + dot(tail_far, last_far, 0, 0)
        out[:, span] = (residual[:, span].astype(F32) + got).astype(BF)


def shards(routes, residual_grad, saved_inputs, saved_preact, expert_grad, w_in, w_out):
    S = jax.ShapeDtypeStruct
    slots, width = saved_inputs.shape[1:]
    units = w_in.shape[1]
    groups = Z_DEV * X_DEV
    ids = routes.reshape(1, 128)
    hbm = pl.BlockSpec(memory_space=pl.ANY)
    experts = ("y", "core")
    everyone = lax.all_to_all(
        jnp.broadcast_to(ids[:, None], (16, 1, 128)), experts, split_axis=0, concat_axis=0, tiled=True
    ).reshape(16, 128)
    (hidden,) = call(
        hidden_body,
        [S((slots, units), BF)],
        expert_grad[0], w_out[0], saved_preact[0],
        flops=2 * slots * units * width,
        limit=63,
        in_specs=[hbm] * 3,
        scratch_shapes=[
            pltpu.VMEM((slots, width), BF),
            pltpu.VMEM((units, width), BF),
            pltpu.VMEM((slots, units), BF),
            pltpu.SemaphoreType.DMA((2 * PARTS + 1,)),
        ],
    )
    (part,) = call(
        weight_body, [S((8 * groups, 1536), BF)], hidden, saved_inputs[0], everyone,
        flops=2 * slots * 384 * width,
    )
    hidden, part = lax.optimization_barrier((hidden, part))
    part = lax.all_to_all(part, ("z", "x"), split_axis=0, concat_axis=0, tiled=True)
    pieces = call(
        slot_body, [S((16, width + 256), BF)] * 8, hidden, w_in[0],
        flops=4 * 128 * units * width,
    )
    near = [pieces[0]] + [None] * 7
    for i in (4, 3, 5, 2, 6, 1, 7):
        near[i] = lax.ppermute(pieces[i], "y", [(j, (j + i) % 8) for j in range(8)])
    far = lax.ppermute(jnp.concatenate([p[8:] for p in near], axis=0), "core", [(0, 1), (1, 0)])
    (token_grad,) = call(
        token_body, [S((128, width), BF)], ids, residual_grad, far, *near,
        flops=6 * 128 * 128 * width,
    )
    token_grad, part = lax.optimization_barrier((token_grad, part))
    (grad_in,) = call(
        functools.partial(sum_body, float(groups)), [S((6, 1, width), F32)], part
    )
    return token_grad, jnp.transpose(grad_in, (1, 0, 2))


def solution(mesh):
    fine = Mesh(mesh.devices.reshape(8, 2, Z_DEV, X_DEV), ("y", "core", "z", "x"))
    tokens = P(("y", "core", "z", "x"), None)
    buffers = P(("y", "core"), ("z", "x"), None)
    weights = P(("y", "core"), None, None)
    return jax.shard_map(
        shards,
        mesh=fine,
        in_specs=(tokens, tokens, buffers, buffers, buffers, weights, weights),
        out_specs=(tokens, buffers),
        check_vma=False,
    )
```

time: 76.4 us -> 85.3 us (1.12)
  the two profiles are of different devices: /device:TPU:12 before, /device:TPU:2 now
where the time goes in v7:
time: 85.3 us; the launch traced here: 84.8 us
  starting transfers between devices  53.4 us (63%)
  waiting for transfers between devices  19.6 us (23%)
  Pallas kernels  8.71 us (10%)
  local copies, waits for them, and re-layouts  2.28 us (3%)
  between operations  0.86 us (1%)
    ppermute x7, starting transfers between devices, shards(): near[i] = lax.ppermute(pieces[i], 'y', [(j, (j + i) % 8) for j in range(8)])  25.6 us
    all_to_all x1, starting transfers between devices, shards(): lax.all_to_all(part, ('z', 'x'), split_axis=0, concat_axis=0, tiled=True)  18.6 us
    all_to_all x1, waiting for transfers between devices, shards(): lax.all_to_all(part, ('z', 'x'), split_axis=0, concat_axis=0, tiled=True)  9.67 us
    pallas_call x5, Pallas kernels, call(): pl.pallas_call(body, out_shape=outs, compiler_params=pltpu.CompilerParams...  8.71 us
    all_to_all x1, starting transfers between devices, shards(): lax.all_to_all(jnp.broadcast_to(ids[:, None], (16, 1, 128)), experts, spl...  7.21 us
    all_to_all x1, waiting for transfers between devices, shards(): lax.all_to_all(jnp.broadcast_to(ids[:, None], (16, 1, 128)), experts, spl...  4.76 us
    ppermute x7, waiting for transfers between devices, shards(): near[i] = lax.ppermute(pieces[i], 'y', [(j, (j + i) % 8) for j in range(8)])  3.6 us
    ppermute x1, starting transfers between devices, shards(): lax.ppermute(jnp.concatenate([p[8:] for p in near], axis=0), 'core', [(0,...  1.91 us
  transfers between devices with their start and end apart: 10, of which 5 were waited for; matrix products, arithmetic and copies ran while one was open for 0% of the time, Pallas kernels for 6%

profile of v7, /device:TPU:2, one launch (start us, length us, event | category | flops | bytes accessed | tf_op | source)
XLA Modules:
  0.0 84.8 jit_solution(15455372717513704880)
XLA Ops:
  0.6 0.0 copy-start.3
  0.6 1.3 %broadcast_in_dim.8 = s32[16,1,128]{2,1,0:T(1,128)} broadcast(s32[128]{0:T(128)} %bitcast.15), dimensions={2} | broadcast | bytes 8704 | tf_op jit(solution)/shard_map/broadcast_in_dim | solution.py:159
  2.0 7.2 %all-to-all-start = ((s32[16,1,128]{2,1,0:T(1,128)}), s32[16,1,128]{2,1,0:T(1,128)S(1)}, u32[]{:S(2)}, u32[]{:S(2)}) async-start(s32[16,1,128]{2,1,0:T(1,128)} %broadcast_in_dim.8), calls=%async_computation | async-start | bytes 16384 | tf_op jit(solution)/shard_map/all_to_all | solution.py:158
  9.2 2.7 %shard_map.86.hidden = bf16[144,288]{1,0:T(8,128)(2,1)} custom-call(bf16[144,2048]{1,0:T(8,128)(2,1)} %bitcast.18, bf16[288,2048]{1,0:T(8,128)(2,1)} %bitcast.17, bf16[144,288]{1,0:T(8,128)(2,1)} %bitcast.19), custom_call_target="tpu_custom_call" | custom-call | flops 169869312 | bytes 1935360 | tf_op jit(solution)/shard_map/pallas_call | solution.py:32
  11.9 4.8 %all-to-all-done = s32[16,1,128]{2,1,0:T(1,128)S(1)} async-done(((s32[16,1,128]{2,1,0:T(1,128)}), s32[16,1,128]{2,1,0:T(1,128)S(1)}, u32[]{:S(2)}, u32[]{:S(2)}) %all-to-all-start) | async-done | bytes 8224 | tf_op jit(solution)/shard_map/all_to_all | solution.py:158
  16.7 0.0 copy-done.3
  16.7 0.0 copy-start.1
  16.7 0.9 %copy-done.1 = bf16[144,288]{1,0:T(8,128)(2,1)S(1)} copy-done((bf16[144,288]{1,0:T(8,128)(2,1)S(1)}, bf16[144,288]{1,0:T(8,128)(2,1)}, u32[]{:S(2)}) %copy-start.1) | copy-done | bytes 82968
  17.6 2.6 %shard_map.87 = bf16[384,1536]{1,0:T(8,128)(2,1)} custom-call(bf16[144,288]{1,0:T(8,128)(2,1)S(1)} %copy-done.1, bf16[144,2048]{1,0:T(8,128)(2,1)S(1)} %bitcast.13, s32[16,128]{1,0:T(8,128)S(1)} %bitcast.14), custom_call_target="tpu_custom_call" | custom-call | flops 226492416 | bytes 1860608 | tf_op jit(solution)/shard_map/pallas_call | solution.py:32
  20.2 0.0 copy-start
  20.2 0.0 copy-start.2
  20.2 18.6 %all-to-all-start.1 = ((bf16[48,8,1536]{2,1,0:T(8,128)(2,1)}), bf16[48,8,1536]{2,1,0:T(8,128)(2,1)S(1)}, u32[]{:S(2)}, u32[]{:S(2)}) async-start(bf16[48,8,1536]{2,1,0:T(8,128)(2,1)} %bitcast.8), calls=%async_computation.1 | async-start | bytes 2359296 | tf_op jit(solution)/shard_map/all_to_all | solution.py:180
  38.9 0.0 copy-start.4
  38.9 0.0 copy-start.5
  38.9 0.0 copy-done
  38.9 0.0 copy-done.2
  38.9 0.8 shard_map.88
  39.7 2.5 %collective-permute-start = (bf16[16,2304]{1,0:T(8,128)(2,1)S(1)}, bf16[16,2304]{1,0:T(8,128)(2,1)S(1)}, u32[]{:S(2)}, u32[]{:S(2)}) collective-permute-start(bf16[16,2304]{1,0:T(8,128)(2,1)S(1)} %get-tuple-element.16), channel_id=1, source_target_pairs={{0,96},{96,192},{192,288},{288,384},{384,480},{480,576},{576,672},... | collective-permute-start | bytes 221192 | tf_op jit(solution)/shard_map/ppermute | solution.py:187
  42.2 2.5 %collective-permute-start.1 = (bf16[16,2304]{1,0:T(8,128)(2,1)S(1)}, bf16[16,2304]{1,0:T(8,128)(2,1)S(1)}, u32[]{:S(2)}, u32[]{:S(2)}) collective-permute-start(bf16[16,2304]{1,0:T(8,128)(2,1)S(1)} %get-tuple-element.17), channel_id=1, source_target_pairs={{0,192},{96,288},{192,384},{288,480},{384,576},{480,672},{576,0},{... | collective-permute-start | bytes 221192 | tf_op jit(solution)/shard_map/ppermute | solution.py:187
  44.7 4.2 %collective-permute-start.2 = (bf16[16,2304]{1,0:T(8,128)(2,1)S(1)}, bf16[16,2304]{1,0:T(8,128)(2,1)S(1)}, u32[]{:S(2)}, u32[]{:S(2)}) collective-permute-start(bf16[16,2304]{1,0:T(8,128)(2,1)S(1)} %get-tuple-element.18), channel_id=1, source_target_pairs={{0,288},{96,384},{192,480},{288,576},{384,672},{480,0},{576,96},{6... | collective-permute-start | bytes 221192 | tf_op jit(solution)/shard_map/ppermute | solution.py:187
  49.0 5.5 %collective-permute-start.3 = (bf16[16,2304]{1,0:T(8,128)(2,1)S(1)}, bf16[16,2304]{1,0:T(8,128)(2,1)S(1)}, u32[]{:S(2)}, u32[]{:S(2)}) collective-permute-start(bf16[16,2304]{1,0:T(8,128)(2,1)S(1)} %get-tuple-element.19), channel_id=1, source_target_pairs={{0,384},{96,480},{192,576},{288,672},{384,0},{480,96},{576,192},{6... | collective-permute-start | bytes 221192 | tf_op jit(solution)/shard_map/ppermute | solution.py:187
  54.5 4.2 %collective-permute-start.4 = (bf16[16,2304]{1,0:T(8,128)(2,1)S(1)}, bf16[16,2304]{1,0:T(8,128)(2,1)S(1)}, u32[]{:S(2)}, u32[]{:S(2)}) collective-permute-start(bf16[16,2304]{1,0:T(8,128)(2,1)S(1)} %get-tuple-element.20), channel_id=1, source_target_pairs={{0,480},{96,576},{192,672},{288,0},{384,96},{480,192},{576,288},{6... | collective-permute-start | bytes 221192 | tf_op jit(solution)/shard_map/ppermute | solution.py:187
  58.7 0.0 collective-permute-done.rest_1_
  58.8 3.7 %collective-permute-start.5 = (bf16[16,2304]{1,0:T(8,128)(2,1)S(1)}, bf16[16,2304]{1,0:T(8,128)(2,1)S(1)}, u32[]{:S(2)}, u32[]{:S(2)}) collective-permute-start(bf16[16,2304]{1,0:T(8,128)(2,1)S(1)} %get-tuple-element.21), channel_id=1, source_target_pairs={{0,576},{96,672},{192,0},{288,96},{384,192},{480,288},{576,384},{6... | collective-permute-start | bytes 221192 | tf_op jit(solution)/shard_map/ppermute | solution.py:187
  62.5 0.0 collective-permute-done.1.rest_2_
  62.5 3.0 %collective-permute-start.6 = (bf16[16,2304]{1,0:T(8,128)(2,1)S(1)}, bf16[16,2304]{1,0:T(8,128)(2,1)S(1)}, u32[]{:S(2)}, u32[]{:S(2)}) collective-permute-start(bf16[16,2304]{1,0:T(8,128)(2,1)S(1)} %get-tuple-element.22), channel_id=1, source_target_pairs={{0,672},{96,0},{192,96},{288,192},{384,288},{480,384},{576,480},{6... | collective-permute-start | bytes 221192 | tf_op jit(solution)/shard_map/ppermute | solution.py:187
  65.5 0.0 collective-permute-done.2.rest_3_
  65.5 0.0 collective-permute-done.3.rest_4_
  65.5 0.0 collective-permute-done.4.rest_5_
  65.6 2.7 %collective-permute-done.5.rest_6_ = bf16[16,2304]{1,0:T(8,128)(2,1)S(1)} collective-permute-done((bf16[16,2304]{1,0:T(8,128)(2,1)S(1)}, bf16[16,2304]{1,0:T(8,128)(2,1)S(1)}, u32[]{:S(2)}, u32[]{:S(2)}) %collective-permute-start.5) | collective-permute-done | bytes 73760 | tf_op jit(solution)/shard_map/ppermute | solution.py:187
  68.2 0.9 %collective-permute-done.6.rest_7_ = bf16[16,2304]{1,0:T(8,128)(2,1)S(1)} collective-permute-done((bf16[16,2304]{1,0:T(8,128)(2,1)S(1)}, bf16[16,2304]{1,0:T(8,128)(2,1)S(1)}, u32[]{:S(2)}, u32[]{:S(2)}) %collective-permute-start.6) | collective-permute-done | bytes 73760 | tf_op jit(solution)/shard_map/ppermute | solution.py:187
  69.2 1.9 %collective-permute-start.7 = (bf16[64,2304]{1,0:T(8,128)(2,1)S(1)}, bf16[64,2304]{1,0:T(8,128)(2,1)S(1)}, u32[]{:S(2)}, u32[]{:S(2)}) collective-permute-start(bf16[64,2304]{1,0:T(8,128)(2,1)S(1)} %slice_dynamic-update-slice_fusion), channel_id=1, source_target_pairs={{0,48},{48,0},{1,49},{49,1},{2,50},{50,2},{3,51},{51,3},{4,52},{52... | collective-permute-start | bytes 884744 | tf_op jit(solution)/shard_map/ppermute | solution.py:188
  71.1 1.5 %collective-permute-done.7.far = bf16[64,2304]{1,0:T(8,128)(2,1)S(1)} collective-permute-done((bf16[64,2304]{1,0:T(8,128)(2,1)S(1)}, bf16[64,2304]{1,0:T(8,128)(2,1)S(1)}, u32[]{:S(2)}, u32[]{:S(2)}) %collective-permute-start.7) | collective-permute-done | bytes 294944 | tf_op jit(solution)/shard_map/ppermute | solution.py:188
  72.6 0.0 copy-done.4
  72.6 0.0 copy-done.5
  72.6 1.7 %shard_map.89 = bf16[128,2048]{1,0:T(8,128)(2,1)} custom-call(s32[1,128]{1,0:T(1,128)S(1)} %bitcast.16, bf16[128,2048]{1,0:T(8,128)(2,1)S(1)} %copy-done.4, bf16[64,2304]{1,0:T(8,128)(2,1)S(1)} %collective-permute-done.7.far, bf16[16,2304]{1,0:T(8,128)(2,1)S(1)} %get-tuple-element.15.rest_0_, bf16[16,2304]{1,0:T(8,128)(2,1)S(1)} %collective-permute-done.rest_1_, ...), custom_call_target="tpu_custom_call" | custom-call | flops 201326592 | bytes 1933824 | tf_op jit(solution)/shard_map/pallas_call | solution.py:32
  74.3 9.7 %all-to-all-done.1 = bf16[48,8,1536]{2,1,0:T(8,128)(2,1)S(1)} async-done(((bf16[48,8,1536]{2,1,0:T(8,128)(2,1)}), bf16[48,8,1536]{2,1,0:T(8,128)(2,1)S(1)}, u32[]{:S(2)}, u32[]{:S(2)}) %all-to-all-start.1) | async-done | bytes 1179680 | tf_op jit(solution)/shard_map/all_to_all | solution.py:180
  84.0 0.8 shard_map.90
  (8 shorter events, 0.0 us)
Async XLA Ops:
  0.6 16.0 %copy-start.3 = (bf16[1,144,2048]{2,1,0:T(8,128)(2,1)S(1)}, bf16[1,144,2048]{2,1,0:T(8,128)(2,1)}, u32[]{:S(2)}) copy-start(bf16[1,144,2048]{2,1,0:T(8,128)(2,1)} %param.9) | copy-start | bytes 1769476
  2.0 14.7 %all-to-all-start = ((s32[16,1,128]{2,1,0:T(1,128)}), s32[16,1,128]{2,1,0:T(1,128)S(1)}, u32[]{:S(2)}, u32[]{:S(2)}) async-start(s32[16,1,128]{2,1,0:T(1,128)} %broadcast_in_dim.8), calls=%async_computation | async-start | bytes 16384 | tf_op jit(solution)/shard_map/all_to_all | solution.py:158
  16.7 0.9 %copy-start.1 = (bf16[144,288]{1,0:T(8,128)(2,1)S(1)}, bf16[144,288]{1,0:T(8,128)(2,1)}, u32[]{:S(2)}) copy-start(bf16[144,288]{1,0:T(8,128)(2,1)} %shard_map.86.hidden) | copy-start | bytes 248836
  20.2 18.7 %copy-start = (bf16[1,288,2048]{2,1,0:T(8,128)(2,1)S(1)}, bf16[1,288,2048]{2,1,0:T(8,128)(2,1)}, u32[]{:S(2)}) copy-start(bf16[1,288,2048]{2,1,0:T(8,128)(2,1)} %param.12) | copy-start | bytes 3538948
  20.2 18.7 %copy-start.2 = (bf16[144,288]{1,0:T(8,128)(2,1)S(1)}, bf16[144,288]{1,0:T(8,128)(2,1)}, u32[]{:S(2)}) copy-start(bf16[144,288]{1,0:T(8,128)(2,1)} %shard_map.86.hidden) | copy-start | bytes 248836
  20.2 63.8 %all-to-all-start.1 = ((bf16[48,8,1536]{2,1,0:T(8,128)(2,1)}), bf16[48,8,1536]{2,1,0:T(8,128)(2,1)S(1)}, u32[]{:S(2)}, u32[]{:S(2)}) async-start(bf16[48,8,1536]{2,1,0:T(8,128)(2,1)} %bitcast.8), calls=%async_computation.1 | async-start | bytes 2359296 | tf_op jit(solution)/shard_map/all_to_all | solution.py:180
  38.9 33.8 %copy-start.4 = (bf16[128,2048]{1,0:T(8,128)(2,1)S(1)}, bf16[128,2048]{1,0:T(8,128)(2,1)}, u32[]{:S(2)}) copy-start(bf16[128,2048]{1,0:T(8,128)(2,1)} %residual.1) | copy-start | bytes 1572868
  38.9 33.8 %copy-start.5 = (s32[128,1]{0,1:T(1,128)S(1)}, s32[128,1]{0,1:T(1,128)}, u32[]{:S(2)}) copy-start(s32[128,1]{0,1:T(1,128)} %param.7) | copy-start | bytes 1540
  39.7 19.0 %collective-permute-start = (bf16[16,2304]{1,0:T(8,128)(2,1)S(1)}, bf16[16,2304]{1,0:T(8,128)(2,1)S(1)}, u32[]{:S(2)}, u32[]{:S(2)}) collective-permute-start(bf16[16,2304]{1,0:T(8,128)(2,1)S(1)} %get-tuple-element.16), channel_id=1, source_target_pairs={{0,96},{96,192},{192,288},{288,384},{384,480},{480,576},{576,672},... | collective-permute-start | bytes 221192 | tf_op jit(solution)/shard_map/ppermute | solution.py:187
  42.2 20.3 %collective-permute-start.1 = (bf16[16,2304]{1,0:T(8,128)(2,1)S(1)}, bf16[16,2304]{1,0:T(8,128)(2,1)S(1)}, u32[]{:S(2)}, u32[]{:S(2)}) collective-permute-start(bf16[16,2304]{1,0:T(8,128)(2,1)S(1)} %get-tuple-element.17), channel_id=1, source_target_pairs={{0,192},{96,288},{192,384},{288,480},{384,576},{480,672},{576,0},{... | collective-permute-start | bytes 221192 | tf_op jit(solution)/shard_map/ppermute | solution.py:187
  44.7 20.8 %collective-permute-start.2 = (bf16[16,2304]{1,0:T(8,128)(2,1)S(1)}, bf16[16,2304]{1,0:T(8,128)(2,1)S(1)}, u32[]{:S(2)}, u32[]{:S(2)}) collective-permute-start(bf16[16,2304]{1,0:T(8,128)(2,1)S(1)} %get-tuple-element.18), channel_id=1, source_target_pairs={{0,288},{96,384},{192,480},{288,576},{384,672},{480,0},{576,96},{6... | collective-permute-start | bytes 221192 | tf_op jit(solution)/shard_map/ppermute | solution.py:187
  49.0 16.5 %collective-permute-start.3 = (bf16[16,2304]{1,0:T(8,128)(2,1)S(1)}, bf16[16,2304]{1,0:T(8,128)(2,1)S(1)}, u32[]{:S(2)}, u32[]{:S(2)}) collective-permute-start(bf16[16,2304]{1,0:T(8,128)(2,1)S(1)} %get-tuple-element.19), channel_id=1, source_target_pairs={{0,384},{96,480},{192,576},{288,672},{384,0},{480,96},{576,192},{6... | collective-permute-start | bytes 221192 | tf_op jit(solution)/shard_map/ppermute | solution.py:187
  54.5 11.1 %collective-permute-start.4 = (bf16[16,2304]{1,0:T(8,128)(2,1)S(1)}, bf16[16,2304]{1,0:T(8,128)(2,1)S(1)}, u32[]{:S(2)}, u32[]{:S(2)}) collective-permute-start(bf16[16,2304]{1,0:T(8,128)(2,1)S(1)} %get-tuple-element.20), channel_id=1, source_target_pairs={{0,480},{96,576},{192,672},{288,0},{384,96},{480,192},{576,288},{6... | collective-permute-start | bytes 221192 | tf_op jit(solution)/shard_map/ppermute | solution.py:187
  58.8 9.5 %collective-permute-start.5 = (bf16[16,2304]{1,0:T(8,128)(2,1)S(1)}, bf16[16,2304]{1,0:T(8,128)(2,1)S(1)}, u32[]{:S(2)}, u32[]{:S(2)}) collective-permute-start(bf16[16,2304]{1,0:T(8,128)(2,1)S(1)} %get-tuple-element.21), channel_id=1, source_target_pairs={{0,576},{96,672},{192,0},{288,96},{384,192},{480,288},{576,384},{6... | collective-permute-start | bytes 221192 | tf_op jit(solution)/shard_map/ppermute | solution.py:187
  62.5 6.6 %collective-permute-start.6 = (bf16[16,2304]{1,0:T(8,128)(2,1)S(1)}, bf16[16,2304]{1,0:T(8,128)(2,1)S(1)}, u32[]{:S(2)}, u32[]{:S(2)}) collective-permute-start(bf16[16,2304]{1,0:T(8,128)(2,1)S(1)} %get-tuple-element.22), channel_id=1, source_target_pairs={{0,672},{96,0},{192,96},{288,192},{384,288},{480,384},{576,480},{6... | collective-permute-start | bytes 221192 | tf_op jit(solution)/shard_map/ppermute | solution.py:187
  69.2 3.5 %collective-permute-start.7 = (bf16[64,2304]{1,0:T(8,128)(2,1)S(1)}, bf16[64,2304]{1,0:T(8,128)(2,1)S(1)}, u32[]{:S(2)}, u32[]{:S(2)}) collective-permute-start(bf16[64,2304]{1,0:T(8,128)(2,1)S(1)} %slice_dynamic-update-slice_fusion), channel_id=1, source_target_pairs={{0,48},{48,0},{1,49},{49,1},{2,50},{50,2},{3,51},{51,3},{4,52},{52... | collective-permute-start | bytes 884744 | tf_op jit(solution)/shard_map/ppermute | solution.py:188

commit v8 on v5

--- a/solution.py
+++ b/solution.py
@@ -1,4 +1,5 @@
 import functools
+import math
 import jax
 import jax.numpy as jnp
 from jax import lax
@@ -28,7 +29,7 @@
 
 
 def call(body, outs, *args, flops=0, limit=32, **more):
-    size = sum(a.size * a.dtype.itemsize for a in args) + sum(o.size * o.dtype.itemsize for o in outs)
+    size = sum(math.prod(a.shape) * a.dtype.itemsize for a in (*args, *outs))
     return pl.pallas_call(
         body,
         out_shape=outs,
@@ -38,10 +39,7 @@
     )(*args)
 
 
-def front_body(
-    grad, w_out, preact, w_in, hidden, slots,
-    grad_v, w_out_v, preact_v, w_in_v, slots_v, sems,
-):
+def hidden_body(grad, w_out, preact, hidden, grad_v, w_out_v, preact_v, sems):
     width = grad.shape[1]
     part = width // PARTS
     loads = []
@@ -49,49 +47,36 @@
         span = pl.ds(i * part, part)
         loads.append(pltpu.make_async_copy(grad.at[:, span], grad_v.at[:, span], sems.at[2 * i]))
         loads.append(pltpu.make_async_copy(w_out.at[:, span], w_out_v.at[:, span], sems.at[2 * i + 1]))
-    n = 2 * PARTS
-    preact_copy = pltpu.make_async_copy(preact, preact_v, sems.at[n])
-    w_in_copy = pltpu.make_async_copy(w_in, w_in_v, sems.at[n + 1])
+    preact_copy = pltpu.make_async_copy(preact, preact_v, sems.at[2 * PARTS])
     for c in loads:
         c.start()
     preact_copy.start()
-    w_in_copy.start()
-    rows, units = preact_v.shape
-    product = jnp.zeros((rows, units), F32)
+    product = jnp.zeros(hidden.shape, F32)
     for i in range(PARTS):
         loads[2 * i].wait()
         loads[2 * i + 1].wait()
         span = slice(i * part, i * part + part)
         product = product + dot(grad_v[:, span], w_out_v[:, span], 1, 1)
     preact_copy.wait()
-    h = jnp.where(preact_v[...].astype(F32) > 0, product, 0.0).astype(BF)
-    hidden[...] = h
+    hidden[...] = jnp.where(preact_v[...].astype(F32) > 0, product, 0.0).astype(BF)
+
+
+def slot_body(hidden, w_in, slots):
+    rows = hidden.shape[0]
+    width = w_in.shape[1]
     k = iota((256, rows), 0)
     j = k & 127
     block = 2 * (j >> 4) + (((j >> 3) & 1) ^ lax.axis_index("core"))
     source = CAP * block + jnp.where(k < 128, j & 7, 8)
-    picked = dot(as_bf(iota((256, rows), 1) == source), h).astype(BF)
-    w_in_copy.wait()
+    picked = dot(as_bf(iota((256, rows), 1) == source), hidden[...]).astype(BF)
     row = iota((128, 256), 0) & 7
     last = jnp.zeros((128, 256), F32)
-    stores = []
     for r in range(8):
         span = slice(256 * r, 256 * r + 256)
-        got = dot(picked, w_in_v[:, span])
-        slots_v[:, span] = got[:128].astype(BF)
+        got = dot(picked, w_in[:, span])
+        slots[:, span] = got[:128].astype(BF)
         last = jnp.where(row == r, got[128:], last)
-        if r % 4 == 3:
-            half = pl.ds(256 * (r - 3), 1024)
-            stores.append(
-                pltpu.make_async_copy(slots_v.at[:, half], slots.at[:, half], sems.at[n + 2 + r // 4])
-            )
-            stores[-1].start()
-    slots_v[:, width:] = last.astype(BF)
-    tail = pl.ds(width, 256)
-    stores.append(pltpu.make_async_copy(slots_v.at[:, tail], slots.at[:, tail], sems.at[n + 4]))
-    stores[-1].start()
-    for c in stores:
-        c.wait()
+    slots[:, width:] = last.astype(BF)
 
 
 def weight_body(hidden, inputs, routes, *outs):
@@ -170,27 +155,25 @@
     groups = lax.axis_size("z") * lax.axis_size("x")
     ids = routes.reshape(1, 128)
     hbm = pl.BlockSpec(memory_space=pl.ANY)
-    vmem = pl.BlockSpec(memory_space=pltpu.VMEM)
     experts = ("y", "core")
     everyone = lax.all_to_all(
         jnp.broadcast_to(ids[:, None], (16, 1, 128)), experts, split_axis=0, concat_axis=0, tiled=True
     ).reshape(16, 128)
-    hidden, slot_grad = call(
-        front_body,
-        [S((slots, units), BF), S((128, width + 256), BF)],
-        expert_grad[0], w_out[0], saved_preact[0], w_in[0],
-        flops=6 * slots * units * width,
-        limit=63,
-        in_specs=[hbm] * 4,
-        out_specs=[vmem, hbm],
+    (hidden,) = call(
+        hidden_body,
+        [pltpu.VMEM((slots, units), BF)],
+        *[pltpu.with_memory_space_constraint(a[0], pltpu.HBM) for a in (expert_grad, w_out, saved_preact)],
+        flops=2 * slots * units * width,
+        in_specs=[hbm] * 3,
         scratch_shapes=[
             pltpu.VMEM((slots, width), BF),
             pltpu.VMEM((units, width), BF),
             pltpu.VMEM((slots, units), BF),
-            pltpu.VMEM((units, width), BF),
-            pltpu.VMEM((128, width + 256), BF),
-            pltpu.SemaphoreType.DMA((2 * PARTS + 5,)),
+            pltpu.SemaphoreType.DMA((2 * PARTS + 1,)),
         ],
+    )
+    (slot_grad,) = call(
+        slot_body, [S((128, width + 256), BF)], hidden, w_in[0], flops=4 * 128 * units * width
     )
     sends = call(
         weight_body, [S((8 * Z_DEV, 1536), BF)] * X_DEV, hidden, saved_inputs[0], everyone,

time: 76.4 us -> 74.9 us (0.980)
  local copies, waits for them, and re-layouts: 2.19 us -> 1.39 us
    unnamed x8, local copies, waits for them, and re-layouts: 0.91 us -> 0.02 us
    pallas_call x5 -> x6, Pallas kernels: 9.34 us -> 8.58 us  [call(): pl.pallas_call(body, out_shape=outs, compiler_params=pltpu.CompilerParams...]
  transfers between devices with their start and end apart: 7 -> 7, of which waited for: 5 -> 5; matrix products, arithmetic and copies ran while one was open for 0% -> 0% of each run, Pallas kernels for 9% -> 8%
where the time goes in v8:
time: 74.9 us; the launch traced here: 74.5 us
  starting transfers between devices  40.7 us (54%)
  waiting for transfers between devices  23.1 us (31%)
  Pallas kernels  8.58 us (11%)
  local copies, waits for them, and re-layouts  1.39 us (2%)
    ppermute x3, starting transfers between devices, shards(): lax.ppermute(sends[i], 'x', [(j, (j + i) % X_DEV) for j in range(X_DEV)])  13.6 us
    all_to_all x1, starting transfers between devices, shards(): part = lax.all_to_all(part, 'z', split_axis=0, concat_axis=0, tiled=True)  12.7 us
    all_to_all x1, waiting for transfers between devices, shards(): part = lax.all_to_all(part, 'z', split_axis=0, concat_axis=0, tiled=True)  12 us
    pallas_call x6, Pallas kernels, call(): pl.pallas_call(body, out_shape=outs, compiler_params=pltpu.CompilerParams...  8.58 us
    all_to_all x1, starting transfers between devices, shards(): lax.all_to_all(jnp.broadcast_to(ids[:, None], (16, 1, 128)), experts, spl...  7.56 us
    ppermute x3, waiting for transfers between devices, shards(): lax.ppermute(sends[i], 'x', [(j, (j + i) % X_DEV) for j in range(X_DEV)])  7.19 us
    all_to_all x1, starting transfers between devices, shards(): lax.all_to_all(slot_grad, 'y', split_axis=0, concat_axis=0, tiled=True)  4.93 us
    all_to_all x1, waiting for transfers between devices, shards(): lax.all_to_all(jnp.broadcast_to(ids[:, None], (16, 1, 128)), experts, spl...  2.36 us
  transfers between devices with their start and end apart: 7, of which 5 were waited for; matrix products, arithmetic and copies ran while one was open for 0% of the time, Pallas kernels for 8%

profile of v8, /device:TPU:12, one launch (start us, length us, event | category | flops | bytes accessed | tf_op | source)
XLA Modules:
  0.0 74.5 jit_solution(1976931425709793708)
XLA Ops:
  0.6 0.0 copy-start
  0.6 1.4 %broadcast_in_dim.8 = s32[16,1,128]{2,1,0:T(1,128)} broadcast(s32[128]{0:T(128)} %bitcast.21), dimensions={2} | broadcast | bytes 8704 | tf_op jit(solution)/shard_map/broadcast_in_dim | solution.py:160
  2.0 7.6 %all-to-all-start = ((s32[16,1,128]{2,1,0:T(1,128)}), s32[16,1,128]{2,1,0:T(1,128)S(1)}, u32[]{:S(2)}, u32[]{:S(2)}) async-start(s32[16,1,128]{2,1,0:T(1,128)} %broadcast_in_dim.8), calls=%async_computation | async-start | bytes 16384 | tf_op jit(solution)/shard_map/all_to_all | solution.py:159
  9.6 2.1 %shard_map.86.hidden = bf16[144,288]{1,0:T(8,128)(2,1)S(1)} custom-call(bf16[144,2048]{1,0:T(8,128)(2,1)} %bitcast.25, bf16[288,2048]{1,0:T(8,128)(2,1)} %bitcast.24, bf16[144,288]{1,0:T(8,128)(2,1)} %bitcast.26), custom_call_target="tpu_custom_call" | custom-call | flops 169869312 | bytes 1935360 | tf_op jit(solution)/shard_map/pallas_call | solution.py:33
  11.6 0.0 copy-start.3
  11.7 0.0 copy-done
  11.7 1.6 %shard_map.88 = bf16[128,2304]{1,0:T(8,128)(2,1)} custom-call(bf16[144,288]{1,0:T(8,128)(2,1)S(1)} %shard_map.86.hidden, bf16[288,2048]{1,0:T(8,128)(2,1)S(1)} %bitcast.18), custom_call_target="tpu_custom_call" | custom-call | flops 301989888 | bytes 1852416 | tf_op jit(solution)/shard_map/pallas_call | solution.py:33
  13.3 2.4 %all-to-all-done = s32[16,1,128]{2,1,0:T(1,128)S(1)} async-done(((s32[16,1,128]{2,1,0:T(1,128)}), s32[16,1,128]{2,1,0:T(1,128)S(1)}, u32[]{:S(2)}, u32[]{:S(2)}) %all-to-all-start) | async-done | bytes 8224 | tf_op jit(solution)/shard_map/all_to_all | solution.py:159
  15.7 0.0 copy-done.3
  15.7 1.6 %shard_map.87 = (bf16[96,1536]{1,0:T(8,128)(2,1)S(1)}, bf16[96,1536]{1,0:T(8,128)(2,1)S(1)}, bf16[96,1536]{1,0:T(8,128)(2,1)S(1)}, bf16[96,1536]{1,0:T(8,128)(2,1)S(1)}) custom-call(bf16[144,288]{1,0:T(8,128)(2,1)S(1)} %shard_map.86.hidden, bf16[144,2048]{1,0:T(8,128)(2,1)S(1)} %bitcast.23, s32[16,128]{1,0:T(8,128)S(1)} %bitcast.20), custom_call_target="tpu_custom_call" | custom-call | flops 226492416 | bytes 1860608 | tf_op jit(solution)/shard_map/pallas_call | solution.py:33
  17.3 4.9 %all-to-all-start.1 = ((bf16[8,16,2304]{2,1,0:T(8,128)(2,1)}), bf16[8,16,2304]{2,1,0:T(8,128)(2,1)S(1)}, u32[]{:S(2)}, u32[]{:S(2)}) async-start(bf16[8,16,2304]{2,1,0:T(8,128)(2,1)} %bitcast.8), calls=%async_computation.1 | async-start | bytes 1179648 | tf_op jit(solution)/shard_map/all_to_all | solution.py:183
  22.2 0.0 copy-start.1
  22.2 0.0 copy-start.2
  22.2 7.7 %collective-permute-start.1 = (bf16[96,1536]{1,0:T(8,128)(2,1)S(1)}, bf16[96,1536]{1,0:T(8,128)(2,1)S(1)}, u32[]{:S(2)}, u32[]{:S(2)}) collective-permute-start(bf16[96,1536]{1,0:T(8,128)(2,1)S(1)} %get-tuple-element.19), channel_id=1, source_target_pairs={{0,2},{1,3},{2,0},{3,1},{4,6},{5,7},{6,4},{7,5},{8,10},{9,11},{10,... | collective-permute-start | bytes 884744 | tf_op jit(solution)/shard_map/ppermute | solution.py:188
  30.0 1.9 %collective-permute-start.2 = (bf16[96,1536]{1,0:T(8,128)(2,1)S(1)}, bf16[96,1536]{1,0:T(8,128)(2,1)S(1)}, u32[]{:S(2)}, u32[]{:S(2)}) collective-permute-start(bf16[96,1536]{1,0:T(8,128)(2,1)S(1)} %get-tuple-element.20), channel_id=1, source_target_pairs={{0,1},{1,2},{2,3},{3,0},{4,5},{5,6},{6,7},{7,4},{8,9},{9,10},{10,1... | collective-permute-start | bytes 884744 | tf_op jit(solution)/shard_map/ppermute | solution.py:188
  31.9 3.9 %collective-permute-start.3 = (bf16[96,1536]{1,0:T(8,128)(2,1)S(1)}, bf16[96,1536]{1,0:T(8,128)(2,1)S(1)}, u32[]{:S(2)}, u32[]{:S(2)}) collective-permute-start(bf16[96,1536]{1,0:T(8,128)(2,1)S(1)} %get-tuple-element.21), channel_id=1, source_target_pairs={{0,3},{1,0},{2,1},{3,2},{4,7},{5,4},{6,5},{7,6},{8,11},{9,8},{10,9... | collective-permute-start | bytes 884744 | tf_op jit(solution)/shard_map/ppermute | solution.py:188
  35.8 2.0 %collective-permute-done.1.one = bf16[96,1536]{1,0:T(8,128)(2,1)S(1)} collective-permute-done((bf16[96,1536]{1,0:T(8,128)(2,1)S(1)}, bf16[96,1536]{1,0:T(8,128)(2,1)S(1)}, u32[]{:S(2)}, u32[]{:S(2)}) %collective-permute-start.1) | collective-permute-done | bytes 294944 | tf_op jit(solution)/shard_map/ppermute | solution.py:188
  37.9 5.2 %collective-permute-done.2.two = bf16[96,1536]{1,0:T(8,128)(2,1)S(1)} collective-permute-done((bf16[96,1536]{1,0:T(8,128)(2,1)S(1)}, bf16[96,1536]{1,0:T(8,128)(2,1)S(1)}, u32[]{:S(2)}, u32[]{:S(2)}) %collective-permute-start.2) | collective-permute-done | bytes 294944 | tf_op jit(solution)/shard_map/ppermute | solution.py:188
  43.0 0.0 collective-permute-done.3.three
  43.0 0.9 %shard_map.90 = bf16[96,1536]{1,0:T(8,128)(2,1)} custom-call(bf16[96,1536]{1,0:T(8,128)(2,1)S(1)} %get-tuple-element.18.own, bf16[96,1536]{1,0:T(8,128)(2,1)S(1)} %collective-permute-done.1.one, bf16[96,1536]{1,0:T(8,128)(2,1)S(1)} %collective-permute-done.2.two, bf16[96,1536]{1,0:T(8,128)(2,1)S(1)} %collective-permute-done.3.three), custom_call_target="tpu_custom_call" | custom-call | bytes 1474560 | tf_op jit(solution)/shard_map/pallas_call | solution.py:33
  43.9 0.0 all-to-all-done.1
  43.9 12.7 %all-to-all-start.2 = ((bf16[12,8,1536]{2,1,0:T(8,128)(2,1)}), bf16[12,8,1536]{2,1,0:T(8,128)(2,1)S(1)}, u32[]{:S(2)}, u32[]{:S(2)}) async-start(bf16[12,8,1536]{2,1,0:T(8,128)(2,1)} %bitcast.12), calls=%async_computation.2 | async-start | bytes 589824 | tf_op jit(solution)/shard_map/all_to_all | solution.py:190
  56.6 1.9 %collective-permute-start = (bf16[64,2304]{1,0:T(8,128)(2,1)S(1)}, bf16[64,2304]{1,0:T(8,128)(2,1)S(1)}, u32[]{:S(2)}, u32[]{:S(2)}) collective-permute-start(bf16[64,2304]{1,0:T(8,128)(2,1)S(1)} %slice_bitcast_fusion), channel_id=1, source_target_pairs={{0,48},{48,0},{1,49},{49,1},{2,50},{50,2},{3,51},{51,3},{4,52},{52... | collective-permute-start | bytes 884744 | tf_op jit(solution)/shard_map/ppermute | solution.py:185
  58.5 1.5 %collective-permute-done.far = bf16[64,2304]{1,0:T(8,128)(2,1)S(1)} collective-permute-done((bf16[64,2304]{1,0:T(8,128)(2,1)S(1)}, bf16[64,2304]{1,0:T(8,128)(2,1)S(1)}, u32[]{:S(2)}, u32[]{:S(2)}) %collective-permute-start) | collective-permute-done | bytes 294944 | tf_op jit(solution)/shard_map/ppermute | solution.py:185
  60.1 0.0 copy-done.1
  60.1 0.0 copy-done.2
  60.1 1.7 %shard_map.89 = bf16[128,2048]{1,0:T(8,128)(2,1)} custom-call(s32[1,128]{1,0:T(1,128)S(1)} %bitcast.22, bf16[128,2048]{1,0:T(8,128)(2,1)S(1)} %copy-done.1, bf16[128,2304]{1,0:T(8,128)(2,1)S(1)} %bitcast.17, bf16[64,2304]{1,0:T(8,128)(2,1)S(1)} %collective-permute-done.far), custom_call_target="tpu_custom_call" | custom-call | flops 201326592 | bytes 1933824 | tf_op jit(solution)/shard_map/pallas_call | solution.py:33
  61.8 12.0 %all-to-all-done.2 = bf16[12,8,1536]{2,1,0:T(8,128)(2,1)S(1)} async-done(((bf16[12,8,1536]{2,1,0:T(8,128)(2,1)}), bf16[12,8,1536]{2,1,0:T(8,128)(2,1)S(1)}, u32[]{:S(2)}, u32[]{:S(2)}) %all-to-all-start.2) | async-done | bytes 294944 | tf_op jit(solution)/shard_map/all_to_all | solution.py:190
  73.8 0.7 shard_map.91
  (1 shorter events, 0.0 us)
Async XLA Ops:
  0.6 11.0 %copy-start = (bf16[1,288,2048]{2,1,0:T(8,128)(2,1)S(1)}, bf16[1,288,2048]{2,1,0:T(8,128)(2,1)}, u32[]{:S(2)}) copy-start(bf16[1,288,2048]{2,1,0:T(8,128)(2,1)} %param.12) | copy-start | bytes 3538948
  2.0 13.7 %all-to-all-start = ((s32[16,1,128]{2,1,0:T(1,128)}), s32[16,1,128]{2,1,0:T(1,128)S(1)}, u32[]{:S(2)}, u32[]{:S(2)}) async-start(s32[16,1,128]{2,1,0:T(1,128)} %broadcast_in_dim.8), calls=%async_computation | async-start | bytes 16384 | tf_op jit(solution)/shard_map/all_to_all | solution.py:159
  11.6 4.0 %copy-start.3 = (bf16[1,144,2048]{2,1,0:T(8,128)(2,1)S(1)}, bf16[1,144,2048]{2,1,0:T(8,128)(2,1)}, u32[]{:S(2)}) copy-start(bf16[1,144,2048]{2,1,0:T(8,128)(2,1)} %param.9) | copy-start | bytes 1769476
  17.3 26.6 %all-to-all-start.1 = ((bf16[8,16,2304]{2,1,0:T(8,128)(2,1)}), bf16[8,16,2304]{2,1,0:T(8,128)(2,1)S(1)}, u32[]{:S(2)}, u32[]{:S(2)}) async-start(bf16[8,16,2304]{2,1,0:T(8,128)(2,1)} %bitcast.8), calls=%async_computation.1 | async-start | bytes 1179648 | tf_op jit(solution)/shard_map/all_to_all | solution.py:183
  22.2 37.9 %copy-start.1 = (bf16[128,2048]{1,0:T(8,128)(2,1)S(1)}, bf16[128,2048]{1,0:T(8,128)(2,1)}, u32[]{:S(2)}) copy-start(bf16[128,2048]{1,0:T(8,128)(2,1)} %residual.1) | copy-start | bytes 1572868
  22.2 37.9 %copy-start.2 = (s32[128,1]{0,1:T(1,128)S(1)}, s32[128,1]{0,1:T(1,128)}, u32[]{:S(2)}) copy-start(s32[128,1]{0,1:T(1,128)} %param.7) | copy-start | bytes 1540
  22.2 15.6 %collective-permute-start.1 = (bf16[96,1536]{1,0:T(8,128)(2,1)S(1)}, bf16[96,1536]{1,0:T(8,128)(2,1)S(1)}, u32[]{:S(2)}, u32[]{:S(2)}) collective-permute-start(bf16[96,1536]{1,0:T(8,128)(2,1)S(1)} %get-tuple-element.19), channel_id=1, source_target_pairs={{0,2},{1,3},{2,0},{3,1},{4,6},{5,7},{6,4},{7,5},{8,10},{9,11},{10,... | collective-permute-start | bytes 884744 | tf_op jit(solution)/shard_map/ppermute | solution.py:188
  30.0 13.0 %collective-permute-start.2 = (bf16[96,1536]{1,0:T(8,128)(2,1)S(1)}, bf16[96,1536]{1,0:T(8,128)(2,1)S(1)}, u32[]{:S(2)}, u32[]{:S(2)}) collective-permute-start(bf16[96,1536]{1,0:T(8,128)(2,1)S(1)} %get-tuple-element.20), channel_id=1, source_target_pairs={{0,1},{1,2},{2,3},{3,0},{4,5},{5,6},{6,7},{7,4},{8,9},{9,10},{10,1... | collective-permute-start | bytes 884744 | tf_op jit(solution)/shard_map/ppermute | solution.py:188
  31.9 11.1 %collective-permute-start.3 = (bf16[96,1536]{1,0:T(8,128)(2,1)S(1)}, bf16[96,1536]{1,0:T(8,128)(2,1)S(1)}, u32[]{:S(2)}, u32[]{:S(2)}) collective-permute-start(bf16[96,1536]{1,0:T(8,128)(2,1)S(1)} %get-tuple-element.21), channel_id=1, source_target_pairs={{0,3},{1,0},{2,1},{3,2},{4,7},{5,4},{6,5},{7,6},{8,11},{9,8},{10,9... | collective-permute-start | bytes 884744 | tf_op jit(solution)/shard_map/ppermute | solution.py:188
  43.9 29.9 %all-to-all-start.2 = ((bf16[12,8,1536]{2,1,0:T(8,128)(2,1)}), bf16[12,8,1536]{2,1,0:T(8,128)(2,1)S(1)}, u32[]{:S(2)}, u32[]{:S(2)}) async-start(bf16[12,8,1536]{2,1,0:T(8,128)(2,1)} %bitcast.12), calls=%async_computation.2 | async-start | bytes 589824 | tf_op jit(solution)/shard_map/all_to_all | solution.py:190
  56.6 3.5 %collective-permute-start = (bf16[64,2304]{1,0:T(8,128)(2,1)S(1)}, bf16[64,2304]{1,0:T(8,128)(2,1)S(1)}, u32[]{:S(2)}, u32[]{:S(2)}) collective-permute-start(bf16[64,2304]{1,0:T(8,128)(2,1)S(1)} %slice_bitcast_fusion), channel_id=1, source_target_pairs={{0,48},{48,0},{1,49},{49,1},{2,50},{50,2},{3,51},{51,3},{4,52},{52... | collective-permute-start | bytes 884744 | tf_op jit(solution)/shard_map/ppermute | solution.py:185

commit v9 on v8

--- a/solution.py
+++ b/solution.py
@@ -79,7 +79,7 @@
     slots[:, width:] = last.astype(BF)
 
 
-def weight_body(hidden, inputs, routes, *outs):
+def weight_body(steps, hidden, inputs, routes, *outs):
     rows, units = hidden.shape
     expert = 2 * lax.axis_index("y") + lax.axis_index("core")
     counts = jnp.sum((routes[...] == expert).astype(F32), axis=1, keepdims=True).astype(jnp.int32)
@@ -90,9 +90,8 @@
     first = CAP * iota((n, rows), 0)
     live = (g >= first) & (g < first + counts)
     mask = as_bf(jnp.sum(live.astype(F32), axis=0, keepdims=True) > 0.5)
-    me = lax.axis_index("x")
-    for k, out in enumerate(outs):
-        owner = X_DEV * (j >> 3) + ((me + k) & 3)
+    for step, out in zip(steps, outs):
+        owner = X_DEV * (j >> 3) + step()
         place = ((j & 7) < 6) & (unit == 6 * owner + (j & 7))
         spread = dot(as_bf(place), hidden[...], 1, 1).astype(BF) * mask
         last = dot(spread, inputs[:, 1536:])
@@ -105,8 +104,20 @@
             out[:, span] = tile.astype(BF)
 
 
-def add_body(own, one, two, three, out):
-    total = (own[...].astype(F32) + one[...].astype(F32)) + (two[...].astype(F32) + three[...].astype(F32))
+def pair_body(hidden, inputs, routes, out):
+    n = out.shape[0] // 2
+    halves = [out.at[pl.ds(h * n, n), :] for h in range(2)]
+    steps = [functools.partial(lambda h: 2 * h + lax.axis_index("xl"), h) for h in range(2)]
+    weight_body(steps, hidden, inputs, routes, *halves)
+
+
+def side_body(hidden, inputs, routes, *outs):
+    me = 2 * lax.axis_index("xh") + lax.axis_index("xl")
+    weight_body([lambda: (me + 1) & 3, lambda: (me + 3) & 3], hidden, inputs, routes, *outs)
+
+
+def add_body(pair, one, three, out):
+    total = pair[...].astype(F32) + (one[...].astype(F32) + three[...].astype(F32))
     out[...] = total.astype(BF)
 
 
@@ -152,7 +163,7 @@
     S = jax.ShapeDtypeStruct
     slots, width = saved_inputs.shape[1:]
     units = w_in.shape[1]
-    groups = lax.axis_size("z") * lax.axis_size("x")
+    groups = Z_DEV * X_DEV
     ids = routes.reshape(1, 128)
     hbm = pl.BlockSpec(memory_space=pl.ANY)
     experts = ("y", "core")
@@ -175,17 +186,22 @@
     (slot_grad,) = call(
         slot_body, [S((128, width + 256), BF)], hidden, w_in[0], flops=4 * 128 * units * width
     )
-    sends = call(
-        weight_body, [S((8 * Z_DEV, 1536), BF)] * X_DEV, hidden, saved_inputs[0], everyone,
-        flops=2 * slots * 384 * width,
-    )
-    *sends, slot_grad = lax.optimization_barrier((*sends, slot_grad))
+    def products(body, outs, hidden):
+        return call(body, outs, hidden, saved_inputs[0], everyone, flops=4 * slots * 96 * width)
+
+    def shift(send, i):
+        return lax.ppermute(send, ("xh", "xl"), [(j, (j + i) % X_DEV) for j in range(X_DEV)])
+
+    rows = 8 * Z_DEV
+    (pair,) = products(pair_body, [S((2 * rows, 1536), BF)], hidden)
+    hidden, pair = lax.optimization_barrier((hidden, pair))
+    pair = lax.psum_scatter(pair, "xh", scatter_dimension=0, tiled=True)
+    right, left = products(side_body, [S((rows, 1536), BF)] * 2, hidden)
+    right, left, slot_grad = lax.optimization_barrier((right, left, slot_grad))
     near = lax.all_to_all(slot_grad, "y", split_axis=0, concat_axis=0, tiled=True)
+    got = [pair, shift(right, 1), shift(left, 3)]
     far = near.reshape(8, 2, 8, width + 256)[:, 1].reshape(64, width + 256)
     far = lax.ppermute(far, "core", [(0, 1), (1, 0)])
-    got = [sends[0]]
-    for i in (2, 1, 3):
-        got.append(lax.ppermute(sends[i], "x", [(j, (j + i) % X_DEV) for j in range(X_DEV)]))
     (part,) = call(add_body, [S((8 * Z_DEV, 1536), BF)], *got)
     part = lax.all_to_all(part, "z", split_axis=0, concat_axis=0, tiled=True)
     (token_grad,) = call(
@@ -200,9 +216,9 @@
 
 
 def solution(mesh):
-    fine = Mesh(mesh.devices.reshape(8, 2, Z_DEV, X_DEV), ("y", "core", "z", "x"))
-    tokens = P(("y", "core", "z", "x"), None)
-    buffers = P(("y", "core"), ("z", "x"), None)
+    fine = Mesh(mesh.devices.reshape(8, 2, Z_DEV, 2, 2), ("y", "core", "z", "xh", "xl"))
+    tokens = P(("y", "core", "z", "xh", "xl"), None)
+    buffers = P(("y", "core"), ("z", "xh", "xl"), None)
     weights = P(("y", "core"), None, None)
     return jax.shard_map(
         shards,

time: 74.9 us -> 94.9 us (1.27)
  the two profiles are of different devices: /device:TPU:12 before, /device:TPU:10 now
where the time goes in v9:
time: 94.9 us; the launch traced here: 94.4 us
  starting transfers between devices  35.3 us (37%)
  waiting for transfers between devices  33.3 us (35%)
  between operations  14.1 us (15%)
  Pallas kernels  9.29 us (10%)
  local copies, waits for them, and re-layouts  2.32 us (2%)
    all_to_all x1, waiting for transfers between devices, shards(): part = lax.all_to_all(part, 'z', split_axis=0, concat_axis=0, tiled=True)  12 us
    ppermute x2, waiting for transfers between devices, shift(): lax.ppermute(send, ('xh', 'xl'), [(j, (j + i) % X_DEV) for j in range(X_D...  11.3 us
    all_to_all x1, starting transfers between devices, shards(): part = lax.all_to_all(part, 'z', split_axis=0, concat_axis=0, tiled=True)  11.2 us
    ppermute x2, starting transfers between devices, shift(): lax.ppermute(send, ('xh', 'xl'), [(j, (j + i) % X_DEV) for j in range(X_D...  9.69 us
    pallas_call x7, Pallas kernels, call(): pl.pallas_call(body, out_shape=outs, compiler_params=pltpu.CompilerParams...  9.29 us
    all_to_all x1, starting transfers between devices, shards(): lax.all_to_all(jnp.broadcast_to(ids[:, None], (16, 1, 128)), experts, spl...  7.56 us
    all_to_all x1, starting transfers between devices, shards(): lax.all_to_all(slot_grad, 'y', split_axis=0, concat_axis=0, tiled=True)  4.93 us
    reduce_scatter x1, waiting for transfers between devices, shards(): pair = lax.psum_scatter(pair, 'xh', scatter_dimension=0, tiled=True)  4.54 us
  transfers between devices with their start and end apart: 7, of which 6 were waited for; matrix products, arithmetic and copies ran while one was open for 0% of the time, Pallas kernels for 7%

profile of v9, /device:TPU:10, one launch (start us, length us, event | category | flops | bytes accessed | tf_op | source)
XLA Modules:
  0.0 94.4 jit_solution(2498476936645188906)
XLA Ops:
  7.2 0.0 copy-start
  7.2 1.3 %broadcast_in_dim.8 = s32[16,1,128]{2,1,0:T(1,128)} broadcast(s32[128]{0:T(128)} %bitcast.24), dimensions={2} | broadcast | bytes 8704 | tf_op jit(solution)/shard_map/broadcast_in_dim | solution.py:171
  8.5 7.6 %all-to-all-start = ((s32[16,1,128]{2,1,0:T(1,128)}), s32[16,1,128]{2,1,0:T(1,128)S(1)}, u32[]{:S(2)}, u32[]{:S(2)}) async-start(s32[16,1,128]{2,1,0:T(1,128)} %broadcast_in_dim.8), calls=%async_computation | async-start | bytes 16384 | tf_op jit(solution)/shard_map/all_to_all | solution.py:170
  16.1 0.0 reduce-scatter.2.cloned.1.call-start
  16.1 2.1 %shard_map.86.hidden = bf16[144,288]{1,0:T(8,128)(2,1)S(1)} custom-call(bf16[144,2048]{1,0:T(8,128)(2,1)} %bitcast.27, bf16[288,2048]{1,0:T(8,128)(2,1)} %bitcast.26, bf16[144,288]{1,0:T(8,128)(2,1)} %bitcast.28), custom_call_target="tpu_custom_call" | custom-call | flops 169869312 | bytes 1935360 | tf_op jit(solution)/shard_map/pallas_call | solution.py:33
  18.2 0.0 copy-start.1
  18.2 4.0 %all-to-all-done = s32[16,1,128]{2,1,0:T(1,128)S(1)} async-done(((s32[16,1,128]{2,1,0:T(1,128)}), s32[16,1,128]{2,1,0:T(1,128)S(1)}, u32[]{:S(2)}, u32[]{:S(2)}) %all-to-all-start) | async-done | bytes 8224 | tf_op jit(solution)/shard_map/all_to_all | solution.py:170
  22.2 0.0 copy-done
  22.2 1.6 %shard_map.87 = bf16[192,1536]{1,0:T(8,128)(2,1)} custom-call(bf16[144,288]{1,0:T(8,128)(2,1)S(1)} %shard_map.86.hidden, bf16[144,2048]{1,0:T(8,128)(2,1)S(1)} %bitcast.18, s32[16,128]{1,0:T(8,128)S(1)} %bitcast.22), custom_call_target="tpu_custom_call" | custom-call | flops 113246208 | bytes 1270784 | tf_op jit(solution)/shard_map/pallas_call | solution.py:33
  23.8 0.0 reduce-scatter.2.cloned.1.call-update
  23.8 0.0 copy-done.1
  23.8 1.6 %shard_map.89 = bf16[128,2304]{1,0:T(8,128)(2,1)} custom-call(bf16[144,288]{1,0:T(8,128)(2,1)S(1)} %shard_map.86.hidden, bf16[288,2048]{1,0:T(8,128)(2,1)S(1)} %bitcast.20), custom_call_target="tpu_custom_call" | custom-call | flops 301989888 | bytes 1852416 | tf_op jit(solution)/shard_map/pallas_call | solution.py:33
  25.5 0.8 shard_map.88
  26.2 0.0 copy-start.4
  26.2 4.9 %all-to-all-start.1 = ((bf16[8,16,2304]{2,1,0:T(8,128)(2,1)}), bf16[8,16,2304]{2,1,0:T(8,128)(2,1)S(1)}, u32[]{:S(2)}, u32[]{:S(2)}) async-start(bf16[8,16,2304]{2,1,0:T(8,128)(2,1)} %bitcast.8), calls=%async_computation.1 | async-start | bytes 1179648 | tf_op jit(solution)/shard_map/all_to_all | solution.py:201
  31.2 0.0 copy-start.2
  31.2 3.5 %collective-permute-start.1 = (bf16[96,1536]{1,0:T(8,128)(2,1)S(1)}, bf16[96,1536]{1,0:T(8,128)(2,1)S(1)}, u32[]{:S(2)}, u32[]{:S(2)}) collective-permute-start(bf16[96,1536]{1,0:T(8,128)(2,1)S(1)} %get-tuple-element.16), channel_id=1, source_target_pairs={{0,1},{1,2},{2,3},{3,0},{4,5},{5,6},{6,7},{7,4},{8,9},{9,10},{10,1... | collective-permute-start | bytes 884744 | tf_op jit(solution)/shard_map/ppermute | solution.py:193
  34.7 6.2 %collective-permute-start.2 = (bf16[96,1536]{1,0:T(8,128)(2,1)S(1)}, bf16[96,1536]{1,0:T(8,128)(2,1)S(1)}, u32[]{:S(2)}, u32[]{:S(2)}) collective-permute-start(bf16[96,1536]{1,0:T(8,128)(2,1)S(1)} %get-tuple-element.17), channel_id=1, source_target_pairs={{0,3},{1,0},{2,1},{3,2},{4,7},{5,4},{6,5},{7,6},{8,11},{9,8},{10,9... | collective-permute-start | bytes 884744 | tf_op jit(solution)/shard_map/ppermute | solution.py:193
  40.9 7.5 %collective-permute-done.1.one = bf16[96,1536]{1,0:T(8,128)(2,1)S(1)} collective-permute-done((bf16[96,1536]{1,0:T(8,128)(2,1)S(1)}, bf16[96,1536]{1,0:T(8,128)(2,1)S(1)}, u32[]{:S(2)}, u32[]{:S(2)}) %collective-permute-start.1) | collective-permute-done | bytes 294944 | tf_op jit(solution)/shard_map/ppermute | solution.py:193
  48.3 3.8 %collective-permute-done.2.three = bf16[96,1536]{1,0:T(8,128)(2,1)S(1)} collective-permute-done((bf16[96,1536]{1,0:T(8,128)(2,1)S(1)}, bf16[96,1536]{1,0:T(8,128)(2,1)S(1)}, u32[]{:S(2)}, u32[]{:S(2)}) %collective-permute-start.2) | collective-permute-done | bytes 294944 | tf_op jit(solution)/shard_map/ppermute | solution.py:193
  52.2 4.5 %reduce-scatter.2.cloned.1.call-done.pair = bf16[96,1536]{1,0:T(8,128)(2,1)} async-done(((bf16[192,1536]{1,0:T(8,128)(2,1)}), bf16[96,1536]{1,0:T(8,128)(2,1)}) %reduce-scatter.2.cloned.1.call-update) | async-done | bytes 294928 | tf_op jit(solution)/shard_map/reduce_scatter | solution.py:198
  56.7 0.0 copy-start.3
  56.7 1.0 %copy-done.3 = bf16[96,1536]{1,0:T(8,128)(2,1)S(1)} copy-done((bf16[96,1536]{1,0:T(8,128)(2,1)S(1)}, bf16[96,1536]{1,0:T(8,128)(2,1)}, u32[]{:S(2)}) %copy-start.3) | copy-done | bytes 294936
  57.6 0.8 shard_map.91
  58.5 0.0 all-to-all-done.1
  58.5 11.2 %all-to-all-start.2 = ((bf16[12,8,1536]{2,1,0:T(8,128)(2,1)}), bf16[12,8,1536]{2,1,0:T(8,128)(2,1)S(1)}, u32[]{:S(2)}, u32[]{:S(2)}) async-start(bf16[12,8,1536]{2,1,0:T(8,128)(2,1)} %bitcast.12), calls=%async_computation.3 | async-start | bytes 589824 | tf_op jit(solution)/shard_map/all_to_all | solution.py:206
  69.7 1.9 %collective-permute-start = (bf16[64,2304]{1,0:T(8,128)(2,1)S(1)}, bf16[64,2304]{1,0:T(8,128)(2,1)S(1)}, u32[]{:S(2)}, u32[]{:S(2)}) collective-permute-start(bf16[64,2304]{1,0:T(8,128)(2,1)S(1)} %slice_bitcast_fusion), channel_id=1, source_target_pairs={{0,48},{48,0},{1,49},{49,1},{2,50},{50,2},{3,51},{51,3},{4,52},{52... | collective-permute-start | bytes 884744 | tf_op jit(solution)/shard_map/ppermute | solution.py:204
  71.6 1.5 %collective-permute-done.far = bf16[64,2304]{1,0:T(8,128)(2,1)S(1)} collective-permute-done((bf16[64,2304]{1,0:T(8,128)(2,1)S(1)}, bf16[64,2304]{1,0:T(8,128)(2,1)S(1)}, u32[]{:S(2)}, u32[]{:S(2)}) %collective-permute-start) | collective-permute-done | bytes 294944 | tf_op jit(solution)/shard_map/ppermute | solution.py:204
  73.2 0.0 copy-done.4
  73.2 0.0 copy-done.2
  73.2 1.7 %shard_map.90 = bf16[128,2048]{1,0:T(8,128)(2,1)} custom-call(s32[1,128]{1,0:T(1,128)S(1)} %bitcast.25, bf16[128,2048]{1,0:T(8,128)(2,1)S(1)} %copy-done.2, bf16[128,2304]{1,0:T(8,128)(2,1)S(1)} %bitcast.17, bf16[64,2304]{1,0:T(8,128)(2,1)S(1)} %collective-permute-done.far), custom_call_target="tpu_custom_call" | custom-call | flops 201326592 | bytes 1933824 | tf_op jit(solution)/shard_map/pallas_call | solution.py:33
  74.9 12.0 %all-to-all-done.2 = bf16[12,8,1536]{2,1,0:T(8,128)(2,1)S(1)} async-done(((bf16[12,8,1536]{2,1,0:T(8,128)(2,1)}), bf16[12,8,1536]{2,1,0:T(8,128)(2,1)S(1)}, u32[]{:S(2)}, u32[]{:S(2)}) %all-to-all-start.2) | async-done | bytes 294944 | tf_op jit(solution)/shard_map/all_to_all | solution.py:206
  86.9 0.7 shard_map.92
  (1 shorter events, 0.0 us)
Async XLA Ops:
  7.2 15.0 %copy-start = (bf16[1,144,2048]{2,1,0:T(8,128)(2,1)S(1)}, bf16[1,144,2048]{2,1,0:T(8,128)(2,1)}, u32[]{:S(2)}) copy-start(bf16[1,144,2048]{2,1,0:T(8,128)(2,1)} %param.9) | copy-start | bytes 1769476
  8.5 13.7 %all-to-all-start = ((s32[16,1,128]{2,1,0:T(1,128)}), s32[16,1,128]{2,1,0:T(1,128)S(1)}, u32[]{:S(2)}, u32[]{:S(2)}) async-start(s32[16,1,128]{2,1,0:T(1,128)} %broadcast_in_dim.8), calls=%async_computation | async-start | bytes 16384 | tf_op jit(solution)/shard_map/all_to_all | solution.py:170
  16.1 40.6 %reduce-scatter.2.cloned.1.call-start = ((), (), s32[]{:S(2)}) async-start(), calls=%async_computation.4 | async-start | bytes 884736 | tf_op jit(solution)/shard_map/reduce_scatter | solution.py:198
  18.2 5.6 %copy-start.1 = (bf16[1,288,2048]{2,1,0:T(8,128)(2,1)S(1)}, bf16[1,288,2048]{2,1,0:T(8,128)(2,1)}, u32[]{:S(2)}) copy-start(bf16[1,288,2048]{2,1,0:T(8,128)(2,1)} %param.12) | copy-start | bytes 3538948
  26.2 47.0 %copy-start.4 = (s32[128,1]{0,1:T(1,128)S(1)}, s32[128,1]{0,1:T(1,128)}, u32[]{:S(2)}) copy-start(s32[128,1]{0,1:T(1,128)} %param.7) | copy-start | bytes 1540
  26.2 32.2 %all-to-all-start.1 = ((bf16[8,16,2304]{2,1,0:T(8,128)(2,1)}), bf16[8,16,2304]{2,1,0:T(8,128)(2,1)S(1)}, u32[]{:S(2)}, u32[]{:S(2)}) async-start(bf16[8,16,2304]{2,1,0:T(8,128)(2,1)} %bitcast.8), calls=%async_computation.1 | async-start | bytes 1179648 | tf_op jit(solution)/shard_map/all_to_all | solution.py:201
  31.2 42.0 %copy-start.2 = (bf16[128,2048]{1,0:T(8,128)(2,1)S(1)}, bf16[128,2048]{1,0:T(8,128)(2,1)}, u32[]{:S(2)}) copy-start(bf16[128,2048]{1,0:T(8,128)(2,1)} %residual.1) | copy-start | bytes 1572868
  31.2 17.2 %collective-permute-start.1 = (bf16[96,1536]{1,0:T(8,128)(2,1)S(1)}, bf16[96,1536]{1,0:T(8,128)(2,1)S(1)}, u32[]{:S(2)}, u32[]{:S(2)}) collective-permute-start(bf16[96,1536]{1,0:T(8,128)(2,1)S(1)} %get-tuple-element.16), channel_id=1, source_target_pairs={{0,1},{1,2},{2,3},{3,0},{4,5},{5,6},{6,7},{7,4},{8,9},{9,10},{10,1... | collective-permute-start | bytes 884744 | tf_op jit(solution)/shard_map/ppermute | solution.py:193
  34.7 17.5 %collective-permute-start.2 = (bf16[96,1536]{1,0:T(8,128)(2,1)S(1)}, bf16[96,1536]{1,0:T(8,128)(2,1)S(1)}, u32[]{:S(2)}, u32[]{:S(2)}) collective-permute-start(bf16[96,1536]{1,0:T(8,128)(2,1)S(1)} %get-tuple-element.17), channel_id=1, source_target_pairs={{0,3},{1,0},{2,1},{3,2},{4,7},{5,4},{6,5},{7,6},{8,11},{9,8},{10,9... | collective-permute-start | bytes 884744 | tf_op jit(solution)/shard_map/ppermute | solution.py:193
  56.7 1.0 %copy-start.3 = (bf16[96,1536]{1,0:T(8,128)(2,1)S(1)}, bf16[96,1536]{1,0:T(8,128)(2,1)}, u32[]{:S(2)}) copy-start(bf16[96,1536]{1,0:T(8,128)(2,1)} %reduce-scatter.2.cloned.1.call-done.pair) | copy-start | bytes 884740
  58.5 28.4 %all-to-all-start.2 = ((bf16[12,8,1536]{2,1,0:T(8,128)(2,1)}), bf16[12,8,1536]{2,1,0:T(8,128)(2,1)S(1)}, u32[]{:S(2)}, u32[]{:S(2)}) async-start(bf16[12,8,1536]{2,1,0:T(8,128)(2,1)} %bitcast.12), calls=%async_computation.3 | async-start | bytes 589824 | tf_op jit(solution)/shard_map/all_to_all | solution.py:206
  69.7 3.5 %collective-permute-start = (bf16[64,2304]{1,0:T(8,128)(2,1)S(1)}, bf16[64,2304]{1,0:T(8,128)(2,1)S(1)}, u32[]{:S(2)}, u32[]{:S(2)}) collective-permute-start(bf16[64,2304]{1,0:T(8,128)(2,1)S(1)} %slice_bitcast_fusion), channel_id=1, source_target_pairs={{0,48},{48,0},{1,49},{49,1},{2,50},{50,2},{3,51},{51,3},{4,52},{52... | collective-permute-start | bytes 884744 | tf_op jit(solution)/shard_map/ppermute | solution.py:204
Sparse Core Ops, SparseCore 0:
  23.9 32.7 reduce-scatter.1

commit v10 on v8

--- a/solution.py
+++ b/solution.py
@@ -12,7 +12,7 @@
 CAP = 9
 X_DEV = 4
 Z_DEV = 12
-PARTS = 4
+AHEAD = 10_000_000_000
 MIB = 1024 * 1024
 
 
@@ -39,26 +39,13 @@
     )(*args)
 
 
-def hidden_body(grad, w_out, preact, hidden, grad_v, w_out_v, preact_v, sems):
-    width = grad.shape[1]
-    part = width // PARTS
-    loads = []
-    for i in range(PARTS):
-        span = pl.ds(i * part, part)
-        loads.append(pltpu.make_async_copy(grad.at[:, span], grad_v.at[:, span], sems.at[2 * i]))
-        loads.append(pltpu.make_async_copy(w_out.at[:, span], w_out_v.at[:, span], sems.at[2 * i + 1]))
-    preact_copy = pltpu.make_async_copy(preact, preact_v, sems.at[2 * PARTS])
-    for c in loads:
-        c.start()
-    preact_copy.start()
-    product = jnp.zeros(hidden.shape, F32)
-    for i in range(PARTS):
-        loads[2 * i].wait()
-        loads[2 * i + 1].wait()
-        span = slice(i * part, i * part + part)
-        product = product + dot(grad_v[:, span], w_out_v[:, span], 1, 1)
-    preact_copy.wait()
-    hidden[...] = jnp.where(preact_v[...].astype(F32) > 0, product, 0.0).astype(BF)
+def spread_body(routes, out):
+    out[...] = jnp.broadcast_to(routes[...], out.shape)
+
+
+def hidden_body(grad, w_out, preact, hidden):
+    product = dot(grad[...], w_out[...], 1, 1)
+    hidden[...] = jnp.where(preact[...].astype(F32) > 0, product, 0.0).astype(BF)
 
 
 def slot_body(hidden, w_in, slots):
@@ -105,8 +92,12 @@
             out[:, span] = tile.astype(BF)
 
 
-def add_body(own, one, two, three, out):
-    total = (own[...].astype(F32) + one[...].astype(F32)) + (two[...].astype(F32) + three[...].astype(F32))
+def first_add_body(own, opposite, out):
+    out[...] = own[...].astype(F32) + opposite[...].astype(F32)
+
+
+def add_body(pair, one, three, out):
+    total = pair[...] + (one[...].astype(F32) + three[...].astype(F32))
     out[...] = total.astype(BF)
 
 
@@ -154,23 +145,16 @@
     units = w_in.shape[1]
     groups = lax.axis_size("z") * lax.axis_size("x")
     ids = routes.reshape(1, 128)
-    hbm = pl.BlockSpec(memory_space=pl.ANY)
     experts = ("y", "core")
+    (everyone,) = call(spread_body, [S((16, 128), jnp.int32)], ids, flops=AHEAD)
     everyone = lax.all_to_all(
-        jnp.broadcast_to(ids[:, None], (16, 1, 128)), experts, split_axis=0, concat_axis=0, tiled=True
+        everyone.reshape(16, 1, 128), experts, split_axis=0, concat_axis=0, tiled=True
     ).reshape(16, 128)
     (hidden,) = call(
         hidden_body,
         [pltpu.VMEM((slots, units), BF)],
-        *[pltpu.with_memory_space_constraint(a[0], pltpu.HBM) for a in (expert_grad, w_out, saved_preact)],
+        *[pltpu.with_memory_space_constraint(a[0], pltpu.VMEM) for a in (expert_grad, w_out, saved_preact)],
         flops=2 * slots * units * width,
-        in_specs=[hbm] * 3,
-        scratch_shapes=[
-            pltpu.VMEM((slots, width), BF),
-            pltpu.VMEM((units, width), BF),
-            pltpu.VMEM((slots, units), BF),
-            pltpu.SemaphoreType.DMA((2 * PARTS + 1,)),
-        ],
     )
     (slot_grad,) = call(
         slot_body, [S((128, width + 256), BF)], hidden, w_in[0], flops=4 * 128 * units * width
@@ -183,10 +167,12 @@
     near = lax.all_to_all(slot_grad, "y", split_axis=0, concat_axis=0, tiled=True)
     far = near.reshape(8, 2, 8, width + 256)[:, 1].reshape(64, width + 256)
     far = lax.ppermute(far, "core", [(0, 1), (1, 0)])
-    got = [sends[0]]
-    for i in (2, 1, 3):
-        got.append(lax.ppermute(sends[i], "x", [(j, (j + i) % X_DEV) for j in range(X_DEV)]))
-    (part,) = call(add_body, [S((8 * Z_DEV, 1536), BF)], *got)
+    def shift(i):
+        return lax.ppermute(sends[i], "x", [(j, (j + i) % X_DEV) for j in range(X_DEV)])
+
+    rows = 8 * Z_DEV
+    (pair,) = call(first_add_body, [S((rows, 1536), F32)], sends[0], shift(2), flops=AHEAD)
+    (part,) = call(add_body, [S((rows, 1536), BF)], pair, shift(1), shift(3))
     part = lax.all_to_all(part, "z", split_axis=0, concat_axis=0, tiled=True)
     (token_grad,) = call(
         token_body, [S((128, width), BF)], ids, residual_grad, near, far,

time: 74.9 us -> 78.7 us (1.051)
  the two profiles are of different devices: /device:TPU:12 before, /device:TPU:1 now
where the time goes in v10:
time: 78.7 us; the launch traced here: 78.2 us
  starting transfers between devices  41 us (52%)
  waiting for transfers between devices  28.1 us (36%)
  Pallas kernels  7.71 us (10%)
    all_to_all x1, starting transfers between devices, shards(): lax.all_to_all(everyone.reshape(16, 1, 128), experts, split_axis=0, conca...  13.9 us
    all_to_all x1, starting transfers between devices, shards(): part = lax.all_to_all(part, 'z', split_axis=0, concat_axis=0, tiled=True)  12.4 us
    all_to_all x1, waiting for transfers between devices, shards(): part = lax.all_to_all(part, 'z', split_axis=0, concat_axis=0, tiled=True)  10.4 us
    ppermute x3, starting transfers between devices, shift(): lax.ppermute(sends[i], 'x', [(j, (j + i) % X_DEV) for j in range(X_DEV)])  8.41 us
    pallas_call x8, Pallas kernels, call(): pl.pallas_call(body, out_shape=outs, compiler_params=pltpu.CompilerParams...  7.71 us
    ppermute x3, waiting for transfers between devices, shift(): lax.ppermute(sends[i], 'x', [(j, (j + i) % X_DEV) for j in range(X_DEV)])  6.25 us
    all_to_all x1, waiting for transfers between devices, shards(): lax.all_to_all(slot_grad, 'y', split_axis=0, concat_axis=0, tiled=True)  5.61 us
    all_to_all x1, waiting for transfers between devices, shards(): lax.all_to_all(everyone.reshape(16, 1, 128), experts, split_axis=0, conca...  4.66 us
  transfers between devices with their start and end apart: 7, of which 5 were waited for; matrix products, arithmetic and copies ran while one was open for 0% of the time, Pallas kernels for 6%

profile of v10, /device:TPU:1, one launch (start us, length us, event | category | flops | bytes accessed | tf_op | source)
XLA Modules:
  0.0 78.2 jit_solution(4775441024322064469)
XLA Ops:
  0.6 0.0 copy-start.5
  0.6 0.6 copy-done.5
  1.3 0.0 copy-start.1
  1.3 0.0 copy-start.2
  1.3 0.0 copy-start.4
  1.3 0.6 shard_map.87
  1.9 0.0 copy-start
  1.9 13.9 %all-to-all-start = ((s32[16,1,128]{2,1,0:T(1,128)}), s32[16,1,128]{2,1,0:T(1,128)S(1)}, u32[]{:S(2)}, u32[]{:S(2)}) async-start(s32[16,1,128]{2,1,0:T(1,128)} %bitcast.6), calls=%async_computation | async-start | bytes 16384 | tf_op jit(solution)/shard_map/all_to_all | solution.py:150
  15.8 0.0 copy-done.1
  15.8 0.0 copy-done.2
  15.8 0.0 copy-done.4
  15.8 0.6 shard_map.86.hidden
  16.4 0.0 copy-start.7
  16.5 0.0 copy-done
  16.5 1.7 %shard_map.89 = bf16[128,2304]{1,0:T(8,128)(2,1)} custom-call(bf16[144,288]{1,0:T(8,128)(2,1)S(1)} %shard_map.86.hidden, bf16[288,2048]{1,0:T(8,128)(2,1)S(1)} %bitcast.20), custom_call_target="tpu_custom_call" | custom-call | flops 301989888 | bytes 1852416 | tf_op jit(solution)/shard_map/pallas_call | solution.py:33
  18.1 4.7 %all-to-all-done = s32[16,1,128]{2,1,0:T(1,128)S(1)} async-done(((s32[16,1,128]{2,1,0:T(1,128)}), s32[16,1,128]{2,1,0:T(1,128)S(1)}, u32[]{:S(2)}, u32[]{:S(2)}) %all-to-all-start) | async-done | bytes 8224 | tf_op jit(solution)/shard_map/all_to_all | solution.py:150
  22.8 0.0 copy-done.7
  22.8 1.6 %shard_map.88 = (bf16[96,1536]{1,0:T(8,128)(2,1)S(1)}, bf16[96,1536]{1,0:T(8,128)(2,1)S(1)}, bf16[96,1536]{1,0:T(8,128)(2,1)S(1)}, bf16[96,1536]{1,0:T(8,128)(2,1)S(1)}) custom-call(bf16[144,288]{1,0:T(8,128)(2,1)S(1)} %shard_map.86.hidden, bf16[144,2048]{1,0:T(8,128)(2,1)S(1)} %bitcast.28, s32[16,128]{1,0:T(8,128)S(1)} %bitcast.25), custom_call_target="tpu_custom_call" | custom-call | flops 226492416 | bytes 1860608 | tf_op jit(solution)/shard_map/pallas_call | solution.py:33
  24.4 1.9 %collective-permute-start.1 = (bf16[96,1536]{1,0:T(8,128)(2,1)S(1)}, bf16[96,1536]{1,0:T(8,128)(2,1)S(1)}, u32[]{:S(2)}, u32[]{:S(2)}) collective-permute-start(bf16[96,1536]{1,0:T(8,128)(2,1)S(1)} %get-tuple-element.19), channel_id=1, source_target_pairs={{0,2},{1,3},{2,0},{3,1},{4,6},{5,7},{6,4},{7,5},{8,10},{9,11},{10,... | collective-permute-start | bytes 884744 | tf_op jit(solution)/shard_map/ppermute | solution.py:171
  26.3 3.5 %all-to-all-start.1 = ((bf16[8,16,2304]{2,1,0:T(8,128)(2,1)}), bf16[8,16,2304]{2,1,0:T(8,128)(2,1)S(1)}, u32[]{:S(2)}, u32[]{:S(2)}) async-start(bf16[8,16,2304]{2,1,0:T(8,128)(2,1)} %bitcast.9), calls=%async_computation.1 | async-start | bytes 1179648 | tf_op jit(solution)/shard_map/all_to_all | solution.py:167
  29.9 1.9 %collective-permute-start.2 = (bf16[96,1536]{1,0:T(8,128)(2,1)S(1)}, bf16[96,1536]{1,0:T(8,128)(2,1)S(1)}, u32[]{:S(2)}, u32[]{:S(2)}) collective-permute-start(bf16[96,1536]{1,0:T(8,128)(2,1)S(1)} %get-tuple-element.20), channel_id=1, source_target_pairs={{0,1},{1,2},{2,3},{3,0},{4,5},{5,6},{6,7},{7,4},{8,9},{9,10},{10,1... | collective-permute-start | bytes 884744 | tf_op jit(solution)/shard_map/ppermute | solution.py:171
  31.8 4.6 %collective-permute-start.3 = (bf16[96,1536]{1,0:T(8,128)(2,1)S(1)}, bf16[96,1536]{1,0:T(8,128)(2,1)S(1)}, u32[]{:S(2)}, u32[]{:S(2)}) collective-permute-start(bf16[96,1536]{1,0:T(8,128)(2,1)S(1)} %get-tuple-element.21), channel_id=1, source_target_pairs={{0,3},{1,0},{2,1},{3,2},{4,7},{5,4},{6,5},{7,6},{8,11},{9,8},{10,9... | collective-permute-start | bytes 884744 | tf_op jit(solution)/shard_map/ppermute | solution.py:171
  36.4 0.0 collective-permute-done.1.opposite
  36.4 0.1 shard_map.91.pair
  36.5 0.0 copy-start.3
  36.5 0.0 copy-start.6
  36.5 6.2 %collective-permute-done.2.one = bf16[96,1536]{1,0:T(8,128)(2,1)S(1)} collective-permute-done((bf16[96,1536]{1,0:T(8,128)(2,1)S(1)}, bf16[96,1536]{1,0:T(8,128)(2,1)S(1)}, u32[]{:S(2)}, u32[]{:S(2)}) %collective-permute-start.2) | collective-permute-done | bytes 294944 | tf_op jit(solution)/shard_map/ppermute | solution.py:171
  42.7 0.0 collective-permute-done.3.three
  42.8 0.8 %shard_map.92 = bf16[96,1536]{1,0:T(8,128)(2,1)} custom-call(f32[96,1536]{1,0:T(8,128)S(1)} %shard_map.91.pair, bf16[96,1536]{1,0:T(8,128)(2,1)S(1)} %collective-permute-done.2.one, bf16[96,1536]{1,0:T(8,128)(2,1)S(1)} %collective-permute-done.3.three), custom_call_target="tpu_custom_call" | custom-call | bytes 1474560 | tf_op jit(solution)/shard_map/pallas_call | solution.py:33
  43.6 5.6 %all-to-all-done.1 = bf16[8,16,2304]{2,1,0:T(8,128)(2,1)S(1)} async-done(((bf16[8,16,2304]{2,1,0:T(8,128)(2,1)}), bf16[8,16,2304]{2,1,0:T(8,128)(2,1)S(1)}, u32[]{:S(2)}, u32[]{:S(2)}) %all-to-all-start.1) | async-done | bytes 589856 | tf_op jit(solution)/shard_map/all_to_all | solution.py:167
  49.2 12.4 %all-to-all-start.2 = ((bf16[12,8,1536]{2,1,0:T(8,128)(2,1)}), bf16[12,8,1536]{2,1,0:T(8,128)(2,1)S(1)}, u32[]{:S(2)}, u32[]{:S(2)}) async-start(bf16[12,8,1536]{2,1,0:T(8,128)(2,1)} %bitcast.13), calls=%async_computation.2 | async-start | bytes 589824 | tf_op jit(solution)/shard_map/all_to_all | solution.py:176
  61.6 2.7 %collective-permute-start = (bf16[64,2304]{1,0:T(8,128)(2,1)S(1)}, bf16[64,2304]{1,0:T(8,128)(2,1)S(1)}, u32[]{:S(2)}, u32[]{:S(2)}) collective-permute-start(bf16[64,2304]{1,0:T(8,128)(2,1)S(1)} %slice_bitcast_fusion), channel_id=1, source_target_pairs={{0,48},{48,0},{1,49},{49,1},{2,50},{50,2},{3,51},{51,3},{4,52},{52... | collective-permute-start | bytes 884744 | tf_op jit(solution)/shard_map/ppermute | solution.py:169
  64.3 1.2 %collective-permute-done.far = bf16[64,2304]{1,0:T(8,128)(2,1)S(1)} collective-permute-done((bf16[64,2304]{1,0:T(8,128)(2,1)S(1)}, bf16[64,2304]{1,0:T(8,128)(2,1)S(1)}, u32[]{:S(2)}, u32[]{:S(2)}) %collective-permute-start) | collective-permute-done | bytes 294944 | tf_op jit(solution)/shard_map/ppermute | solution.py:169
  65.5 0.0 copy-done.3
  65.5 0.0 copy-done.6
  65.5 1.7 %shard_map.90 = bf16[128,2048]{1,0:T(8,128)(2,1)} custom-call(s32[1,128]{1,0:T(1,128)S(1)} %bitcast.27, bf16[128,2048]{1,0:T(8,128)(2,1)S(1)} %copy-done.3, bf16[128,2304]{1,0:T(8,128)(2,1)S(1)} %bitcast.19, bf16[64,2304]{1,0:T(8,128)(2,1)S(1)} %collective-permute-done.far), custom_call_target="tpu_custom_call" | custom-call | flops 201326592 | bytes 1933824 | tf_op jit(solution)/shard_map/pallas_call | solution.py:33
  67.2 10.4 %all-to-all-done.2 = bf16[12,8,1536]{2,1,0:T(8,128)(2,1)S(1)} async-done(((bf16[12,8,1536]{2,1,0:T(8,128)(2,1)}), bf16[12,8,1536]{2,1,0:T(8,128)(2,1)S(1)}, u32[]{:S(2)}, u32[]{:S(2)}) %all-to-all-start.2) | async-done | bytes 294944 | tf_op jit(solution)/shard_map/all_to_all | solution.py:176
  77.6 0.7 shard_map.93
  (1 shorter events, 0.0 us)
Async XLA Ops:
  0.6 0.7 copy-start.5
  1.3 14.5 %copy-start.1 = (bf16[1,288,2048]{2,1,0:T(8,128)(2,1)S(1)}, bf16[1,288,2048]{2,1,0:T(8,128)(2,1)}, u32[]{:S(2)}) copy-start(bf16[1,288,2048]{2,1,0:T(8,128)(2,1)} %param.13) | copy-start | bytes 3538948
  1.3 14.5 %copy-start.2 = (bf16[1,144,2048]{2,1,0:T(8,128)(2,1)S(1)}, bf16[1,144,2048]{2,1,0:T(8,128)(2,1)}, u32[]{:S(2)}) copy-start(bf16[1,144,2048]{2,1,0:T(8,128)(2,1)} %param.11) | copy-start | bytes 1769476
  1.3 14.5 %copy-start.4 = (bf16[1,144,288]{2,1,0:T(8,128)(2,1)S(1)}, bf16[1,144,288]{2,1,0:T(8,128)(2,1)}, u32[]{:S(2)}) copy-start(bf16[1,144,288]{2,1,0:T(8,128)(2,1)} %param.10) | copy-start | bytes 248836
  1.9 14.6 %copy-start = (bf16[1,288,2048]{2,1,0:T(8,128)(2,1)S(1)}, bf16[1,288,2048]{2,1,0:T(8,128)(2,1)}, u32[]{:S(2)}) copy-start(bf16[1,288,2048]{2,1,0:T(8,128)(2,1)} %param.12) | copy-start | bytes 3538948
  1.9 20.9 %all-to-all-start = ((s32[16,1,128]{2,1,0:T(1,128)}), s32[16,1,128]{2,1,0:T(1,128)S(1)}, u32[]{:S(2)}, u32[]{:S(2)}) async-start(s32[16,1,128]{2,1,0:T(1,128)} %bitcast.6), calls=%async_computation | async-start | bytes 16384 | tf_op jit(solution)/shard_map/all_to_all | solution.py:150
  16.4 6.3 %copy-start.7 = (bf16[1,144,2048]{2,1,0:T(8,128)(2,1)S(1)}, bf16[1,144,2048]{2,1,0:T(8,128)(2,1)}, u32[]{:S(2)}) copy-start(bf16[1,144,2048]{2,1,0:T(8,128)(2,1)} %param.9) | copy-start | bytes 1769476
  24.4 12.0 %collective-permute-start.1 = (bf16[96,1536]{1,0:T(8,128)(2,1)S(1)}, bf16[96,1536]{1,0:T(8,128)(2,1)S(1)}, u32[]{:S(2)}, u32[]{:S(2)}) collective-permute-start(bf16[96,1536]{1,0:T(8,128)(2,1)S(1)} %get-tuple-element.19), channel_id=1, source_target_pairs={{0,2},{1,3},{2,0},{3,1},{4,6},{5,7},{6,4},{7,5},{8,10},{9,11},{10,... | collective-permute-start | bytes 884744 | tf_op jit(solution)/shard_map/ppermute | solution.py:171
  26.3 22.8 %all-to-all-start.1 = ((bf16[8,16,2304]{2,1,0:T(8,128)(2,1)}), bf16[8,16,2304]{2,1,0:T(8,128)(2,1)S(1)}, u32[]{:S(2)}, u32[]{:S(2)}) async-start(bf16[8,16,2304]{2,1,0:T(8,128)(2,1)} %bitcast.9), calls=%async_computation.1 | async-start | bytes 1179648 | tf_op jit(solution)/shard_map/all_to_all | solution.py:167
  29.9 12.9 %collective-permute-start.2 = (bf16[96,1536]{1,0:T(8,128)(2,1)S(1)}, bf16[96,1536]{1,0:T(8,128)(2,1)S(1)}, u32[]{:S(2)}, u32[]{:S(2)}) collective-permute-start(bf16[96,1536]{1,0:T(8,128)(2,1)S(1)} %get-tuple-element.20), channel_id=1, source_target_pairs={{0,1},{1,2},{2,3},{3,0},{4,5},{5,6},{6,7},{7,4},{8,9},{9,10},{10,1... | collective-permute-start | bytes 884744 | tf_op jit(solution)/shard_map/ppermute | solution.py:171
  31.8 10.9 %collective-permute-start.3 = (bf16[96,1536]{1,0:T(8,128)(2,1)S(1)}, bf16[96,1536]{1,0:T(8,128)(2,1)S(1)}, u32[]{:S(2)}, u32[]{:S(2)}) collective-permute-start(bf16[96,1536]{1,0:T(8,128)(2,1)S(1)} %get-tuple-element.21), channel_id=1, source_target_pairs={{0,3},{1,0},{2,1},{3,2},{4,7},{5,4},{6,5},{7,6},{8,11},{9,8},{10,9... | collective-permute-start | bytes 884744 | tf_op jit(solution)/shard_map/ppermute | solution.py:171
  36.5 29.0 %copy-start.3 = (bf16[128,2048]{1,0:T(8,128)(2,1)S(1)}, bf16[128,2048]{1,0:T(8,128)(2,1)}, u32[]{:S(2)}) copy-start(bf16[128,2048]{1,0:T(8,128)(2,1)} %residual.1) | copy-start | bytes 1572868
  36.5 29.0 %copy-start.6 = (s32[128,1]{0,1:T(1,128)S(1)}, s32[128,1]{0,1:T(1,128)}, u32[]{:S(2)}) copy-start(s32[128,1]{0,1:T(1,128)} %param.7) | copy-start | bytes 1540
  49.2 28.4 %all-to-all-start.2 = ((bf16[12,8,1536]{2,1,0:T(8,128)(2,1)}), bf16[12,8,1536]{2,1,0:T(8,128)(2,1)S(1)}, u32[]{:S(2)}, u32[]{:S(2)}) async-start(bf16[12,8,1536]{2,1,0:T(8,128)(2,1)} %bitcast.13), calls=%async_computation.2 | async-start | bytes 589824 | tf_op jit(solution)/shard_map/all_to_all | solution.py:176
  61.6 3.9 %collective-permute-start = (bf16[64,2304]{1,0:T(8,128)(2,1)S(1)}, bf16[64,2304]{1,0:T(8,128)(2,1)S(1)}, u32[]{:S(2)}, u32[]{:S(2)}) collective-permute-start(bf16[64,2304]{1,0:T(8,128)(2,1)S(1)} %slice_bitcast_fusion), channel_id=1, source_target_pairs={{0,48},{48,0},{1,49},{49,1},{2,50},{50,2},{3,51},{51,3},{4,52},{52... | collective-permute-start | bytes 884744 | tf_op jit(solution)/shard_map/ppermute | solution.py:169

commit v11 on v10

--- a/solution.py
+++ b/solution.py
@@ -92,12 +92,8 @@
             out[:, span] = tile.astype(BF)
 
 
-def first_add_body(own, opposite, out):
-    out[...] = own[...].astype(F32) + opposite[...].astype(F32)
-
-
-def add_body(pair, one, three, out):
-    total = pair[...] + (one[...].astype(F32) + three[...].astype(F32))
+def add_body(own, one, two, three, out):
+    total = (own[...].astype(F32) + one[...].astype(F32)) + (two[...].astype(F32) + three[...].astype(F32))
     out[...] = total.astype(BF)
 
 
@@ -163,16 +159,13 @@
         weight_body, [S((8 * Z_DEV, 1536), BF)] * X_DEV, hidden, saved_inputs[0], everyone,
         flops=2 * slots * 384 * width,
     )
-    *sends, slot_grad = lax.optimization_barrier((*sends, slot_grad))
     near = lax.all_to_all(slot_grad, "y", split_axis=0, concat_axis=0, tiled=True)
     far = near.reshape(8, 2, 8, width + 256)[:, 1].reshape(64, width + 256)
     far = lax.ppermute(far, "core", [(0, 1), (1, 0)])
     def shift(i):
         return lax.ppermute(sends[i], "x", [(j, (j + i) % X_DEV) for j in range(X_DEV)])
 
-    rows = 8 * Z_DEV
-    (pair,) = call(first_add_body, [S((rows, 1536), F32)], sends[0], shift(2), flops=AHEAD)
-    (part,) = call(add_body, [S((rows, 1536), BF)], pair, shift(1), shift(3))
+    (part,) = call(add_body, [S((8 * Z_DEV, 1536), BF)], sends[0], shift(2), shift(1), shift(3))
     part = lax.all_to_all(part, "z", split_axis=0, concat_axis=0, tiled=True)
     (token_grad,) = call(
         token_body, [S((128, width), BF)], ids, residual_grad, near, far,

time: 78.7 us -> 74.8 us (0.950)
  the two profiles are of different devices: /device:TPU:1 before, /device:TPU:12 now
where the time goes in v11:
time: 74.8 us; the launch traced here: 74.4 us
  starting transfers between devices  40.7 us (54%)
  waiting for transfers between devices  24.5 us (33%)
  Pallas kernels  7.71 us (10%)
  between operations  0.75 us (1%)
    ppermute x3, starting transfers between devices, shift(): lax.ppermute(sends[i], 'x', [(j, (j + i) % X_DEV) for j in range(X_DEV)])  13.5 us
    all_to_all x1, starting transfers between devices, shards(): part = lax.all_to_all(part, 'z', split_axis=0, concat_axis=0, tiled=True)  12.7 us
    all_to_all x1, waiting for transfers between devices, shards(): part = lax.all_to_all(part, 'z', split_axis=0, concat_axis=0, tiled=True)  12 us
    pallas_call x7, Pallas kernels, call(): pl.pallas_call(body, out_shape=outs, compiler_params=pltpu.CompilerParams...  7.71 us
    all_to_all x1, starting transfers between devices, shards(): lax.all_to_all(everyone.reshape(16, 1, 128), experts, split_axis=0, conca...  7.69 us
    ppermute x3, waiting for transfers between devices, shift(): lax.ppermute(sends[i], 'x', [(j, (j + i) % X_DEV) for j in range(X_DEV)])  7.18 us
    all_to_all x1, starting transfers between devices, shards(): lax.all_to_all(slot_grad, 'y', split_axis=0, concat_axis=0, tiled=True)  4.92 us
    all_to_all x1, waiting for transfers between devices, shards(): lax.all_to_all(everyone.reshape(16, 1, 128), experts, split_axis=0, conca...  3.8 us
  transfers between devices with their start and end apart: 7, of which 5 were waited for; matrix products, arithmetic and copies ran while one was open for 0% of the time, Pallas kernels for 9%

profile of v11, /device:TPU:12, one launch (start us, length us, event | category | flops | bytes accessed | tf_op | source)
XLA Modules:
  0.0 74.4 jit_solution(16660829583801141657)
XLA Ops:
  0.6 0.0 copy-start.5
  0.6 0.6 copy-done.5
  1.3 0.0 copy-start.1
  1.3 0.0 copy-start.2
  1.3 0.0 copy-start.4
  1.3 0.6 shard_map.89
  1.9 0.0 copy-start
  1.9 7.7 %all-to-all-start.1 = ((s32[16,1,128]{2,1,0:T(1,128)}), s32[16,1,128]{2,1,0:T(1,128)S(1)}, u32[]{:S(2)}, u32[]{:S(2)}) async-start(s32[16,1,128]{2,1,0:T(1,128)} %bitcast.11), calls=%async_computation.1 | async-start | bytes 16384 | tf_op jit(solution)/shard_map/all_to_all | solution.py:146
  9.6 0.0 copy-done.1
  9.6 0.0 copy-done.2
  9.6 0.0 copy-done.4
  9.6 0.6 shard_map.86.hidden
  10.2 0.0 copy-done
  10.3 0.0 copy-start.7
  10.3 1.7 %shard_map.87 = bf16[128,2304]{1,0:T(8,128)(2,1)} custom-call(bf16[144,288]{1,0:T(8,128)(2,1)S(1)} %shard_map.86.hidden, bf16[288,2048]{1,0:T(8,128)(2,1)S(1)} %bitcast.20), custom_call_target="tpu_custom_call" | custom-call | flops 301989888 | bytes 1852416 | tf_op jit(solution)/shard_map/pallas_call | solution.py:33
  11.9 3.8 %all-to-all-done.1 = s32[16,1,128]{2,1,0:T(1,128)S(1)} async-done(((s32[16,1,128]{2,1,0:T(1,128)}), s32[16,1,128]{2,1,0:T(1,128)S(1)}, u32[]{:S(2)}, u32[]{:S(2)}) %all-to-all-start.1) | async-done | bytes 8224 | tf_op jit(solution)/shard_map/all_to_all | solution.py:146
  15.7 4.9 %all-to-all-start = ((bf16[8,16,2304]{2,1,0:T(8,128)(2,1)}), bf16[8,16,2304]{2,1,0:T(8,128)(2,1)S(1)}, u32[]{:S(2)}, u32[]{:S(2)}) async-start(bf16[8,16,2304]{2,1,0:T(8,128)(2,1)} %bitcast.5), calls=%async_computation | async-start | bytes 1179648 | tf_op jit(solution)/shard_map/all_to_all | solution.py:162
  20.6 0.0 copy-done.7
  20.6 1.6 %shard_map.90 = (bf16[96,1536]{1,0:T(8,128)(2,1)S(1)}, bf16[96,1536]{1,0:T(8,128)(2,1)S(1)}, bf16[96,1536]{1,0:T(8,128)(2,1)S(1)}, bf16[96,1536]{1,0:T(8,128)(2,1)S(1)}) custom-call(bf16[144,288]{1,0:T(8,128)(2,1)S(1)} %shard_map.86.hidden, bf16[144,2048]{1,0:T(8,128)(2,1)S(1)} %bitcast.28, s32[16,128]{1,0:T(8,128)S(1)} %bitcast.25), custom_call_target="tpu_custom_call" | custom-call | flops 226492416 | bytes 1860608 | tf_op jit(solution)/shard_map/pallas_call | solution.py:33
  22.2 7.6 %collective-permute-start.1 = (bf16[96,1536]{1,0:T(8,128)(2,1)S(1)}, bf16[96,1536]{1,0:T(8,128)(2,1)S(1)}, u32[]{:S(2)}, u32[]{:S(2)}) collective-permute-start(bf16[96,1536]{1,0:T(8,128)(2,1)S(1)} %get-tuple-element.9), channel_id=1, source_target_pairs={{0,2},{1,3},{2,0},{3,1},{4,6},{5,7},{6,4},{7,5},{8,10},{9,11},{10,... | collective-permute-start | bytes 884744 | tf_op jit(solution)/shard_map/ppermute | solution.py:166
  29.9 1.9 %collective-permute-start.2 = (bf16[96,1536]{1,0:T(8,128)(2,1)S(1)}, bf16[96,1536]{1,0:T(8,128)(2,1)S(1)}, u32[]{:S(2)}, u32[]{:S(2)}) collective-permute-start(bf16[96,1536]{1,0:T(8,128)(2,1)S(1)} %get-tuple-element.10), channel_id=1, source_target_pairs={{0,1},{1,2},{2,3},{3,0},{4,5},{5,6},{6,7},{7,4},{8,9},{9,10},{10,1... | collective-permute-start | bytes 884744 | tf_op jit(solution)/shard_map/ppermute | solution.py:166
  31.8 3.9 %collective-permute-start.3 = (bf16[96,1536]{1,0:T(8,128)(2,1)S(1)}, bf16[96,1536]{1,0:T(8,128)(2,1)S(1)}, u32[]{:S(2)}, u32[]{:S(2)}) collective-permute-start(bf16[96,1536]{1,0:T(8,128)(2,1)S(1)} %get-tuple-element.11), channel_id=1, source_target_pairs={{0,3},{1,0},{2,1},{3,2},{4,7},{5,4},{6,5},{7,6},{8,11},{9,8},{10,9... | collective-permute-start | bytes 884744 | tf_op jit(solution)/shard_map/ppermute | solution.py:166
  35.7 2.0 %collective-permute-done.1.one = bf16[96,1536]{1,0:T(8,128)(2,1)S(1)} collective-permute-done((bf16[96,1536]{1,0:T(8,128)(2,1)S(1)}, bf16[96,1536]{1,0:T(8,128)(2,1)S(1)}, u32[]{:S(2)}, u32[]{:S(2)}) %collective-permute-start.1) | collective-permute-done | bytes 294944 | tf_op jit(solution)/shard_map/ppermute | solution.py:166
  37.8 5.1 %collective-permute-done.2.two = bf16[96,1536]{1,0:T(8,128)(2,1)S(1)} collective-permute-done((bf16[96,1536]{1,0:T(8,128)(2,1)S(1)}, bf16[96,1536]{1,0:T(8,128)(2,1)S(1)}, u32[]{:S(2)}, u32[]{:S(2)}) %collective-permute-start.2) | collective-permute-done | bytes 294944 | tf_op jit(solution)/shard_map/ppermute | solution.py:166
  42.9 0.0 collective-permute-done.3.three
  42.9 0.0 copy-start.3
  42.9 0.0 copy-start.6
  42.9 0.9 %shard_map.91 = bf16[96,1536]{1,0:T(8,128)(2,1)} custom-call(bf16[96,1536]{1,0:T(8,128)(2,1)S(1)} %get-tuple-element.8.own, bf16[96,1536]{1,0:T(8,128)(2,1)S(1)} %collective-permute-done.1.one, bf16[96,1536]{1,0:T(8,128)(2,1)S(1)} %collective-permute-done.2.two, bf16[96,1536]{1,0:T(8,128)(2,1)S(1)} %collective-permute-done.3.three), custom_call_target="tpu_custom_call" | custom-call | bytes 1474560 | tf_op jit(solution)/shard_map/pallas_call | solution.py:33
  43.8 0.0 all-to-all-done
  43.8 12.7 %all-to-all-start.2 = ((bf16[12,8,1536]{2,1,0:T(8,128)(2,1)}), bf16[12,8,1536]{2,1,0:T(8,128)(2,1)S(1)}, u32[]{:S(2)}, u32[]{:S(2)}) async-start(bf16[12,8,1536]{2,1,0:T(8,128)(2,1)} %bitcast.13), calls=%async_computation.2 | async-start | bytes 589824 | tf_op jit(solution)/shard_map/all_to_all | solution.py:169
  56.5 1.9 %collective-permute-start = (bf16[64,2304]{1,0:T(8,128)(2,1)S(1)}, bf16[64,2304]{1,0:T(8,128)(2,1)S(1)}, u32[]{:S(2)}, u32[]{:S(2)}) collective-permute-start(bf16[64,2304]{1,0:T(8,128)(2,1)S(1)} %slice_bitcast_fusion), channel_id=1, source_target_pairs={{0,48},{48,0},{1,49},{49,1},{2,50},{50,2},{3,51},{51,3},{4,52},{52... | collective-permute-start | bytes 884744 | tf_op jit(solution)/shard_map/ppermute | solution.py:164
  58.4 1.5 %collective-permute-done.far = bf16[64,2304]{1,0:T(8,128)(2,1)S(1)} collective-permute-done((bf16[64,2304]{1,0:T(8,128)(2,1)S(1)}, bf16[64,2304]{1,0:T(8,128)(2,1)S(1)}, u32[]{:S(2)}, u32[]{:S(2)}) %collective-permute-start) | collective-permute-done | bytes 294944 | tf_op jit(solution)/shard_map/ppermute | solution.py:164
  60.0 0.0 copy-done.3
  60.0 0.0 copy-done.6
  60.0 1.7 %shard_map.88 = bf16[128,2048]{1,0:T(8,128)(2,1)} custom-call(s32[1,128]{1,0:T(1,128)S(1)} %bitcast.27, bf16[128,2048]{1,0:T(8,128)(2,1)S(1)} %copy-done.3, bf16[128,2304]{1,0:T(8,128)(2,1)S(1)} %bitcast.19, bf16[64,2304]{1,0:T(8,128)(2,1)S(1)} %collective-permute-done.far), custom_call_target="tpu_custom_call" | custom-call | flops 201326592 | bytes 1933824 | tf_op jit(solution)/shard_map/pallas_call | solution.py:33
  61.7 12.0 %all-to-all-done.2 = bf16[12,8,1536]{2,1,0:T(8,128)(2,1)S(1)} async-done(((bf16[12,8,1536]{2,1,0:T(8,128)(2,1)}), bf16[12,8,1536]{2,1,0:T(8,128)(2,1)S(1)}, u32[]{:S(2)}, u32[]{:S(2)}) %all-to-all-start.2) | async-done | bytes 294944 | tf_op jit(solution)/shard_map/all_to_all | solution.py:169
  73.7 0.7 shard_map.92
  (1 shorter events, 0.0 us)
Async XLA Ops:
  0.6 0.7 copy-start.5
  1.3 8.3 %copy-start.1 = (bf16[1,288,2048]{2,1,0:T(8,128)(2,1)S(1)}, bf16[1,288,2048]{2,1,0:T(8,128)(2,1)}, u32[]{:S(2)}) copy-start(bf16[1,288,2048]{2,1,0:T(8,128)(2,1)} %param.13) | copy-start | bytes 3538948
  1.3 8.3 %copy-start.2 = (bf16[1,144,2048]{2,1,0:T(8,128)(2,1)S(1)}, bf16[1,144,2048]{2,1,0:T(8,128)(2,1)}, u32[]{:S(2)}) copy-start(bf16[1,144,2048]{2,1,0:T(8,128)(2,1)} %param.11) | copy-start | bytes 1769476
  1.3 8.3 %copy-start.4 = (bf16[1,144,288]{2,1,0:T(8,128)(2,1)S(1)}, bf16[1,144,288]{2,1,0:T(8,128)(2,1)}, u32[]{:S(2)}) copy-start(bf16[1,144,288]{2,1,0:T(8,128)(2,1)} %param.10) | copy-start | bytes 248836
  1.9 8.3 %copy-start = (bf16[1,288,2048]{2,1,0:T(8,128)(2,1)S(1)}, bf16[1,288,2048]{2,1,0:T(8,128)(2,1)}, u32[]{:S(2)}) copy-start(bf16[1,288,2048]{2,1,0:T(8,128)(2,1)} %param.12) | copy-start | bytes 3538948
  1.9 13.8 %all-to-all-start.1 = ((s32[16,1,128]{2,1,0:T(1,128)}), s32[16,1,128]{2,1,0:T(1,128)S(1)}, u32[]{:S(2)}, u32[]{:S(2)}) async-start(s32[16,1,128]{2,1,0:T(1,128)} %bitcast.11), calls=%async_computation.1 | async-start | bytes 16384 | tf_op jit(solution)/shard_map/all_to_all | solution.py:146
  10.3 10.4 %copy-start.7 = (bf16[1,144,2048]{2,1,0:T(8,128)(2,1)S(1)}, bf16[1,144,2048]{2,1,0:T(8,128)(2,1)}, u32[]{:S(2)}) copy-start(bf16[1,144,2048]{2,1,0:T(8,128)(2,1)} %param.9) | copy-start | bytes 1769476
  15.7 28.1 %all-to-all-start = ((bf16[8,16,2304]{2,1,0:T(8,128)(2,1)}), bf16[8,16,2304]{2,1,0:T(8,128)(2,1)S(1)}, u32[]{:S(2)}, u32[]{:S(2)}) async-start(bf16[8,16,2304]{2,1,0:T(8,128)(2,1)} %bitcast.5), calls=%async_computation | async-start | bytes 1179648 | tf_op jit(solution)/shard_map/all_to_all | solution.py:162
  22.2 15.5 %collective-permute-start.1 = (bf16[96,1536]{1,0:T(8,128)(2,1)S(1)}, bf16[96,1536]{1,0:T(8,128)(2,1)S(1)}, u32[]{:S(2)}, u32[]{:S(2)}) collective-permute-start(bf16[96,1536]{1,0:T(8,128)(2,1)S(1)} %get-tuple-element.9), channel_id=1, source_target_pairs={{0,2},{1,3},{2,0},{3,1},{4,6},{5,7},{6,4},{7,5},{8,10},{9,11},{10,... | collective-permute-start | bytes 884744 | tf_op jit(solution)/shard_map/ppermute | solution.py:166
  29.9 13.0 %collective-permute-start.2 = (bf16[96,1536]{1,0:T(8,128)(2,1)S(1)}, bf16[96,1536]{1,0:T(8,128)(2,1)S(1)}, u32[]{:S(2)}, u32[]{:S(2)}) collective-permute-start(bf16[96,1536]{1,0:T(8,128)(2,1)S(1)} %get-tuple-element.10), channel_id=1, source_target_pairs={{0,1},{1,2},{2,3},{3,0},{4,5},{5,6},{6,7},{7,4},{8,9},{9,10},{10,1... | collective-permute-start | bytes 884744 | tf_op jit(solution)/shard_map/ppermute | solution.py:166
  31.8 11.1 %collective-permute-start.3 = (bf16[96,1536]{1,0:T(8,128)(2,1)S(1)}, bf16[96,1536]{1,0:T(8,128)(2,1)S(1)}, u32[]{:S(2)}, u32[]{:S(2)}) collective-permute-start(bf16[96,1536]{1,0:T(8,128)(2,1)S(1)} %get-tuple-element.11), channel_id=1, source_target_pairs={{0,3},{1,0},{2,1},{3,2},{4,7},{5,4},{6,5},{7,6},{8,11},{9,8},{10,9... | collective-permute-start | bytes 884744 | tf_op jit(solution)/shard_map/ppermute | solution.py:166
  42.9 17.1 %copy-start.3 = (bf16[128,2048]{1,0:T(8,128)(2,1)S(1)}, bf16[128,2048]{1,0:T(8,128)(2,1)}, u32[]{:S(2)}) copy-start(bf16[128,2048]{1,0:T(8,128)(2,1)} %residual.1) | copy-start | bytes 1572868
  42.9 17.1 %copy-start.6 = (s32[128,1]{0,1:T(1,128)S(1)}, s32[128,1]{0,1:T(1,128)}, u32[]{:S(2)}) copy-start(s32[128,1]{0,1:T(1,128)} %param.7) | copy-start | bytes 1540
  43.8 29.9 %all-to-all-start.2 = ((bf16[12,8,1536]{2,1,0:T(8,128)(2,1)}), bf16[12,8,1536]{2,1,0:T(8,128)(2,1)S(1)}, u32[]{:S(2)}, u32[]{:S(2)}) async-start(bf16[12,8,1536]{2,1,0:T(8,128)(2,1)} %bitcast.13), calls=%async_computation.2 | async-start | bytes 589824 | tf_op jit(solution)/shard_map/all_to_all | solution.py:169
  56.5 3.5 %collective-permute-start = (bf16[64,2304]{1,0:T(8,128)(2,1)S(1)}, bf16[64,2304]{1,0:T(8,128)(2,1)S(1)}, u32[]{:S(2)}, u32[]{:S(2)}) collective-permute-start(bf16[64,2304]{1,0:T(8,128)(2,1)S(1)} %slice_bitcast_fusion), channel_id=1, source_target_pairs={{0,48},{48,0},{1,49},{49,1},{2,50},{50,2},{3,51},{51,3},{4,52},{52... | collective-permute-start | bytes 884744 | tf_op jit(solution)/shard_map/ppermute | solution.py:164

commit v12 on v11

--- a/solution.py
+++ b/solution.py
@@ -48,7 +48,7 @@
     hidden[...] = jnp.where(preact[...].astype(F32) > 0, product, 0.0).astype(BF)
 
 
-def slot_body(hidden, w_in, slots):
+def slot_body(hidden, w_in, slots, spread):
     rows = hidden.shape[0]
     width = w_in.shape[1]
     k = iota((256, rows), 0)
@@ -64,32 +64,37 @@
         slots[:, span] = got[:128].astype(BF)
         last = jnp.where(row == r, got[128:], last)
     slots[:, width:] = last.astype(BF)
-
-
-def weight_body(hidden, inputs, routes, *outs):
-    rows, units = hidden.shape
+    me = lax.axis_index("x")
+    units = hidden.shape[1]
+    m = spread.shape[0] // X_DEV
+    j = iota((m, units), 0)
+    unit = iota((m, units), 1)
+    for k in range(X_DEV):
+        owner = X_DEV * (j >> 3) + ((me + k) & 3)
+        place = ((j & 7) < 6) & (unit == 6 * owner + (j & 7))
+        spread[m * k : m * k + m, :] = dot(as_bf(place), hidden[...], 1, 1).astype(BF)
+
+
+def weight_body(spread, inputs, routes, *outs):
+    rows = spread.shape[1]
     expert = 2 * lax.axis_index("y") + lax.axis_index("core")
     counts = jnp.sum((routes[...] == expert).astype(F32), axis=1, keepdims=True).astype(jnp.int32)
-    j = iota((96, units), 0)
-    unit = iota((96, units), 1)
     n = routes.shape[0]
     g = iota((n, rows), 1)
     first = CAP * iota((n, rows), 0)
     live = (g >= first) & (g < first + counts)
     mask = as_bf(jnp.sum(live.astype(F32), axis=0, keepdims=True) > 0.5)
-    me = lax.axis_index("x")
-    for k, out in enumerate(outs):
-        owner = X_DEV * (j >> 3) + ((me + k) & 3)
-        place = ((j & 7) < 6) & (unit == 6 * owner + (j & 7))
-        spread = dot(as_bf(place), hidden[...], 1, 1).astype(BF) * mask
-        last = dot(spread, inputs[:, 1536:])
-        sub = iota(last.shape, 0) & 7
-        for w in range(3):
-            span = slice(512 * w, 512 * w + 512)
-            tile = dot(spread, inputs[:, span])
-            tile = jnp.where(sub == 6, pltpu.roll(last, 6 - w, 0), tile)
-            tile = jnp.where(sub == 7, pltpu.roll(last, 4 - w, 0), tile)
-            out[:, span] = tile.astype(BF)
+    gated = spread[...] * mask
+    last = dot(gated, inputs[:, 1536:])
+    sub = iota(last.shape, 0) & 7
+    m = outs[0].shape[0]
+    for w in range(3):
+        span = slice(512 * w, 512 * w + 512)
+        tile = dot(gated, inputs[:, span])
+        tile = jnp.where(sub == 6, pltpu.roll(last, 6 - w, 0), tile)
+        tile = jnp.where(sub == 7, pltpu.roll(last, 4 - w, 0), tile).astype(BF)
+        for k, out in enumerate(outs):
+            out[:, span] = tile[m * k : m * k + m]
 
 
 def add_body(own, one, two, three, out):
@@ -152,11 +157,14 @@
         *[pltpu.with_memory_space_constraint(a[0], pltpu.VMEM) for a in (expert_grad, w_out, saved_preact)],
         flops=2 * slots * units * width,
     )
-    (slot_grad,) = call(
-        slot_body, [S((128, width + 256), BF)], hidden, w_in[0], flops=4 * 128 * units * width
+    slot_grad, spread = call(
+        slot_body,
+        [S((128, width + 256), BF), pltpu.VMEM((8 * groups, slots), BF)],
+        hidden, w_in[0],
+        flops=4 * 128 * units * width,
     )
     sends = call(
-        weight_body, [S((8 * Z_DEV, 1536), BF)] * X_DEV, hidden, saved_inputs[0], everyone,
+        weight_body, [S((8 * Z_DEV, 1536), BF)] * X_DEV, spread, saved_inputs[0], everyone,
         flops=2 * slots * 384 * width,
     )
     near = lax.all_to_all(slot_grad, "y", split_axis=0, concat_axis=0, tiled=True)

time: 74.8 us -> 74.1 us (level)
  transfers between devices with their start and end apart: 7 -> 7, of which waited for: 5 -> 5; matrix products, arithmetic and copies ran while one was open for 0% -> 0% of each run, Pallas kernels for 9% -> 8%
where the time goes in v12:
time: 74.1 us; the launch traced here: 73.7 us
  starting transfers between devices  40.7 us (55%)
  waiting for transfers between devices  24.5 us (33%)
  Pallas kernels  7.04 us (10%)
  between operations  0.75 us (1%)
    ppermute x3, starting transfers between devices, shift(): lax.ppermute(sends[i], 'x', [(j, (j + i) % X_DEV) for j in range(X_DEV)])  13.5 us
    all_to_all x1, starting transfers between devices, shards(): part = lax.all_to_all(part, 'z', split_axis=0, concat_axis=0, tiled=True)  12.7 us
    all_to_all x1, waiting for transfers between devices, shards(): part = lax.all_to_all(part, 'z', split_axis=0, concat_axis=0, tiled=True)  12 us
    all_to_all x1, starting transfers between devices, shards(): lax.all_to_all(everyone.reshape(16, 1, 128), experts, split_axis=0, conca...  7.69 us
    ppermute x3, waiting for transfers between devices, shift(): lax.ppermute(sends[i], 'x', [(j, (j + i) % X_DEV) for j in range(X_DEV)])  7.18 us
    pallas_call x7, Pallas kernels, call(): pl.pallas_call(body, out_shape=outs, compiler_params=pltpu.CompilerParams...  7.04 us
    all_to_all x1, starting transfers between devices, shards(): lax.all_to_all(slot_grad, 'y', split_axis=0, concat_axis=0, tiled=True)  4.92 us
    all_to_all x1, waiting for transfers between devices, shards(): lax.all_to_all(everyone.reshape(16, 1, 128), experts, split_axis=0, conca...  3.78 us
  transfers between devices with their start and end apart: 7, of which 5 were waited for; matrix products, arithmetic and copies ran while one was open for 0% of the time, Pallas kernels for 8%

profile of v12, /device:TPU:12, one launch (start us, length us, event | category | flops | bytes accessed | tf_op | source)
XLA Modules:
  0.0 73.7 jit_solution(7361554319427195438)
XLA Ops:
  0.6 0.0 copy-start.5
  0.6 0.6 copy-done.5
  1.3 0.0 copy-start.1
  1.3 0.0 copy-start.2
  1.3 0.0 copy-start.4
  1.3 0.6 shard_map.89
  1.9 0.0 copy-start
  1.9 7.7 %all-to-all-start.1 = ((s32[16,1,128]{2,1,0:T(1,128)}), s32[16,1,128]{2,1,0:T(1,128)S(1)}, u32[]{:S(2)}, u32[]{:S(2)}) async-start(s32[16,1,128]{2,1,0:T(1,128)} %bitcast.11), calls=%async_computation.1 | async-start | bytes 16384 | tf_op jit(solution)/shard_map/all_to_all | solution.py:151
  9.6 0.0 copy-done.1
  9.6 0.0 copy-done.2
  9.6 0.0 copy-done.4
  9.6 0.6 shard_map.86.hidden
  10.2 0.0 copy-done
  10.3 0.0 copy-start.7
  10.3 1.7 %shard_map.87 = (bf16[128,2304]{1,0:T(8,128)(2,1)}, bf16[384,144]{1,0:T(8,128)(2,1)S(1)}) custom-call(bf16[144,288]{1,0:T(8,128)(2,1)S(1)} %shard_map.86.hidden, bf16[288,2048]{1,0:T(8,128)(2,1)S(1)} %bitcast.20), custom_call_target="tpu_custom_call" | custom-call | flops 301989888 | bytes 1963008 | tf_op jit(solution)/shard_map/pallas_call | solution.py:33
  11.9 3.8 %all-to-all-done.1 = s32[16,1,128]{2,1,0:T(1,128)S(1)} async-done(((s32[16,1,128]{2,1,0:T(1,128)}), s32[16,1,128]{2,1,0:T(1,128)S(1)}, u32[]{:S(2)}, u32[]{:S(2)}) %all-to-all-start.1) | async-done | bytes 8224 | tf_op jit(solution)/shard_map/all_to_all | solution.py:151
  15.7 4.9 %all-to-all-start = ((bf16[8,16,2304]{2,1,0:T(8,128)(2,1)}), bf16[8,16,2304]{2,1,0:T(8,128)(2,1)S(1)}, u32[]{:S(2)}, u32[]{:S(2)}) async-start(bf16[8,16,2304]{2,1,0:T(8,128)(2,1)} %bitcast.5), calls=%async_computation | async-start | bytes 1179648 | tf_op jit(solution)/shard_map/all_to_all | solution.py:170
  20.6 0.0 copy-done.7
  20.6 0.9 %shard_map.90 = (bf16[96,1536]{1,0:T(8,128)(2,1)S(1)}, bf16[96,1536]{1,0:T(8,128)(2,1)S(1)}, bf16[96,1536]{1,0:T(8,128)(2,1)S(1)}, bf16[96,1536]{1,0:T(8,128)(2,1)S(1)}) custom-call(bf16[384,144]{1,0:T(8,128)(2,1)S(1)} %get-tuple-element.11.spread, bf16[144,2048]{1,0:T(8,128)(2,1)S(1)} %bitcast.28, s32[16,128]{1,0:T(8,128)S(1)} %bitcast.25), custom_call_target="tpu_custom_call" | custom-call | flops 226492416 | bytes 1888256 | tf_op jit(solution)/shard_map/pallas_call | solution.py:33
  21.6 7.6 %collective-permute-start.1 = (bf16[96,1536]{1,0:T(8,128)(2,1)S(1)}, bf16[96,1536]{1,0:T(8,128)(2,1)S(1)}, u32[]{:S(2)}, u32[]{:S(2)}) collective-permute-start(bf16[96,1536]{1,0:T(8,128)(2,1)S(1)} %get-tuple-element.13), channel_id=1, source_target_pairs={{0,2},{1,3},{2,0},{3,1},{4,6},{5,7},{6,4},{7,5},{8,10},{9,11},{10,... | collective-permute-start | bytes 884744 | tf_op jit(solution)/shard_map/ppermute | solution.py:174
  29.2 1.9 %collective-permute-start.2 = (bf16[96,1536]{1,0:T(8,128)(2,1)S(1)}, bf16[96,1536]{1,0:T(8,128)(2,1)S(1)}, u32[]{:S(2)}, u32[]{:S(2)}) collective-permute-start(bf16[96,1536]{1,0:T(8,128)(2,1)S(1)} %get-tuple-element.14), channel_id=1, source_target_pairs={{0,1},{1,2},{2,3},{3,0},{4,5},{5,6},{6,7},{7,4},{8,9},{9,10},{10,1... | collective-permute-start | bytes 884744 | tf_op jit(solution)/shard_map/ppermute | solution.py:174
  31.1 3.9 %collective-permute-start.3 = (bf16[96,1536]{1,0:T(8,128)(2,1)S(1)}, bf16[96,1536]{1,0:T(8,128)(2,1)S(1)}, u32[]{:S(2)}, u32[]{:S(2)}) collective-permute-start(bf16[96,1536]{1,0:T(8,128)(2,1)S(1)} %get-tuple-element.15), channel_id=1, source_target_pairs={{0,3},{1,0},{2,1},{3,2},{4,7},{5,4},{6,5},{7,6},{8,11},{9,8},{10,9... | collective-permute-start | bytes 884744 | tf_op jit(solution)/shard_map/ppermute | solution.py:174
  35.1 2.0 %collective-permute-done.1.one = bf16[96,1536]{1,0:T(8,128)(2,1)S(1)} collective-permute-done((bf16[96,1536]{1,0:T(8,128)(2,1)S(1)}, bf16[96,1536]{1,0:T(8,128)(2,1)S(1)}, u32[]{:S(2)}, u32[]{:S(2)}) %collective-permute-start.1) | collective-permute-done | bytes 294944 | tf_op jit(solution)/shard_map/ppermute | solution.py:174
  37.1 5.1 %collective-permute-done.2.two = bf16[96,1536]{1,0:T(8,128)(2,1)S(1)} collective-permute-done((bf16[96,1536]{1,0:T(8,128)(2,1)S(1)}, bf16[96,1536]{1,0:T(8,128)(2,1)S(1)}, u32[]{:S(2)}, u32[]{:S(2)}) %collective-permute-start.2) | collective-permute-done | bytes 294944 | tf_op jit(solution)/shard_map/ppermute | solution.py:174
  42.2 0.0 collective-permute-done.3.three
  42.2 0.0 copy-start.3
  42.2 0.0 copy-start.6
  42.2 0.9 %shard_map.91 = bf16[96,1536]{1,0:T(8,128)(2,1)} custom-call(bf16[96,1536]{1,0:T(8,128)(2,1)S(1)} %get-tuple-element.12.own, bf16[96,1536]{1,0:T(8,128)(2,1)S(1)} %collective-permute-done.1.one, bf16[96,1536]{1,0:T(8,128)(2,1)S(1)} %collective-permute-done.2.two, bf16[96,1536]{1,0:T(8,128)(2,1)S(1)} %collective-permute-done.3.three), custom_call_target="tpu_custom_call" | custom-call | bytes 1474560 | tf_op jit(solution)/shard_map/pallas_call | solution.py:33
  43.1 0.0 all-to-all-done
  43.1 12.7 %all-to-all-start.2 = ((bf16[12,8,1536]{2,1,0:T(8,128)(2,1)}), bf16[12,8,1536]{2,1,0:T(8,128)(2,1)S(1)}, u32[]{:S(2)}, u32[]{:S(2)}) async-start(bf16[12,8,1536]{2,1,0:T(8,128)(2,1)} %bitcast.13), calls=%async_computation.2 | async-start | bytes 589824 | tf_op jit(solution)/shard_map/all_to_all | solution.py:177
  55.8 1.9 %collective-permute-start = (bf16[64,2304]{1,0:T(8,128)(2,1)S(1)}, bf16[64,2304]{1,0:T(8,128)(2,1)S(1)}, u32[]{:S(2)}, u32[]{:S(2)}) collective-permute-start(bf16[64,2304]{1,0:T(8,128)(2,1)S(1)} %slice_bitcast_fusion), channel_id=1, source_target_pairs={{0,48},{48,0},{1,49},{49,1},{2,50},{50,2},{3,51},{51,3},{4,52},{52... | collective-permute-start | bytes 884744 | tf_op jit(solution)/shard_map/ppermute | solution.py:172
  57.8 1.5 %collective-permute-done.far = bf16[64,2304]{1,0:T(8,128)(2,1)S(1)} collective-permute-done((bf16[64,2304]{1,0:T(8,128)(2,1)S(1)}, bf16[64,2304]{1,0:T(8,128)(2,1)S(1)}, u32[]{:S(2)}, u32[]{:S(2)}) %collective-permute-start) | collective-permute-done | bytes 294944 | tf_op jit(solution)/shard_map/ppermute | solution.py:172
  59.3 0.0 copy-done.3
  59.3 0.0 copy-done.6
  59.3 1.7 %shard_map.88 = bf16[128,2048]{1,0:T(8,128)(2,1)} custom-call(s32[1,128]{1,0:T(1,128)S(1)} %bitcast.27, bf16[128,2048]{1,0:T(8,128)(2,1)S(1)} %copy-done.3, bf16[128,2304]{1,0:T(8,128)(2,1)S(1)} %bitcast.19, bf16[64,2304]{1,0:T(8,128)(2,1)S(1)} %collective-permute-done.far), custom_call_target="tpu_custom_call" | custom-call | flops 201326592 | bytes 1933824 | tf_op jit(solution)/shard_map/pallas_call | solution.py:33
  61.0 12.0 %all-to-all-done.2 = bf16[12,8,1536]{2,1,0:T(8,128)(2,1)S(1)} async-done(((bf16[12,8,1536]{2,1,0:T(8,128)(2,1)}), bf16[12,8,1536]{2,1,0:T(8,128)(2,1)S(1)}, u32[]{:S(2)}, u32[]{:S(2)}) %all-to-all-start.2) | async-done | bytes 294944 | tf_op jit(solution)/shard_map/all_to_all | solution.py:177
  73.0 0.7 shard_map.92
  (1 shorter events, 0.0 us)
Async XLA Ops:
  0.6 0.7 copy-start.5
  1.3 8.3 %copy-start.1 = (bf16[1,288,2048]{2,1,0:T(8,128)(2,1)S(1)}, bf16[1,288,2048]{2,1,0:T(8,128)(2,1)}, u32[]{:S(2)}) copy-start(bf16[1,288,2048]{2,1,0:T(8,128)(2,1)} %param.13) | copy-start | bytes 3538948
  1.3 8.3 %copy-start.2 = (bf16[1,144,2048]{2,1,0:T(8,128)(2,1)S(1)}, bf16[1,144,2048]{2,1,0:T(8,128)(2,1)}, u32[]{:S(2)}) copy-start(bf16[1,144,2048]{2,1,0:T(8,128)(2,1)} %param.11) | copy-start | bytes 1769476
  1.3 8.3 %copy-start.4 = (bf16[1,144,288]{2,1,0:T(8,128)(2,1)S(1)}, bf16[1,144,288]{2,1,0:T(8,128)(2,1)}, u32[]{:S(2)}) copy-start(bf16[1,144,288]{2,1,0:T(8,128)(2,1)} %param.10) | copy-start | bytes 248836
  1.9 8.3 %copy-start = (bf16[1,288,2048]{2,1,0:T(8,128)(2,1)S(1)}, bf16[1,288,2048]{2,1,0:T(8,128)(2,1)}, u32[]{:S(2)}) copy-start(bf16[1,288,2048]{2,1,0:T(8,128)(2,1)} %param.12) | copy-start | bytes 3538948
  1.9 13.8 %all-to-all-start.1 = ((s32[16,1,128]{2,1,0:T(1,128)}), s32[16,1,128]{2,1,0:T(1,128)S(1)}, u32[]{:S(2)}, u32[]{:S(2)}) async-start(s32[16,1,128]{2,1,0:T(1,128)} %bitcast.11), calls=%async_computation.1 | async-start | bytes 16384 | tf_op jit(solution)/shard_map/all_to_all | solution.py:151
  10.3 10.4 %copy-start.7 = (bf16[1,144,2048]{2,1,0:T(8,128)(2,1)S(1)}, bf16[1,144,2048]{2,1,0:T(8,128)(2,1)}, u32[]{:S(2)}) copy-start(bf16[1,144,2048]{2,1,0:T(8,128)(2,1)} %param.9) | copy-start | bytes 1769476
  15.7 27.4 %all-to-all-start = ((bf16[8,16,2304]{2,1,0:T(8,128)(2,1)}), bf16[8,16,2304]{2,1,0:T(8,128)(2,1)S(1)}, u32[]{:S(2)}, u32[]{:S(2)}) async-start(bf16[8,16,2304]{2,1,0:T(8,128)(2,1)} %bitcast.5), calls=%async_computation | async-start | bytes 1179648 | tf_op jit(solution)/shard_map/all_to_all | solution.py:170
  21.6 15.5 %collective-permute-start.1 = (bf16[96,1536]{1,0:T(8,128)(2,1)S(1)}, bf16[96,1536]{1,0:T(8,128)(2,1)S(1)}, u32[]{:S(2)}, u32[]{:S(2)}) collective-permute-start(bf16[96,1536]{1,0:T(8,128)(2,1)S(1)} %get-tuple-element.13), channel_id=1, source_target_pairs={{0,2},{1,3},{2,0},{3,1},{4,6},{5,7},{6,4},{7,5},{8,10},{9,11},{10,... | collective-permute-start | bytes 884744 | tf_op jit(solution)/shard_map/ppermute | solution.py:174
  29.2 13.0 %collective-permute-start.2 = (bf16[96,1536]{1,0:T(8,128)(2,1)S(1)}, bf16[96,1536]{1,0:T(8,128)(2,1)S(1)}, u32[]{:S(2)}, u32[]{:S(2)}) collective-permute-start(bf16[96,1536]{1,0:T(8,128)(2,1)S(1)} %get-tuple-element.14), channel_id=1, source_target_pairs={{0,1},{1,2},{2,3},{3,0},{4,5},{5,6},{6,7},{7,4},{8,9},{9,10},{10,1... | collective-permute-start | bytes 884744 | tf_op jit(solution)/shard_map/ppermute | solution.py:174
  31.1 11.1 %collective-permute-start.3 = (bf16[96,1536]{1,0:T(8,128)(2,1)S(1)}, bf16[96,1536]{1,0:T(8,128)(2,1)S(1)}, u32[]{:S(2)}, u32[]{:S(2)}) collective-permute-start(bf16[96,1536]{1,0:T(8,128)(2,1)S(1)} %get-tuple-element.15), channel_id=1, source_target_pairs={{0,3},{1,0},{2,1},{3,2},{4,7},{5,4},{6,5},{7,6},{8,11},{9,8},{10,9... | collective-permute-start | bytes 884744 | tf_op jit(solution)/shard_map/ppermute | solution.py:174
  42.2 17.1 %copy-start.3 = (bf16[128,2048]{1,0:T(8,128)(2,1)S(1)}, bf16[128,2048]{1,0:T(8,128)(2,1)}, u32[]{:S(2)}) copy-start(bf16[128,2048]{1,0:T(8,128)(2,1)} %residual.1) | copy-start | bytes 1572868
  42.2 17.1 %copy-start.6 = (s32[128,1]{0,1:T(1,128)S(1)}, s32[128,1]{0,1:T(1,128)}, u32[]{:S(2)}) copy-start(s32[128,1]{0,1:T(1,128)} %param.7) | copy-start | bytes 1540
  43.1 29.9 %all-to-all-start.2 = ((bf16[12,8,1536]{2,1,0:T(8,128)(2,1)}), bf16[12,8,1536]{2,1,0:T(8,128)(2,1)S(1)}, u32[]{:S(2)}, u32[]{:S(2)}) async-start(bf16[12,8,1536]{2,1,0:T(8,128)(2,1)} %bitcast.13), calls=%async_computation.2 | async-start | bytes 589824 | tf_op jit(solution)/shard_map/all_to_all | solution.py:177
  55.8 3.5 %collective-permute-start = (bf16[64,2304]{1,0:T(8,128)(2,1)S(1)}, bf16[64,2304]{1,0:T(8,128)(2,1)S(1)}, u32[]{:S(2)}, u32[]{:S(2)}) collective-permute-start(bf16[64,2304]{1,0:T(8,128)(2,1)S(1)} %slice_bitcast_fusion), channel_id=1, source_target_pairs={{0,48},{48,0},{1,49},{49,1},{2,50},{50,2},{3,51},{51,3},{4,52},{52... | collective-permute-start | bytes 884744 | tf_op jit(solution)/shard_map/ppermute | solution.py:172

commit v13 on v12

--- a/solution.py
+++ b/solution.py
@@ -97,7 +97,7 @@
             out[:, span] = tile[m * k : m * k + m]
 
 
-def add_body(own, one, two, three, out):
+def add_body(own, two, three, one, out):
     total = (own[...].astype(F32) + one[...].astype(F32)) + (two[...].astype(F32) + three[...].astype(F32))
     out[...] = total.astype(BF)
 
@@ -173,7 +173,7 @@
     def shift(i):
         return lax.ppermute(sends[i], "x", [(j, (j + i) % X_DEV) for j in range(X_DEV)])
 
-    (part,) = call(add_body, [S((8 * Z_DEV, 1536), BF)], sends[0], shift(2), shift(1), shift(3))
+    (part,) = call(add_body, [S((8 * Z_DEV, 1536), BF)], sends[0], shift(2), shift(3), shift(1))
     part = lax.all_to_all(part, "z", split_axis=0, concat_axis=0, tiled=True)
     (token_grad,) = call(
         token_body, [S((128, width), BF)], ids, residual_grad, near, far,

time: 74.1 us -> 74.1 us (level)
  the two profiles are of different devices: /device:TPU:12 before, /device:TPU:14 now
where the time goes in v13:
time: 74.1 us; the launch traced here: 73.7 us
  starting transfers between devices  39 us (53%)
  waiting for transfers between devices  26.2 us (35%)
  Pallas kernels  7.05 us (10%)
  between operations  0.75 us (1%)
    ppermute x3, starting transfers between devices, shift(): lax.ppermute(sends[i], 'x', [(j, (j + i) % X_DEV) for j in range(X_DEV)])  12.3 us
    all_to_all x1, starting transfers between devices, shards(): part = lax.all_to_all(part, 'z', split_axis=0, concat_axis=0, tiled=True)  12.2 us
    all_to_all x1, waiting for transfers between devices, shards(): part = lax.all_to_all(part, 'z', split_axis=0, concat_axis=0, tiled=True)  12 us
    ppermute x3, waiting for transfers between devices, shift(): lax.ppermute(sends[i], 'x', [(j, (j + i) % X_DEV) for j in range(X_DEV)])  8.9 us
    all_to_all x1, starting transfers between devices, shards(): lax.all_to_all(everyone.reshape(16, 1, 128), experts, split_axis=0, conca...  7.69 us
    pallas_call x7, Pallas kernels, call(): pl.pallas_call(body, out_shape=outs, compiler_params=pltpu.CompilerParams...  7.05 us
    all_to_all x1, starting transfers between devices, shards(): lax.all_to_all(slot_grad, 'y', split_axis=0, concat_axis=0, tiled=True)  4.92 us
    all_to_all x1, waiting for transfers between devices, shards(): lax.all_to_all(everyone.reshape(16, 1, 128), experts, split_axis=0, conca...  3.77 us
  transfers between devices with their start and end apart: 7, of which 6 were waited for; matrix products, arithmetic and copies ran while one was open for 0% of the time, Pallas kernels for 8%

profile of v13, /device:TPU:14, one launch (start us, length us, event | category | flops | bytes accessed | tf_op | source)
XLA Modules:
  0.0 73.7 jit_solution(12250558177787558299)
XLA Ops:
  0.6 0.0 copy-start.5
  0.6 0.6 copy-done.5
  1.3 0.0 copy-start.1
  1.3 0.0 copy-start.2
  1.3 0.0 copy-start.4
  1.3 0.6 shard_map.89
  1.9 0.0 copy-start
  1.9 7.7 %all-to-all-start.1 = ((s32[16,1,128]{2,1,0:T(1,128)}), s32[16,1,128]{2,1,0:T(1,128)S(1)}, u32[]{:S(2)}, u32[]{:S(2)}) async-start(s32[16,1,128]{2,1,0:T(1,128)} %bitcast.11), calls=%async_computation.1 | async-start | bytes 16384 | tf_op jit(solution)/shard_map/all_to_all | solution.py:151
  9.6 0.0 copy-done.1
  9.6 0.0 copy-done.2
  9.6 0.0 copy-done.4
  9.6 0.6 shard_map.86.hidden
  10.2 0.0 copy-done
  10.3 0.0 copy-start.7
  10.3 1.7 %shard_map.87 = (bf16[128,2304]{1,0:T(8,128)(2,1)}, bf16[384,144]{1,0:T(8,128)(2,1)S(1)}) custom-call(bf16[144,288]{1,0:T(8,128)(2,1)S(1)} %shard_map.86.hidden, bf16[288,2048]{1,0:T(8,128)(2,1)S(1)} %bitcast.20), custom_call_target="tpu_custom_call" | custom-call | flops 301989888 | bytes 1963008 | tf_op jit(solution)/shard_map/pallas_call | solution.py:33
  11.9 3.8 %all-to-all-done.1 = s32[16,1,128]{2,1,0:T(1,128)S(1)} async-done(((s32[16,1,128]{2,1,0:T(1,128)}), s32[16,1,128]{2,1,0:T(1,128)S(1)}, u32[]{:S(2)}, u32[]{:S(2)}) %all-to-all-start.1) | async-done | bytes 8224 | tf_op jit(solution)/shard_map/all_to_all | solution.py:151
  15.7 4.9 %all-to-all-start = ((bf16[8,16,2304]{2,1,0:T(8,128)(2,1)}), bf16[8,16,2304]{2,1,0:T(8,128)(2,1)S(1)}, u32[]{:S(2)}, u32[]{:S(2)}) async-start(bf16[8,16,2304]{2,1,0:T(8,128)(2,1)} %bitcast.5), calls=%async_computation | async-start | bytes 1179648 | tf_op jit(solution)/shard_map/all_to_all | solution.py:170
  20.6 0.0 copy-done.7
  20.6 0.9 %shard_map.90 = (bf16[96,1536]{1,0:T(8,128)(2,1)S(1)}, bf16[96,1536]{1,0:T(8,128)(2,1)S(1)}, bf16[96,1536]{1,0:T(8,128)(2,1)S(1)}, bf16[96,1536]{1,0:T(8,128)(2,1)S(1)}) custom-call(bf16[384,144]{1,0:T(8,128)(2,1)S(1)} %get-tuple-element.11.spread, bf16[144,2048]{1,0:T(8,128)(2,1)S(1)} %bitcast.28, s32[16,128]{1,0:T(8,128)S(1)} %bitcast.25), custom_call_target="tpu_custom_call" | custom-call | flops 226492416 | bytes 1888256 | tf_op jit(solution)/shard_map/pallas_call | solution.py:33
  21.6 3.3 %collective-permute-start.1 = (bf16[96,1536]{1,0:T(8,128)(2,1)S(1)}, bf16[96,1536]{1,0:T(8,128)(2,1)S(1)}, u32[]{:S(2)}, u32[]{:S(2)}) collective-permute-start(bf16[96,1536]{1,0:T(8,128)(2,1)S(1)} %get-tuple-element.13), channel_id=1, source_target_pairs={{0,2},{1,3},{2,0},{3,1},{4,6},{5,7},{6,4},{7,5},{8,10},{9,11},{10,... | collective-permute-start | bytes 884744 | tf_op jit(solution)/shard_map/ppermute | solution.py:174
  24.9 7.1 %collective-permute-start.2 = (bf16[96,1536]{1,0:T(8,128)(2,1)S(1)}, bf16[96,1536]{1,0:T(8,128)(2,1)S(1)}, u32[]{:S(2)}, u32[]{:S(2)}) collective-permute-start(bf16[96,1536]{1,0:T(8,128)(2,1)S(1)} %get-tuple-element.14), channel_id=1, source_target_pairs={{0,3},{1,0},{2,1},{3,2},{4,7},{5,4},{6,5},{7,6},{8,11},{9,8},{10,9... | collective-permute-start | bytes 884744 | tf_op jit(solution)/shard_map/ppermute | solution.py:174
  31.9 1.9 %collective-permute-start.3 = (bf16[96,1536]{1,0:T(8,128)(2,1)S(1)}, bf16[96,1536]{1,0:T(8,128)(2,1)S(1)}, u32[]{:S(2)}, u32[]{:S(2)}) collective-permute-start(bf16[96,1536]{1,0:T(8,128)(2,1)S(1)} %get-tuple-element.15), channel_id=1, source_target_pairs={{0,1},{1,2},{2,3},{3,0},{4,5},{5,6},{6,7},{7,4},{8,9},{9,10},{10,1... | collective-permute-start | bytes 884744 | tf_op jit(solution)/shard_map/ppermute | solution.py:174
  33.9 0.3 collective-permute-done.1.two
  34.2 5.6 %collective-permute-done.2.three = bf16[96,1536]{1,0:T(8,128)(2,1)S(1)} collective-permute-done((bf16[96,1536]{1,0:T(8,128)(2,1)S(1)}, bf16[96,1536]{1,0:T(8,128)(2,1)S(1)}, u32[]{:S(2)}, u32[]{:S(2)}) %collective-permute-start.2) | collective-permute-done | bytes 294944 | tf_op jit(solution)/shard_map/ppermute | solution.py:174
  39.8 3.0 %collective-permute-done.3.one = bf16[96,1536]{1,0:T(8,128)(2,1)S(1)} collective-permute-done((bf16[96,1536]{1,0:T(8,128)(2,1)S(1)}, bf16[96,1536]{1,0:T(8,128)(2,1)S(1)}, u32[]{:S(2)}, u32[]{:S(2)}) %collective-permute-start.3) | collective-permute-done | bytes 294944 | tf_op jit(solution)/shard_map/ppermute | solution.py:174
  42.8 0.0 copy-start.3
  42.8 0.0 copy-start.6
  42.8 0.9 %shard_map.91 = bf16[96,1536]{1,0:T(8,128)(2,1)} custom-call(bf16[96,1536]{1,0:T(8,128)(2,1)S(1)} %get-tuple-element.12.own, bf16[96,1536]{1,0:T(8,128)(2,1)S(1)} %collective-permute-done.1.two, bf16[96,1536]{1,0:T(8,128)(2,1)S(1)} %collective-permute-done.2.three, bf16[96,1536]{1,0:T(8,128)(2,1)S(1)} %collective-permute-done.3.one), custom_call_target="tpu_custom_call" | custom-call | bytes 1474560 | tf_op jit(solution)/shard_map/pallas_call | solution.py:33
  43.6 0.0 all-to-all-done
  43.6 12.2 %all-to-all-start.2 = ((bf16[12,8,1536]{2,1,0:T(8,128)(2,1)}), bf16[12,8,1536]{2,1,0:T(8,128)(2,1)S(1)}, u32[]{:S(2)}, u32[]{:S(2)}) async-start(bf16[12,8,1536]{2,1,0:T(8,128)(2,1)} %bitcast.13), calls=%async_computation.2 | async-start | bytes 589824 | tf_op jit(solution)/shard_map/all_to_all | solution.py:177
  55.8 1.9 %collective-permute-start = (bf16[64,2304]{1,0:T(8,128)(2,1)S(1)}, bf16[64,2304]{1,0:T(8,128)(2,1)S(1)}, u32[]{:S(2)}, u32[]{:S(2)}) collective-permute-start(bf16[64,2304]{1,0:T(8,128)(2,1)S(1)} %slice_bitcast_fusion), channel_id=1, source_target_pairs={{0,48},{48,0},{1,49},{49,1},{2,50},{50,2},{3,51},{51,3},{4,52},{52... | collective-permute-start | bytes 884744 | tf_op jit(solution)/shard_map/ppermute | solution.py:172
  57.7 1.5 %collective-permute-done.far = bf16[64,2304]{1,0:T(8,128)(2,1)S(1)} collective-permute-done((bf16[64,2304]{1,0:T(8,128)(2,1)S(1)}, bf16[64,2304]{1,0:T(8,128)(2,1)S(1)}, u32[]{:S(2)}, u32[]{:S(2)}) %collective-permute-start) | collective-permute-done | bytes 294944 | tf_op jit(solution)/shard_map/ppermute | solution.py:172
  59.3 0.0 copy-done.3
  59.3 0.0 copy-done.6
  59.3 1.7 %shard_map.88 = bf16[128,2048]{1,0:T(8,128)(2,1)} custom-call(s32[1,128]{1,0:T(1,128)S(1)} %bitcast.27, bf16[128,2048]{1,0:T(8,128)(2,1)S(1)} %copy-done.3, bf16[128,2304]{1,0:T(8,128)(2,1)S(1)} %bitcast.19, bf16[64,2304]{1,0:T(8,128)(2,1)S(1)} %collective-permute-done.far), custom_call_target="tpu_custom_call" | custom-call | flops 201326592 | bytes 1933824 | tf_op jit(solution)/shard_map/pallas_call | solution.py:33
  61.0 12.0 %all-to-all-done.2 = bf16[12,8,1536]{2,1,0:T(8,128)(2,1)S(1)} async-done(((bf16[12,8,1536]{2,1,0:T(8,128)(2,1)}), bf16[12,8,1536]{2,1,0:T(8,128)(2,1)S(1)}, u32[]{:S(2)}, u32[]{:S(2)}) %all-to-all-start.2) | async-done | bytes 294944 | tf_op jit(solution)/shard_map/all_to_all | solution.py:177
  73.0 0.7 shard_map.92
  (1 shorter events, 0.0 us)
Async XLA Ops:
  0.6 0.7 copy-start.5
  1.3 8.3 %copy-start.1 = (bf16[1,288,2048]{2,1,0:T(8,128)(2,1)S(1)}, bf16[1,288,2048]{2,1,0:T(8,128)(2,1)}, u32[]{:S(2)}) copy-start(bf16[1,288,2048]{2,1,0:T(8,128)(2,1)} %param.13) | copy-start | bytes 3538948
  1.3 8.3 %copy-start.2 = (bf16[1,144,2048]{2,1,0:T(8,128)(2,1)S(1)}, bf16[1,144,2048]{2,1,0:T(8,128)(2,1)}, u32[]{:S(2)}) copy-start(bf16[1,144,2048]{2,1,0:T(8,128)(2,1)} %param.11) | copy-start | bytes 1769476
  1.3 8.3 %copy-start.4 = (bf16[1,144,288]{2,1,0:T(8,128)(2,1)S(1)}, bf16[1,144,288]{2,1,0:T(8,128)(2,1)}, u32[]{:S(2)}) copy-start(bf16[1,144,288]{2,1,0:T(8,128)(2,1)} %param.10) | copy-start | bytes 248836
  1.9 8.3 %copy-start = (bf16[1,288,2048]{2,1,0:T(8,128)(2,1)S(1)}, bf16[1,288,2048]{2,1,0:T(8,128)(2,1)}, u32[]{:S(2)}) copy-start(bf16[1,288,2048]{2,1,0:T(8,128)(2,1)} %param.12) | copy-start | bytes 3538948
  1.9 13.8 %all-to-all-start.1 = ((s32[16,1,128]{2,1,0:T(1,128)}), s32[16,1,128]{2,1,0:T(1,128)S(1)}, u32[]{:S(2)}, u32[]{:S(2)}) async-start(s32[16,1,128]{2,1,0:T(1,128)} %bitcast.11), calls=%async_computation.1 | async-start | bytes 16384 | tf_op jit(solution)/shard_map/all_to_all | solution.py:151
  10.3 10.4 %copy-start.7 = (bf16[1,144,2048]{2,1,0:T(8,128)(2,1)S(1)}, bf16[1,144,2048]{2,1,0:T(8,128)(2,1)}, u32[]{:S(2)}) copy-start(bf16[1,144,2048]{2,1,0:T(8,128)(2,1)} %param.9) | copy-start | bytes 1769476
  15.7 27.9 %all-to-all-start = ((bf16[8,16,2304]{2,1,0:T(8,128)(2,1)}), bf16[8,16,2304]{2,1,0:T(8,128)(2,1)S(1)}, u32[]{:S(2)}, u32[]{:S(2)}) async-start(bf16[8,16,2304]{2,1,0:T(8,128)(2,1)} %bitcast.5), calls=%async_computation | async-start | bytes 1179648 | tf_op jit(solution)/shard_map/all_to_all | solution.py:170
  21.6 12.6 %collective-permute-start.1 = (bf16[96,1536]{1,0:T(8,128)(2,1)S(1)}, bf16[96,1536]{1,0:T(8,128)(2,1)S(1)}, u32[]{:S(2)}, u32[]{:S(2)}) collective-permute-start(bf16[96,1536]{1,0:T(8,128)(2,1)S(1)} %get-tuple-element.13), channel_id=1, source_target_pairs={{0,2},{1,3},{2,0},{3,1},{4,6},{5,7},{6,4},{7,5},{8,10},{9,11},{10,... | collective-permute-start | bytes 884744 | tf_op jit(solution)/shard_map/ppermute | solution.py:174
  24.9 14.9 %collective-permute-start.2 = (bf16[96,1536]{1,0:T(8,128)(2,1)S(1)}, bf16[96,1536]{1,0:T(8,128)(2,1)S(1)}, u32[]{:S(2)}, u32[]{:S(2)}) collective-permute-start(bf16[96,1536]{1,0:T(8,128)(2,1)S(1)} %get-tuple-element.14), channel_id=1, source_target_pairs={{0,3},{1,0},{2,1},{3,2},{4,7},{5,4},{6,5},{7,6},{8,11},{9,8},{10,9... | collective-permute-start | bytes 884744 | tf_op jit(solution)/shard_map/ppermute | solution.py:174
  31.9 10.8 %collective-permute-start.3 = (bf16[96,1536]{1,0:T(8,128)(2,1)S(1)}, bf16[96,1536]{1,0:T(8,128)(2,1)S(1)}, u32[]{:S(2)}, u32[]{:S(2)}) collective-permute-start(bf16[96,1536]{1,0:T(8,128)(2,1)S(1)} %get-tuple-element.15), channel_id=1, source_target_pairs={{0,1},{1,2},{2,3},{3,0},{4,5},{5,6},{6,7},{7,4},{8,9},{9,10},{10,1... | collective-permute-start | bytes 884744 | tf_op jit(solution)/shard_map/ppermute | solution.py:174
  42.8 16.5 %copy-start.3 = (bf16[128,2048]{1,0:T(8,128)(2,1)S(1)}, bf16[128,2048]{1,0:T(8,128)(2,1)}, u32[]{:S(2)}) copy-start(bf16[128,2048]{1,0:T(8,128)(2,1)} %residual.1) | copy-start | bytes 1572868
  42.8 16.5 %copy-start.6 = (s32[128,1]{0,1:T(1,128)S(1)}, s32[128,1]{0,1:T(1,128)}, u32[]{:S(2)}) copy-start(s32[128,1]{0,1:T(1,128)} %param.7) | copy-start | bytes 1540
  43.6 29.4 %all-to-all-start.2 = ((bf16[12,8,1536]{2,1,0:T(8,128)(2,1)}), bf16[12,8,1536]{2,1,0:T(8,128)(2,1)S(1)}, u32[]{:S(2)}, u32[]{:S(2)}) async-start(bf16[12,8,1536]{2,1,0:T(8,128)(2,1)} %bitcast.13), calls=%async_computation.2 | async-start | bytes 589824 | tf_op jit(solution)/shard_map/all_to_all | solution.py:177
  55.8 3.5 %collective-permute-start = (bf16[64,2304]{1,0:T(8,128)(2,1)S(1)}, bf16[64,2304]{1,0:T(8,128)(2,1)S(1)}, u32[]{:S(2)}, u32[]{:S(2)}) collective-permute-start(bf16[64,2304]{1,0:T(8,128)(2,1)S(1)} %slice_bitcast_fusion), channel_id=1, source_target_pairs={{0,48},{48,0},{1,49},{49,1},{2,50},{50,2},{3,51},{51,3},{4,52},{52... | collective-permute-start | bytes 884744 | tf_op jit(solution)/shard_map/ppermute | solution.py:172

commit v14 on v13

--- a/solution.py
+++ b/solution.py
@@ -70,7 +70,7 @@
     j = iota((m, units), 0)
     unit = iota((m, units), 1)
     for k in range(X_DEV):
-        owner = X_DEV * (j >> 3) + ((me + k) & 3)
+        owner = X_DEV * (j >> 3) + (me ^ k)
         place = ((j & 7) < 6) & (unit == 6 * owner + (j & 7))
         spread[m * k : m * k + m, :] = dot(as_bf(place), hidden[...], 1, 1).astype(BF)
 
@@ -97,8 +97,8 @@
             out[:, span] = tile[m * k : m * k + m]
 
 
-def add_body(own, two, three, one, out):
-    total = (own[...].astype(F32) + one[...].astype(F32)) + (two[...].astype(F32) + three[...].astype(F32))
+def add_body(own, two, one, three, out):
+    total = (own[...].astype(F32) + two[...].astype(F32)) + (one[...].astype(F32) + three[...].astype(F32))
     out[...] = total.astype(BF)
 
 
@@ -170,10 +170,10 @@
     near = lax.all_to_all(slot_grad, "y", split_axis=0, concat_axis=0, tiled=True)
     far = near.reshape(8, 2, 8, width + 256)[:, 1].reshape(64, width + 256)
     far = lax.ppermute(far, "core", [(0, 1), (1, 0)])
-    def shift(i):
-        return lax.ppermute(sends[i], "x", [(j, (j + i) % X_DEV) for j in range(X_DEV)])
-
-    (part,) = call(add_body, [S((8 * Z_DEV, 1536), BF)], sends[0], shift(2), shift(3), shift(1))
+    def swap(k):
+        return lax.ppermute(sends[k], "x", [(j, j ^ k) for j in range(X_DEV)])
+
+    (part,) = call(add_body, [S((8 * Z_DEV, 1536), BF)], sends[0], swap(2), swap(1), swap(3))
     part = lax.all_to_all(part, "z", split_axis=0, concat_axis=0, tiled=True)
     (token_grad,) = call(
         token_body, [S((128, width), BF)], ids, residual_grad, near, far,

time: 74.1 us -> 73.6 us (level)
  the two profiles are of different devices: /device:TPU:14 before, /device:TPU:12 now
where the time goes in v14:
time: 73.6 us; the launch traced here: 73 us
  starting transfers between devices  39.2 us (53%)
  waiting for transfers between devices  25.3 us (34%)
  Pallas kernels  7.04 us (10%)
  between operations  0.75 us (1%)
    all_to_all x1, starting transfers between devices, shards(): part = lax.all_to_all(part, 'z', split_axis=0, concat_axis=0, tiled=True)  12.6 us
    ppermute x3, starting transfers between devices, swap(): return lax.ppermute(sends[k], 'x', [(j, j ^ k) for j in range(X_DEV)])  12 us
    all_to_all x1, waiting for transfers between devices, shards(): part = lax.all_to_all(part, 'z', split_axis=0, concat_axis=0, tiled=True)  11.3 us
    ppermute x3, waiting for transfers between devices, swap(): return lax.ppermute(sends[k], 'x', [(j, j ^ k) for j in range(X_DEV)])  8.69 us
    all_to_all x1, starting transfers between devices, shards(): lax.all_to_all(everyone.reshape(16, 1, 128), experts, split_axis=0, conca...  7.69 us
    pallas_call x7, Pallas kernels, call(): pl.pallas_call(body, out_shape=outs, compiler_params=pltpu.CompilerParams...  7.04 us
    all_to_all x1, starting transfers between devices, shards(): lax.all_to_all(slot_grad, 'y', split_axis=0, concat_axis=0, tiled=True)  4.92 us
    all_to_all x1, waiting for transfers between devices, shards(): lax.all_to_all(everyone.reshape(16, 1, 128), experts, split_axis=0, conca...  3.78 us
  transfers between devices with their start and end apart: 7, of which 6 were waited for; matrix products, arithmetic and copies ran while one was open for 0% of the time, Pallas kernels for 8%

profile of v14, /device:TPU:12, one launch (start us, length us, event | category | flops | bytes accessed | tf_op | source)
XLA Modules:
  0.0 73.0 jit_solution(1943567331948135421)
XLA Ops:
  0.6 0.0 copy-start.5
  0.6 0.6 copy-done.5
  1.3 0.0 copy-start.1
  1.3 0.0 copy-start.2
  1.3 0.0 copy-start.4
  1.3 0.6 shard_map.89
  1.9 0.0 copy-start
  1.9 7.7 %all-to-all-start.1 = ((s32[16,1,128]{2,1,0:T(1,128)}), s32[16,1,128]{2,1,0:T(1,128)S(1)}, u32[]{:S(2)}, u32[]{:S(2)}) async-start(s32[16,1,128]{2,1,0:T(1,128)} %bitcast.11), calls=%async_computation.1 | async-start | bytes 16384 | tf_op jit(solution)/shard_map/all_to_all | solution.py:151
  9.6 0.0 copy-done.1
  9.6 0.0 copy-done.2
  9.6 0.0 copy-done.4
  9.6 0.6 shard_map.86.hidden
  10.2 0.0 copy-done
  10.3 0.0 copy-start.7
  10.3 1.7 %shard_map.87 = (bf16[128,2304]{1,0:T(8,128)(2,1)}, bf16[384,144]{1,0:T(8,128)(2,1)S(1)}) custom-call(bf16[144,288]{1,0:T(8,128)(2,1)S(1)} %shard_map.86.hidden, bf16[288,2048]{1,0:T(8,128)(2,1)S(1)} %bitcast.20), custom_call_target="tpu_custom_call" | custom-call | flops 301989888 | bytes 1963008 | tf_op jit(solution)/shard_map/pallas_call | solution.py:33
  11.9 3.8 %all-to-all-done.1 = s32[16,1,128]{2,1,0:T(1,128)S(1)} async-done(((s32[16,1,128]{2,1,0:T(1,128)}), s32[16,1,128]{2,1,0:T(1,128)S(1)}, u32[]{:S(2)}, u32[]{:S(2)}) %all-to-all-start.1) | async-done | bytes 8224 | tf_op jit(solution)/shard_map/all_to_all | solution.py:151
  15.7 4.9 %all-to-all-start = ((bf16[8,16,2304]{2,1,0:T(8,128)(2,1)}), bf16[8,16,2304]{2,1,0:T(8,128)(2,1)S(1)}, u32[]{:S(2)}, u32[]{:S(2)}) async-start(bf16[8,16,2304]{2,1,0:T(8,128)(2,1)} %bitcast.5), calls=%async_computation | async-start | bytes 1179648 | tf_op jit(solution)/shard_map/all_to_all | solution.py:170
  20.6 0.0 copy-done.7
  20.6 0.9 %shard_map.90 = (bf16[96,1536]{1,0:T(8,128)(2,1)S(1)}, bf16[96,1536]{1,0:T(8,128)(2,1)S(1)}, bf16[96,1536]{1,0:T(8,128)(2,1)S(1)}, bf16[96,1536]{1,0:T(8,128)(2,1)S(1)}) custom-call(bf16[384,144]{1,0:T(8,128)(2,1)S(1)} %get-tuple-element.11.spread, bf16[144,2048]{1,0:T(8,128)(2,1)S(1)} %bitcast.28, s32[16,128]{1,0:T(8,128)S(1)} %bitcast.25), custom_call_target="tpu_custom_call" | custom-call | flops 226492416 | bytes 1888256 | tf_op jit(solution)/shard_map/pallas_call | solution.py:33
  21.6 7.6 %collective-permute-start.1 = (bf16[96,1536]{1,0:T(8,128)(2,1)S(1)}, bf16[96,1536]{1,0:T(8,128)(2,1)S(1)}, u32[]{:S(2)}, u32[]{:S(2)}) collective-permute-start(bf16[96,1536]{1,0:T(8,128)(2,1)S(1)} %get-tuple-element.13), channel_id=1, source_target_pairs={{0,2},{1,3},{2,0},{3,1},{4,6},{5,7},{6,4},{7,5},{8,10},{9,11},{10,... | collective-permute-start | bytes 884744 | tf_op jit(solution)/shard_map/ppermute | solution.py:174
  29.2 1.9 %collective-permute-start.2 = (bf16[96,1536]{1,0:T(8,128)(2,1)S(1)}, bf16[96,1536]{1,0:T(8,128)(2,1)S(1)}, u32[]{:S(2)}, u32[]{:S(2)}) collective-permute-start(bf16[96,1536]{1,0:T(8,128)(2,1)S(1)} %get-tuple-element.14), channel_id=1, source_target_pairs={{0,1},{1,0},{2,3},{3,2},{4,5},{5,4},{6,7},{7,6},{8,9},{9,8},{10,11... | collective-permute-start | bytes 884744 | tf_op jit(solution)/shard_map/ppermute | solution.py:174
  31.1 2.5 %collective-permute-start.3 = (bf16[96,1536]{1,0:T(8,128)(2,1)S(1)}, bf16[96,1536]{1,0:T(8,128)(2,1)S(1)}, u32[]{:S(2)}, u32[]{:S(2)}) collective-permute-start(bf16[96,1536]{1,0:T(8,128)(2,1)S(1)} %get-tuple-element.15), channel_id=1, source_target_pairs={{0,3},{1,2},{2,1},{3,0},{4,7},{5,6},{6,5},{7,4},{8,11},{9,10},{10,... | collective-permute-start | bytes 884744 | tf_op jit(solution)/shard_map/ppermute | solution.py:174
  33.6 3.5 %collective-permute-done.1.two = bf16[96,1536]{1,0:T(8,128)(2,1)S(1)} collective-permute-done((bf16[96,1536]{1,0:T(8,128)(2,1)S(1)}, bf16[96,1536]{1,0:T(8,128)(2,1)S(1)}, u32[]{:S(2)}, u32[]{:S(2)}) %collective-permute-start.1) | collective-permute-done | bytes 294944 | tf_op jit(solution)/shard_map/ppermute | solution.py:174
  37.1 4.4 %collective-permute-done.2.one = bf16[96,1536]{1,0:T(8,128)(2,1)S(1)} collective-permute-done((bf16[96,1536]{1,0:T(8,128)(2,1)S(1)}, bf16[96,1536]{1,0:T(8,128)(2,1)S(1)}, u32[]{:S(2)}, u32[]{:S(2)}) %collective-permute-start.2) | collective-permute-done | bytes 294944 | tf_op jit(solution)/shard_map/ppermute | solution.py:174
  41.5 0.8 %collective-permute-done.3.three = bf16[96,1536]{1,0:T(8,128)(2,1)S(1)} collective-permute-done((bf16[96,1536]{1,0:T(8,128)(2,1)S(1)}, bf16[96,1536]{1,0:T(8,128)(2,1)S(1)}, u32[]{:S(2)}, u32[]{:S(2)}) %collective-permute-start.3) | collective-permute-done | bytes 294944 | tf_op jit(solution)/shard_map/ppermute | solution.py:174
  42.3 0.0 copy-start.3
  42.3 0.0 copy-start.6
  42.3 0.9 %shard_map.91 = bf16[96,1536]{1,0:T(8,128)(2,1)} custom-call(bf16[96,1536]{1,0:T(8,128)(2,1)S(1)} %get-tuple-element.12.own, bf16[96,1536]{1,0:T(8,128)(2,1)S(1)} %collective-permute-done.1.two, bf16[96,1536]{1,0:T(8,128)(2,1)S(1)} %collective-permute-done.2.one, bf16[96,1536]{1,0:T(8,128)(2,1)S(1)} %collective-permute-done.3.three), custom_call_target="tpu_custom_call" | custom-call | bytes 1474560 | tf_op jit(solution)/shard_map/pallas_call | solution.py:33
  43.2 0.0 all-to-all-done
  43.2 12.6 %all-to-all-start.2 = ((bf16[12,8,1536]{2,1,0:T(8,128)(2,1)}), bf16[12,8,1536]{2,1,0:T(8,128)(2,1)S(1)}, u32[]{:S(2)}, u32[]{:S(2)}) async-start(bf16[12,8,1536]{2,1,0:T(8,128)(2,1)} %bitcast.13), calls=%async_computation.2 | async-start | bytes 589824 | tf_op jit(solution)/shard_map/all_to_all | solution.py:177
  55.8 1.9 %collective-permute-start = (bf16[64,2304]{1,0:T(8,128)(2,1)S(1)}, bf16[64,2304]{1,0:T(8,128)(2,1)S(1)}, u32[]{:S(2)}, u32[]{:S(2)}) collective-permute-start(bf16[64,2304]{1,0:T(8,128)(2,1)S(1)} %slice_bitcast_fusion), channel_id=1, source_target_pairs={{0,48},{48,0},{1,49},{49,1},{2,50},{50,2},{3,51},{51,3},{4,52},{52... | collective-permute-start | bytes 884744 | tf_op jit(solution)/shard_map/ppermute | solution.py:172
  57.7 1.5 %collective-permute-done.far = bf16[64,2304]{1,0:T(8,128)(2,1)S(1)} collective-permute-done((bf16[64,2304]{1,0:T(8,128)(2,1)S(1)}, bf16[64,2304]{1,0:T(8,128)(2,1)S(1)}, u32[]{:S(2)}, u32[]{:S(2)}) %collective-permute-start) | collective-permute-done | bytes 294944 | tf_op jit(solution)/shard_map/ppermute | solution.py:172
  59.3 0.0 copy-done.3
  59.3 0.0 copy-done.6
  59.3 1.7 %shard_map.88 = bf16[128,2048]{1,0:T(8,128)(2,1)} custom-call(s32[1,128]{1,0:T(1,128)S(1)} %bitcast.27, bf16[128,2048]{1,0:T(8,128)(2,1)S(1)} %copy-done.3, bf16[128,2304]{1,0:T(8,128)(2,1)S(1)} %bitcast.19, bf16[64,2304]{1,0:T(8,128)(2,1)S(1)} %collective-permute-done.far), custom_call_target="tpu_custom_call" | custom-call | flops 201326592 | bytes 1933824 | tf_op jit(solution)/shard_map/pallas_call | solution.py:33
  61.0 11.3 %all-to-all-done.2 = bf16[12,8,1536]{2,1,0:T(8,128)(2,1)S(1)} async-done(((bf16[12,8,1536]{2,1,0:T(8,128)(2,1)}), bf16[12,8,1536]{2,1,0:T(8,128)(2,1)S(1)}, u32[]{:S(2)}, u32[]{:S(2)}) %all-to-all-start.2) | async-done | bytes 294944 | tf_op jit(solution)/shard_map/all_to_all | solution.py:177
  72.3 0.7 shard_map.92
  (1 shorter events, 0.0 us)
Async XLA Ops:
  0.6 0.7 copy-start.5
  1.3 8.3 %copy-start.1 = (bf16[1,288,2048]{2,1,0:T(8,128)(2,1)S(1)}, bf16[1,288,2048]{2,1,0:T(8,128)(2,1)}, u32[]{:S(2)}) copy-start(bf16[1,288,2048]{2,1,0:T(8,128)(2,1)} %param.13) | copy-start | bytes 3538948
  1.3 8.3 %copy-start.2 = (bf16[1,144,2048]{2,1,0:T(8,128)(2,1)S(1)}, bf16[1,144,2048]{2,1,0:T(8,128)(2,1)}, u32[]{:S(2)}) copy-start(bf16[1,144,2048]{2,1,0:T(8,128)(2,1)} %param.11) | copy-start | bytes 1769476
  1.3 8.3 %copy-start.4 = (bf16[1,144,288]{2,1,0:T(8,128)(2,1)S(1)}, bf16[1,144,288]{2,1,0:T(8,128)(2,1)}, u32[]{:S(2)}) copy-start(bf16[1,144,288]{2,1,0:T(8,128)(2,1)} %param.10) | copy-start | bytes 248836
  1.9 8.3 %copy-start = (bf16[1,288,2048]{2,1,0:T(8,128)(2,1)S(1)}, bf16[1,288,2048]{2,1,0:T(8,128)(2,1)}, u32[]{:S(2)}) copy-start(bf16[1,288,2048]{2,1,0:T(8,128)(2,1)} %param.12) | copy-start | bytes 3538948
  1.9 13.8 %all-to-all-start.1 = ((s32[16,1,128]{2,1,0:T(1,128)}), s32[16,1,128]{2,1,0:T(1,128)S(1)}, u32[]{:S(2)}, u32[]{:S(2)}) async-start(s32[16,1,128]{2,1,0:T(1,128)} %bitcast.11), calls=%async_computation.1 | async-start | bytes 16384 | tf_op jit(solution)/shard_map/all_to_all | solution.py:151
  10.3 10.4 %copy-start.7 = (bf16[1,144,2048]{2,1,0:T(8,128)(2,1)S(1)}, bf16[1,144,2048]{2,1,0:T(8,128)(2,1)}, u32[]{:S(2)}) copy-start(bf16[1,144,2048]{2,1,0:T(8,128)(2,1)} %param.9) | copy-start | bytes 1769476
  15.7 27.4 %all-to-all-start = ((bf16[8,16,2304]{2,1,0:T(8,128)(2,1)}), bf16[8,16,2304]{2,1,0:T(8,128)(2,1)S(1)}, u32[]{:S(2)}, u32[]{:S(2)}) async-start(bf16[8,16,2304]{2,1,0:T(8,128)(2,1)} %bitcast.5), calls=%async_computation | async-start | bytes 1179648 | tf_op jit(solution)/shard_map/all_to_all | solution.py:170
  21.6 15.5 %collective-permute-start.1 = (bf16[96,1536]{1,0:T(8,128)(2,1)S(1)}, bf16[96,1536]{1,0:T(8,128)(2,1)S(1)}, u32[]{:S(2)}, u32[]{:S(2)}) collective-permute-start(bf16[96,1536]{1,0:T(8,128)(2,1)S(1)} %get-tuple-element.13), channel_id=1, source_target_pairs={{0,2},{1,3},{2,0},{3,1},{4,6},{5,7},{6,4},{7,5},{8,10},{9,11},{10,... | collective-permute-start | bytes 884744 | tf_op jit(solution)/shard_map/ppermute | solution.py:174
  29.2 12.3 %collective-permute-start.2 = (bf16[96,1536]{1,0:T(8,128)(2,1)S(1)}, bf16[96,1536]{1,0:T(8,128)(2,1)S(1)}, u32[]{:S(2)}, u32[]{:S(2)}) collective-permute-start(bf16[96,1536]{1,0:T(8,128)(2,1)S(1)} %get-tuple-element.14), channel_id=1, source_target_pairs={{0,1},{1,0},{2,3},{3,2},{4,5},{5,4},{6,7},{7,6},{8,9},{9,8},{10,11... | collective-permute-start | bytes 884744 | tf_op jit(solution)/shard_map/ppermute | solution.py:174
  31.1 11.2 %collective-permute-start.3 = (bf16[96,1536]{1,0:T(8,128)(2,1)S(1)}, bf16[96,1536]{1,0:T(8,128)(2,1)S(1)}, u32[]{:S(2)}, u32[]{:S(2)}) collective-permute-start(bf16[96,1536]{1,0:T(8,128)(2,1)S(1)} %get-tuple-element.15), channel_id=1, source_target_pairs={{0,3},{1,2},{2,1},{3,0},{4,7},{5,6},{6,5},{7,4},{8,11},{9,10},{10,... | collective-permute-start | bytes 884744 | tf_op jit(solution)/shard_map/ppermute | solution.py:174
  42.3 17.0 %copy-start.3 = (bf16[128,2048]{1,0:T(8,128)(2,1)S(1)}, bf16[128,2048]{1,0:T(8,128)(2,1)}, u32[]{:S(2)}) copy-start(bf16[128,2048]{1,0:T(8,128)(2,1)} %residual.1) | copy-start | bytes 1572868
  42.3 17.0 %copy-start.6 = (s32[128,1]{0,1:T(1,128)S(1)}, s32[128,1]{0,1:T(1,128)}, u32[]{:S(2)}) copy-start(s32[128,1]{0,1:T(1,128)} %param.7) | copy-start | bytes 1540
  43.2 29.2 %all-to-all-start.2 = ((bf16[12,8,1536]{2,1,0:T(8,128)(2,1)}), bf16[12,8,1536]{2,1,0:T(8,128)(2,1)S(1)}, u32[]{:S(2)}, u32[]{:S(2)}) async-start(bf16[12,8,1536]{2,1,0:T(8,128)(2,1)} %bitcast.13), calls=%async_computation.2 | async-start | bytes 589824 | tf_op jit(solution)/shard_map/all_to_all | solution.py:177
  55.8 3.5 %collective-permute-start = (bf16[64,2304]{1,0:T(8,128)(2,1)S(1)}, bf16[64,2304]{1,0:T(8,128)(2,1)S(1)}, u32[]{:S(2)}, u32[]{:S(2)}) collective-permute-start(bf16[64,2304]{1,0:T(8,128)(2,1)S(1)} %slice_bitcast_fusion), channel_id=1, source_target_pairs={{0,48},{48,0},{1,49},{49,1},{2,50},{50,2},{3,51},{51,3},{4,52},{52... | collective-permute-start | bytes 884744 | tf_op jit(solution)/shard_map/ppermute | solution.py:172

commit v15 on v14

--- a/solution.py
+++ b/solution.py
@@ -103,9 +103,10 @@
 
 
 def sum_body(scale, parts, out):
-    total = parts[0:8, :].astype(F32)
-    for z in range(1, parts.shape[0] // 8):
-        total = total + parts[8 * z : 8 * z + 8, :].astype(F32)
+    every = parts[...].astype(F32)
+    total = every[0:8]
+    for z in range(1, every.shape[0] // 8):
+        total = total + every[8 * z : 8 * z + 8]
     total = total / scale
     for u in range(6):
         v, w = u // 3, u % 3

time: 73.6 us -> 73.6 us (level)
  the two profiles are of different devices: /device:TPU:12 before, /device:TPU:4 now
where the time goes in v15:
time: 73.6 us; the launch traced here: 73.2 us
  starting transfers between devices  37.5 us (51%)
  waiting for transfers between devices  27.1 us (37%)
  Pallas kernels  7.05 us (10%)
  between operations  0.77 us (1%)
    all_to_all x1, starting transfers between devices, shards(): part = lax.all_to_all(part, 'z', split_axis=0, concat_axis=0, tiled=True)  12.7 us
    ppermute x3, starting transfers between devices, swap(): return lax.ppermute(sends[k], 'x', [(j, j ^ k) for j in range(X_DEV)])  12 us
    all_to_all x1, waiting for transfers between devices, shards(): part = lax.all_to_all(part, 'z', split_axis=0, concat_axis=0, tiled=True)  11.5 us
    ppermute x3, waiting for transfers between devices, swap(): return lax.ppermute(sends[k], 'x', [(j, j ^ k) for j in range(X_DEV)])  8.91 us
    all_to_all x1, starting transfers between devices, shards(): lax.all_to_all(everyone.reshape(16, 1, 128), experts, split_axis=0, conca...  7.34 us
    pallas_call x7, Pallas kernels, call(): pl.pallas_call(body, out_shape=outs, compiler_params=pltpu.CompilerParams...  7.05 us
    all_to_all x1, waiting for transfers between devices, shards(): lax.all_to_all(everyone.reshape(16, 1, 128), experts, split_axis=0, conca...  5.15 us
    all_to_all x1, starting transfers between devices, shards(): lax.all_to_all(slot_grad, 'y', split_axis=0, concat_axis=0, tiled=True)  3.54 us
  transfers between devices with their start and end apart: 7, of which 6 were waited for; matrix products, arithmetic and copies ran while one was open for 0% of the time, Pallas kernels for 8%

profile of v15, /device:TPU:4, one launch (start us, length us, event | category | flops | bytes accessed | tf_op | source)
XLA Modules:
  0.0 73.2 jit_solution(6764732616559709800)
XLA Ops:
  0.6 0.0 copy-start.5
  0.6 0.6 copy-done.5
  1.3 0.0 copy-start.1
  1.3 0.0 copy-start.2
  1.3 0.0 copy-start.4
  1.3 0.6 shard_map.89
  1.9 0.0 copy-start
  1.9 7.3 %all-to-all-start.1 = ((s32[16,1,128]{2,1,0:T(1,128)}), s32[16,1,128]{2,1,0:T(1,128)S(1)}, u32[]{:S(2)}, u32[]{:S(2)}) async-start(s32[16,1,128]{2,1,0:T(1,128)} %bitcast.11), calls=%async_computation.1 | async-start | bytes 16384 | tf_op jit(solution)/shard_map/all_to_all | solution.py:152
  9.2 0.0 copy-done.1
  9.3 0.0 copy-done.2
  9.3 0.0 copy-done.4
  9.3 0.6 shard_map.86.hidden
  9.9 0.0 copy-done
  9.9 0.0 copy-start.7
  9.9 1.7 %shard_map.87 = (bf16[128,2304]{1,0:T(8,128)(2,1)}, bf16[384,144]{1,0:T(8,128)(2,1)S(1)}) custom-call(bf16[144,288]{1,0:T(8,128)(2,1)S(1)} %shard_map.86.hidden, bf16[288,2048]{1,0:T(8,128)(2,1)S(1)} %bitcast.20), custom_call_target="tpu_custom_call" | custom-call | flops 301989888 | bytes 1963008 | tf_op jit(solution)/shard_map/pallas_call | solution.py:33
  11.6 5.2 %all-to-all-done.1 = s32[16,1,128]{2,1,0:T(1,128)S(1)} async-done(((s32[16,1,128]{2,1,0:T(1,128)}), s32[16,1,128]{2,1,0:T(1,128)S(1)}, u32[]{:S(2)}, u32[]{:S(2)}) %all-to-all-start.1) | async-done | bytes 8224 | tf_op jit(solution)/shard_map/all_to_all | solution.py:152
  16.7 3.5 %all-to-all-start = ((bf16[8,16,2304]{2,1,0:T(8,128)(2,1)}), bf16[8,16,2304]{2,1,0:T(8,128)(2,1)S(1)}, u32[]{:S(2)}, u32[]{:S(2)}) async-start(bf16[8,16,2304]{2,1,0:T(8,128)(2,1)} %bitcast.5), calls=%async_computation | async-start | bytes 1179648 | tf_op jit(solution)/shard_map/all_to_all | solution.py:171
  20.3 0.0 copy-done.7
  20.3 0.9 %shard_map.90 = (bf16[96,1536]{1,0:T(8,128)(2,1)S(1)}, bf16[96,1536]{1,0:T(8,128)(2,1)S(1)}, bf16[96,1536]{1,0:T(8,128)(2,1)S(1)}, bf16[96,1536]{1,0:T(8,128)(2,1)S(1)}) custom-call(bf16[384,144]{1,0:T(8,128)(2,1)S(1)} %get-tuple-element.11.spread, bf16[144,2048]{1,0:T(8,128)(2,1)S(1)} %bitcast.28, s32[16,128]{1,0:T(8,128)S(1)} %bitcast.25), custom_call_target="tpu_custom_call" | custom-call | flops 226492416 | bytes 1888256 | tf_op jit(solution)/shard_map/pallas_call | solution.py:33
  21.2 7.6 %collective-permute-start.1 = (bf16[96,1536]{1,0:T(8,128)(2,1)S(1)}, bf16[96,1536]{1,0:T(8,128)(2,1)S(1)}, u32[]{:S(2)}, u32[]{:S(2)}) collective-permute-start(bf16[96,1536]{1,0:T(8,128)(2,1)S(1)} %get-tuple-element.13), channel_id=1, source_target_pairs={{0,2},{1,3},{2,0},{3,1},{4,6},{5,7},{6,4},{7,5},{8,10},{9,11},{10,... | collective-permute-start | bytes 884744 | tf_op jit(solution)/shard_map/ppermute | solution.py:175
  28.9 1.9 %collective-permute-start.2 = (bf16[96,1536]{1,0:T(8,128)(2,1)S(1)}, bf16[96,1536]{1,0:T(8,128)(2,1)S(1)}, u32[]{:S(2)}, u32[]{:S(2)}) collective-permute-start(bf16[96,1536]{1,0:T(8,128)(2,1)S(1)} %get-tuple-element.14), channel_id=1, source_target_pairs={{0,1},{1,0},{2,3},{3,2},{4,5},{5,4},{6,7},{7,6},{8,9},{9,8},{10,11... | collective-permute-start | bytes 884744 | tf_op jit(solution)/shard_map/ppermute | solution.py:175
  30.8 2.5 %collective-permute-start.3 = (bf16[96,1536]{1,0:T(8,128)(2,1)S(1)}, bf16[96,1536]{1,0:T(8,128)(2,1)S(1)}, u32[]{:S(2)}, u32[]{:S(2)}) collective-permute-start(bf16[96,1536]{1,0:T(8,128)(2,1)S(1)} %get-tuple-element.15), channel_id=1, source_target_pairs={{0,3},{1,2},{2,1},{3,0},{4,7},{5,6},{6,5},{7,4},{8,11},{9,10},{10,... | collective-permute-start | bytes 884744 | tf_op jit(solution)/shard_map/ppermute | solution.py:175
  33.3 3.4 %collective-permute-done.1.two = bf16[96,1536]{1,0:T(8,128)(2,1)S(1)} collective-permute-done((bf16[96,1536]{1,0:T(8,128)(2,1)S(1)}, bf16[96,1536]{1,0:T(8,128)(2,1)S(1)}, u32[]{:S(2)}, u32[]{:S(2)}) %collective-permute-start.1) | collective-permute-done | bytes 294944 | tf_op jit(solution)/shard_map/ppermute | solution.py:175
  36.7 4.7 %collective-permute-done.2.one = bf16[96,1536]{1,0:T(8,128)(2,1)S(1)} collective-permute-done((bf16[96,1536]{1,0:T(8,128)(2,1)S(1)}, bf16[96,1536]{1,0:T(8,128)(2,1)S(1)}, u32[]{:S(2)}, u32[]{:S(2)}) %collective-permute-start.2) | collective-permute-done | bytes 294944 | tf_op jit(solution)/shard_map/ppermute | solution.py:175
  41.4 0.7 %collective-permute-done.3.three = bf16[96,1536]{1,0:T(8,128)(2,1)S(1)} collective-permute-done((bf16[96,1536]{1,0:T(8,128)(2,1)S(1)}, bf16[96,1536]{1,0:T(8,128)(2,1)S(1)}, u32[]{:S(2)}, u32[]{:S(2)}) %collective-permute-start.3) | collective-permute-done | bytes 294944 | tf_op jit(solution)/shard_map/ppermute | solution.py:175
  42.2 0.0 copy-start.3
  42.2 0.0 copy-start.6
  42.2 0.9 %shard_map.91 = bf16[96,1536]{1,0:T(8,128)(2,1)} custom-call(bf16[96,1536]{1,0:T(8,128)(2,1)S(1)} %get-tuple-element.12.own, bf16[96,1536]{1,0:T(8,128)(2,1)S(1)} %collective-permute-done.1.two, bf16[96,1536]{1,0:T(8,128)(2,1)S(1)} %collective-permute-done.2.one, bf16[96,1536]{1,0:T(8,128)(2,1)S(1)} %collective-permute-done.3.three), custom_call_target="tpu_custom_call" | custom-call | bytes 1474560 | tf_op jit(solution)/shard_map/pallas_call | solution.py:33
  43.0 0.0 all-to-all-done
  43.0 12.7 %all-to-all-start.2 = ((bf16[12,8,1536]{2,1,0:T(8,128)(2,1)}), bf16[12,8,1536]{2,1,0:T(8,128)(2,1)S(1)}, u32[]{:S(2)}, u32[]{:S(2)}) async-start(bf16[12,8,1536]{2,1,0:T(8,128)(2,1)} %bitcast.13), calls=%async_computation.2 | async-start | bytes 589824 | tf_op jit(solution)/shard_map/all_to_all | solution.py:178
  55.8 1.9 %collective-permute-start = (bf16[64,2304]{1,0:T(8,128)(2,1)S(1)}, bf16[64,2304]{1,0:T(8,128)(2,1)S(1)}, u32[]{:S(2)}, u32[]{:S(2)}) collective-permute-start(bf16[64,2304]{1,0:T(8,128)(2,1)S(1)} %slice_bitcast_fusion), channel_id=1, source_target_pairs={{0,48},{48,0},{1,49},{49,1},{2,50},{50,2},{3,51},{51,3},{4,52},{52... | collective-permute-start | bytes 884744 | tf_op jit(solution)/shard_map/ppermute | solution.py:173
  57.7 1.5 %collective-permute-done.far = bf16[64,2304]{1,0:T(8,128)(2,1)S(1)} collective-permute-done((bf16[64,2304]{1,0:T(8,128)(2,1)S(1)}, bf16[64,2304]{1,0:T(8,128)(2,1)S(1)}, u32[]{:S(2)}, u32[]{:S(2)}) %collective-permute-start) | collective-permute-done | bytes 294944 | tf_op jit(solution)/shard_map/ppermute | solution.py:173
  59.2 0.0 copy-done.3
  59.2 0.0 copy-done.6
  59.2 1.7 %shard_map.88 = bf16[128,2048]{1,0:T(8,128)(2,1)} custom-call(s32[1,128]{1,0:T(1,128)S(1)} %bitcast.27, bf16[128,2048]{1,0:T(8,128)(2,1)S(1)} %copy-done.3, bf16[128,2304]{1,0:T(8,128)(2,1)S(1)} %bitcast.19, bf16[64,2304]{1,0:T(8,128)(2,1)S(1)} %collective-permute-done.far), custom_call_target="tpu_custom_call" | custom-call | flops 201326592 | bytes 1933824 | tf_op jit(solution)/shard_map/pallas_call | solution.py:33
  61.0 11.5 %all-to-all-done.2 = bf16[12,8,1536]{2,1,0:T(8,128)(2,1)S(1)} async-done(((bf16[12,8,1536]{2,1,0:T(8,128)(2,1)}), bf16[12,8,1536]{2,1,0:T(8,128)(2,1)S(1)}, u32[]{:S(2)}, u32[]{:S(2)}) %all-to-all-start.2) | async-done | bytes 294944 | tf_op jit(solution)/shard_map/all_to_all | solution.py:178
  72.5 0.7 shard_map.92
  (1 shorter events, 0.0 us)
Async XLA Ops:
  0.6 0.7 copy-start.5
  1.3 8.0 %copy-start.1 = (bf16[1,288,2048]{2,1,0:T(8,128)(2,1)S(1)}, bf16[1,288,2048]{2,1,0:T(8,128)(2,1)}, u32[]{:S(2)}) copy-start(bf16[1,288,2048]{2,1,0:T(8,128)(2,1)} %param.13) | copy-start | bytes 3538948
  1.3 8.0 %copy-start.2 = (bf16[1,144,2048]{2,1,0:T(8,128)(2,1)S(1)}, bf16[1,144,2048]{2,1,0:T(8,128)(2,1)}, u32[]{:S(2)}) copy-start(bf16[1,144,2048]{2,1,0:T(8,128)(2,1)} %param.11) | copy-start | bytes 1769476
  1.3 8.0 %copy-start.4 = (bf16[1,144,288]{2,1,0:T(8,128)(2,1)S(1)}, bf16[1,144,288]{2,1,0:T(8,128)(2,1)}, u32[]{:S(2)}) copy-start(bf16[1,144,288]{2,1,0:T(8,128)(2,1)} %param.10) | copy-start | bytes 248836
  1.9 8.0 %copy-start = (bf16[1,288,2048]{2,1,0:T(8,128)(2,1)S(1)}, bf16[1,288,2048]{2,1,0:T(8,128)(2,1)}, u32[]{:S(2)}) copy-start(bf16[1,288,2048]{2,1,0:T(8,128)(2,1)} %param.12) | copy-start | bytes 3538948
  1.9 14.8 %all-to-all-start.1 = ((s32[16,1,128]{2,1,0:T(1,128)}), s32[16,1,128]{2,1,0:T(1,128)S(1)}, u32[]{:S(2)}, u32[]{:S(2)}) async-start(s32[16,1,128]{2,1,0:T(1,128)} %bitcast.11), calls=%async_computation.1 | async-start | bytes 16384 | tf_op jit(solution)/shard_map/all_to_all | solution.py:152
  9.9 10.4 %copy-start.7 = (bf16[1,144,2048]{2,1,0:T(8,128)(2,1)S(1)}, bf16[1,144,2048]{2,1,0:T(8,128)(2,1)}, u32[]{:S(2)}) copy-start(bf16[1,144,2048]{2,1,0:T(8,128)(2,1)} %param.9) | copy-start | bytes 1769476
  16.7 26.3 %all-to-all-start = ((bf16[8,16,2304]{2,1,0:T(8,128)(2,1)}), bf16[8,16,2304]{2,1,0:T(8,128)(2,1)S(1)}, u32[]{:S(2)}, u32[]{:S(2)}) async-start(bf16[8,16,2304]{2,1,0:T(8,128)(2,1)} %bitcast.5), calls=%async_computation | async-start | bytes 1179648 | tf_op jit(solution)/shard_map/all_to_all | solution.py:171
  21.2 15.5 %collective-permute-start.1 = (bf16[96,1536]{1,0:T(8,128)(2,1)S(1)}, bf16[96,1536]{1,0:T(8,128)(2,1)S(1)}, u32[]{:S(2)}, u32[]{:S(2)}) collective-permute-start(bf16[96,1536]{1,0:T(8,128)(2,1)S(1)} %get-tuple-element.13), channel_id=1, source_target_pairs={{0,2},{1,3},{2,0},{3,1},{4,6},{5,7},{6,4},{7,5},{8,10},{9,11},{10,... | collective-permute-start | bytes 884744 | tf_op jit(solution)/shard_map/ppermute | solution.py:175
  28.9 12.6 %collective-permute-start.2 = (bf16[96,1536]{1,0:T(8,128)(2,1)S(1)}, bf16[96,1536]{1,0:T(8,128)(2,1)S(1)}, u32[]{:S(2)}, u32[]{:S(2)}) collective-permute-start(bf16[96,1536]{1,0:T(8,128)(2,1)S(1)} %get-tuple-element.14), channel_id=1, source_target_pairs={{0,1},{1,0},{2,3},{3,2},{4,5},{5,4},{6,7},{7,6},{8,9},{9,8},{10,11... | collective-permute-start | bytes 884744 | tf_op jit(solution)/shard_map/ppermute | solution.py:175
  30.8 11.4 %collective-permute-start.3 = (bf16[96,1536]{1,0:T(8,128)(2,1)S(1)}, bf16[96,1536]{1,0:T(8,128)(2,1)S(1)}, u32[]{:S(2)}, u32[]{:S(2)}) collective-permute-start(bf16[96,1536]{1,0:T(8,128)(2,1)S(1)} %get-tuple-element.15), channel_id=1, source_target_pairs={{0,3},{1,2},{2,1},{3,0},{4,7},{5,6},{6,5},{7,4},{8,11},{9,10},{10,... | collective-permute-start | bytes 884744 | tf_op jit(solution)/shard_map/ppermute | solution.py:175
  42.2 17.1 %copy-start.3 = (bf16[128,2048]{1,0:T(8,128)(2,1)S(1)}, bf16[128,2048]{1,0:T(8,128)(2,1)}, u32[]{:S(2)}) copy-start(bf16[128,2048]{1,0:T(8,128)(2,1)} %residual.1) | copy-start | bytes 1572868
  42.2 17.1 %copy-start.6 = (s32[128,1]{0,1:T(1,128)S(1)}, s32[128,1]{0,1:T(1,128)}, u32[]{:S(2)}) copy-start(s32[128,1]{0,1:T(1,128)} %param.7) | copy-start | bytes 1540
  43.0 29.4 %all-to-all-start.2 = ((bf16[12,8,1536]{2,1,0:T(8,128)(2,1)}), bf16[12,8,1536]{2,1,0:T(8,128)(2,1)S(1)}, u32[]{:S(2)}, u32[]{:S(2)}) async-start(bf16[12,8,1536]{2,1,0:T(8,128)(2,1)} %bitcast.13), calls=%async_computation.2 | async-start | bytes 589824 | tf_op jit(solution)/shard_map/all_to_all | solution.py:178
  55.8 3.5 %collective-permute-start = (bf16[64,2304]{1,0:T(8,128)(2,1)S(1)}, bf16[64,2304]{1,0:T(8,128)(2,1)S(1)}, u32[]{:S(2)}, u32[]{:S(2)}) collective-permute-start(bf16[64,2304]{1,0:T(8,128)(2,1)S(1)} %slice_bitcast_fusion), channel_id=1, source_target_pairs={{0,48},{48,0},{1,49},{49,1},{2,50},{50,2},{3,51},{51,3},{4,52},{52... | collective-permute-start | bytes 884744 | tf_op jit(solution)/shard_map/ppermute | solution.py:173

commit v16 on v15

--- a/solution.py
+++ b/solution.py
@@ -97,11 +97,6 @@
             out[:, span] = tile[m * k : m * k + m]
 
 
-def add_body(own, two, one, three, out):
-    total = (own[...].astype(F32) + two[...].astype(F32)) + (one[...].astype(F32) + three[...].astype(F32))
-    out[...] = total.astype(BF)
-
-
 def sum_body(scale, parts, out):
     every = parts[...].astype(F32)
     total = every[0:8]
@@ -174,7 +169,8 @@
     def swap(k):
         return lax.ppermute(sends[k], "x", [(j, j ^ k) for j in range(X_DEV)])
 
-    (part,) = call(add_body, [S((8 * Z_DEV, 1536), BF)], sends[0], swap(2), swap(1), swap(3))
+    two, one, three = [swap(k).astype(F32) for k in (2, 1, 3)]
+    part = ((sends[0].astype(F32) + two) + (one + three)).astype(BF)
     part = lax.all_to_all(part, "z", split_axis=0, concat_axis=0, tiled=True)
     (token_grad,) = call(
         token_body, [S((128, width), BF)], ids, residual_grad, near, far,

time: 73.6 us -> 73.6 us (level)
  other arithmetic: 0 us -> 0.88 us
  Pallas kernels: 7.05 us -> 6.2 us
    all_to_all x0 -> x1, other arithmetic: none -> 0.88 us  [shards(): part = lax.all_to_all(part, 'z', split_axis=0, concat_axis=0, tiled=True)]
    pallas_call x7 -> x6, Pallas kernels: 7.05 us -> 6.2 us  [call(): pl.pallas_call(body, out_shape=outs, compiler_params=pltpu.CompilerParams...]
  transfers between devices with their start and end apart: 7 -> 7, of which waited for: 6 -> 6; matrix products, arithmetic and copies ran while one was open for 0% -> 1% of each run, Pallas kernels for 8% -> 7%
where the time goes in v16:
time: 73.6 us; the launch traced here: 73.2 us
  starting transfers between devices  37.5 us (51%)
  waiting for transfers between devices  27.1 us (37%)
  Pallas kernels  6.2 us (8%)
  other arithmetic  0.88 us (1%)
  between operations  0.77 us (1%)
    all_to_all x1, starting transfers between devices, shards(): part = lax.all_to_all(part, 'z', split_axis=0, concat_axis=0, tiled=True)  12.7 us
    ppermute x3, starting transfers between devices, swap(): return lax.ppermute(sends[k], 'x', [(j, j ^ k) for j in range(X_DEV)])  12 us
    all_to_all x1, waiting for transfers between devices, shards(): part = lax.all_to_all(part, 'z', split_axis=0, concat_axis=0, tiled=True)  11.5 us
    ppermute x3, waiting for transfers between devices, swap(): return lax.ppermute(sends[k], 'x', [(j, j ^ k) for j in range(X_DEV)])  8.91 us
    all_to_all x1, starting transfers between devices, shards(): lax.all_to_all(everyone.reshape(16, 1, 128), experts, split_axis=0, conca...  7.34 us
    pallas_call x6, Pallas kernels, call(): pl.pallas_call(body, out_shape=outs, compiler_params=pltpu.CompilerParams...  6.2 us
    all_to_all x1, waiting for transfers between devices, shards(): lax.all_to_all(everyone.reshape(16, 1, 128), experts, split_axis=0, conca...  5.15 us
    all_to_all x1, starting transfers between devices, shards(): lax.all_to_all(slot_grad, 'y', split_axis=0, concat_axis=0, tiled=True)  3.54 us
  transfers between devices with their start and end apart: 7, of which 6 were waited for; matrix products, arithmetic and copies ran while one was open for 1% of the time, Pallas kernels for 7%

profile of v16, /device:TPU:4, one launch (start us, length us, event | category | flops | bytes accessed | tf_op | source)
XLA Modules:
  0.0 73.2 jit_solution(7662778119879727976)
XLA Ops:
  0.6 0.0 copy-start.5
  0.6 0.6 copy-done.5
  1.3 0.0 copy-start.1
  1.3 0.0 copy-start.2
  1.3 0.0 copy-start.4
  1.3 0.6 shard_map.89
  1.9 0.0 copy-start
  1.9 7.3 %all-to-all-start.1 = ((s32[16,1,128]{2,1,0:T(1,128)}), s32[16,1,128]{2,1,0:T(1,128)S(1)}, u32[]{:S(2)}, u32[]{:S(2)}) async-start(s32[16,1,128]{2,1,0:T(1,128)} %bitcast.11), calls=%async_computation.1 | async-start | bytes 16384 | tf_op jit(solution)/shard_map/all_to_all | solution.py:147
  9.2 0.0 copy-done.1
  9.3 0.0 copy-done.2
  9.3 0.0 copy-done.4
  9.3 0.6 shard_map.86.hidden
  9.9 0.0 copy-done
  9.9 0.0 copy-start.7
  9.9 1.7 %shard_map.87 = (bf16[128,2304]{1,0:T(8,128)(2,1)}, bf16[384,144]{1,0:T(8,128)(2,1)S(1)}) custom-call(bf16[144,288]{1,0:T(8,128)(2,1)S(1)} %shard_map.86.hidden, bf16[288,2048]{1,0:T(8,128)(2,1)S(1)} %bitcast.21), custom_call_target="tpu_custom_call" | custom-call | flops 301989888 | bytes 1963008 | tf_op jit(solution)/shard_map/pallas_call | solution.py:33
  11.6 5.2 %all-to-all-done.1 = s32[16,1,128]{2,1,0:T(1,128)S(1)} async-done(((s32[16,1,128]{2,1,0:T(1,128)}), s32[16,1,128]{2,1,0:T(1,128)S(1)}, u32[]{:S(2)}, u32[]{:S(2)}) %all-to-all-start.1) | async-done | bytes 8224 | tf_op jit(solution)/shard_map/all_to_all | solution.py:147
  16.7 3.5 %all-to-all-start = ((bf16[8,16,2304]{2,1,0:T(8,128)(2,1)}), bf16[8,16,2304]{2,1,0:T(8,128)(2,1)S(1)}, u32[]{:S(2)}, u32[]{:S(2)}) async-start(bf16[8,16,2304]{2,1,0:T(8,128)(2,1)} %bitcast.5), calls=%async_computation | async-start | bytes 1179648 | tf_op jit(solution)/shard_map/all_to_all | solution.py:166
  20.3 0.0 copy-done.7
  20.3 0.9 %shard_map.90 = (bf16[96,1536]{1,0:T(8,128)(2,1)S(1)}, bf16[96,1536]{1,0:T(8,128)(2,1)S(1)}, bf16[96,1536]{1,0:T(8,128)(2,1)S(1)}, bf16[96,1536]{1,0:T(8,128)(2,1)S(1)}) custom-call(bf16[384,144]{1,0:T(8,128)(2,1)S(1)} %get-tuple-element.11.spread, bf16[144,2048]{1,0:T(8,128)(2,1)S(1)} %bitcast.29, s32[16,128]{1,0:T(8,128)S(1)} %bitcast.26), custom_call_target="tpu_custom_call" | custom-call | flops 226492416 | bytes 1888256 | tf_op jit(solution)/shard_map/pallas_call | solution.py:33
  21.2 7.6 %collective-permute-start.1 = (bf16[96,1536]{1,0:T(8,128)(2,1)S(1)}, bf16[96,1536]{1,0:T(8,128)(2,1)S(1)}, u32[]{:S(2)}, u32[]{:S(2)}) collective-permute-start(bf16[96,1536]{1,0:T(8,128)(2,1)S(1)} %get-tuple-element.13), channel_id=1, source_target_pairs={{0,2},{1,3},{2,0},{3,1},{4,6},{5,7},{6,4},{7,5},{8,10},{9,11},{10,... | collective-permute-start | bytes 884744 | tf_op jit(solution)/shard_map/ppermute | solution.py:170
  28.9 1.9 %collective-permute-start.2 = (bf16[96,1536]{1,0:T(8,128)(2,1)S(1)}, bf16[96,1536]{1,0:T(8,128)(2,1)S(1)}, u32[]{:S(2)}, u32[]{:S(2)}) collective-permute-start(bf16[96,1536]{1,0:T(8,128)(2,1)S(1)} %get-tuple-element.14), channel_id=1, source_target_pairs={{0,1},{1,0},{2,3},{3,2},{4,5},{5,4},{6,7},{7,6},{8,9},{9,8},{10,11... | collective-permute-start | bytes 884744 | tf_op jit(solution)/shard_map/ppermute | solution.py:170
  30.8 2.5 %collective-permute-start.3 = (bf16[96,1536]{1,0:T(8,128)(2,1)S(1)}, bf16[96,1536]{1,0:T(8,128)(2,1)S(1)}, u32[]{:S(2)}, u32[]{:S(2)}) collective-permute-start(bf16[96,1536]{1,0:T(8,128)(2,1)S(1)} %get-tuple-element.15), channel_id=1, source_target_pairs={{0,3},{1,2},{2,1},{3,0},{4,7},{5,6},{6,5},{7,4},{8,11},{9,10},{10,... | collective-permute-start | bytes 884744 | tf_op jit(solution)/shard_map/ppermute | solution.py:170
  33.3 3.4 %collective-permute-done.1 = bf16[96,1536]{1,0:T(8,128)(2,1)S(1)} collective-permute-done((bf16[96,1536]{1,0:T(8,128)(2,1)S(1)}, bf16[96,1536]{1,0:T(8,128)(2,1)S(1)}, u32[]{:S(2)}, u32[]{:S(2)}) %collective-permute-start.1) | collective-permute-done | bytes 294944 | tf_op jit(solution)/shard_map/ppermute | solution.py:170
  36.7 4.7 %collective-permute-done.2 = bf16[96,1536]{1,0:T(8,128)(2,1)S(1)} collective-permute-done((bf16[96,1536]{1,0:T(8,128)(2,1)S(1)}, bf16[96,1536]{1,0:T(8,128)(2,1)S(1)}, u32[]{:S(2)}, u32[]{:S(2)}) %collective-permute-start.2) | collective-permute-done | bytes 294944 | tf_op jit(solution)/shard_map/ppermute | solution.py:170
  41.4 0.7 %collective-permute-done.3 = bf16[96,1536]{1,0:T(8,128)(2,1)S(1)} collective-permute-done((bf16[96,1536]{1,0:T(8,128)(2,1)S(1)}, bf16[96,1536]{1,0:T(8,128)(2,1)S(1)}, u32[]{:S(2)}, u32[]{:S(2)}) %collective-permute-start.3) | collective-permute-done | bytes 294944 | tf_op jit(solution)/shard_map/ppermute | solution.py:170
  42.2 0.0 copy-start.3
  42.2 0.0 copy-start.6
  42.2 0.9 %fusion = bf16[12,8,1536]{2,1,0:T(8,128)(2,1)} fusion(bf16[96,1536]{1,0:T(8,128)(2,1)S(1)} %collective-permute-done.3, bf16[96,1536]{1,0:T(8,128)(2,1)S(1)} %collective-permute-done.2, bf16[96,1536]{1,0:T(8,128)(2,1)S(1)} %collective-permute-done.1, bf16[96,1536]{1,0:T(8,128)(2,1)S(1)} %get-tuple-element.12), kind=kLoop, calls=%fused_computation.1 | loop fusion | flops 1179648 | bytes 1474560 | tf_op jit(solution)/shard_map/all_to_all | solution.py:174
  43.1 0.0 all-to-all-done
  43.1 12.7 %all-to-all-start.2 = ((bf16[12,8,1536]{2,1,0:T(8,128)(2,1)}), bf16[12,8,1536]{2,1,0:T(8,128)(2,1)S(1)}, u32[]{:S(2)}, u32[]{:S(2)}) async-start(bf16[12,8,1536]{2,1,0:T(8,128)(2,1)} %fusion), calls=%async_computation.2 | async-start | bytes 589824 | tf_op jit(solution)/shard_map/all_to_all | solution.py:174
  55.8 1.9 %collective-permute-start = (bf16[64,2304]{1,0:T(8,128)(2,1)S(1)}, bf16[64,2304]{1,0:T(8,128)(2,1)S(1)}, u32[]{:S(2)}, u32[]{:S(2)}) collective-permute-start(bf16[64,2304]{1,0:T(8,128)(2,1)S(1)} %slice_bitcast_fusion), channel_id=1, source_target_pairs={{0,48},{48,0},{1,49},{49,1},{2,50},{50,2},{3,51},{51,3},{4,52},{52... | collective-permute-start | bytes 884744 | tf_op jit(solution)/shard_map/ppermute | solution.py:168
  57.7 1.5 %collective-permute-done.far = bf16[64,2304]{1,0:T(8,128)(2,1)S(1)} collective-permute-done((bf16[64,2304]{1,0:T(8,128)(2,1)S(1)}, bf16[64,2304]{1,0:T(8,128)(2,1)S(1)}, u32[]{:S(2)}, u32[]{:S(2)}) %collective-permute-start) | collective-permute-done | bytes 294944 | tf_op jit(solution)/shard_map/ppermute | solution.py:168
  59.3 0.0 copy-done.3
  59.3 0.0 copy-done.6
  59.3 1.7 %shard_map.88 = bf16[128,2048]{1,0:T(8,128)(2,1)} custom-call(s32[1,128]{1,0:T(1,128)S(1)} %bitcast.28, bf16[128,2048]{1,0:T(8,128)(2,1)S(1)} %copy-done.3, bf16[128,2304]{1,0:T(8,128)(2,1)S(1)} %bitcast.20, bf16[64,2304]{1,0:T(8,128)(2,1)S(1)} %collective-permute-done.far), custom_call_target="tpu_custom_call" | custom-call | flops 201326592 | bytes 1933824 | tf_op jit(solution)/shard_map/pallas_call | solution.py:33
  61.0 11.5 %all-to-all-done.2 = bf16[12,8,1536]{2,1,0:T(8,128)(2,1)S(1)} async-done(((bf16[12,8,1536]{2,1,0:T(8,128)(2,1)}), bf16[12,8,1536]{2,1,0:T(8,128)(2,1)S(1)}, u32[]{:S(2)}, u32[]{:S(2)}) %all-to-all-start.2) | async-done | bytes 294944 | tf_op jit(solution)/shard_map/all_to_all | solution.py:174
  72.5 0.7 shard_map.91
  (1 shorter events, 0.0 us)
Async XLA Ops:
  0.6 0.7 copy-start.5
  1.3 8.0 %copy-start.1 = (bf16[1,288,2048]{2,1,0:T(8,128)(2,1)S(1)}, bf16[1,288,2048]{2,1,0:T(8,128)(2,1)}, u32[]{:S(2)}) copy-start(bf16[1,288,2048]{2,1,0:T(8,128)(2,1)} %param.13) | copy-start | bytes 3538948
  1.3 8.0 %copy-start.2 = (bf16[1,144,2048]{2,1,0:T(8,128)(2,1)S(1)}, bf16[1,144,2048]{2,1,0:T(8,128)(2,1)}, u32[]{:S(2)}) copy-start(bf16[1,144,2048]{2,1,0:T(8,128)(2,1)} %param.11) | copy-start | bytes 1769476
  1.3 8.0 %copy-start.4 = (bf16[1,144,288]{2,1,0:T(8,128)(2,1)S(1)}, bf16[1,144,288]{2,1,0:T(8,128)(2,1)}, u32[]{:S(2)}) copy-start(bf16[1,144,288]{2,1,0:T(8,128)(2,1)} %param.10) | copy-start | bytes 248836
  1.9 8.0 %copy-start = (bf16[1,288,2048]{2,1,0:T(8,128)(2,1)S(1)}, bf16[1,288,2048]{2,1,0:T(8,128)(2,1)}, u32[]{:S(2)}) copy-start(bf16[1,288,2048]{2,1,0:T(8,128)(2,1)} %param.12) | copy-start | bytes 3538948
  1.9 14.8 %all-to-all-start.1 = ((s32[16,1,128]{2,1,0:T(1,128)}), s32[16,1,128]{2,1,0:T(1,128)S(1)}, u32[]{:S(2)}, u32[]{:S(2)}) async-start(s32[16,1,128]{2,1,0:T(1,128)} %bitcast.11), calls=%async_computation.1 | async-start | bytes 16384 | tf_op jit(solution)/shard_map/all_to_all | solution.py:147
  9.9 10.4 %copy-start.7 = (bf16[1,144,2048]{2,1,0:T(8,128)(2,1)S(1)}, bf16[1,144,2048]{2,1,0:T(8,128)(2,1)}, u32[]{:S(2)}) copy-start(bf16[1,144,2048]{2,1,0:T(8,128)(2,1)} %param.9) | copy-start | bytes 1769476
  16.7 26.3 %all-to-all-start = ((bf16[8,16,2304]{2,1,0:T(8,128)(2,1)}), bf16[8,16,2304]{2,1,0:T(8,128)(2,1)S(1)}, u32[]{:S(2)}, u32[]{:S(2)}) async-start(bf16[8,16,2304]{2,1,0:T(8,128)(2,1)} %bitcast.5), calls=%async_computation | async-start | bytes 1179648 | tf_op jit(solution)/shard_map/all_to_all | solution.py:166
  21.2 15.5 %collective-permute-start.1 = (bf16[96,1536]{1,0:T(8,128)(2,1)S(1)}, bf16[96,1536]{1,0:T(8,128)(2,1)S(1)}, u32[]{:S(2)}, u32[]{:S(2)}) collective-permute-start(bf16[96,1536]{1,0:T(8,128)(2,1)S(1)} %get-tuple-element.13), channel_id=1, source_target_pairs={{0,2},{1,3},{2,0},{3,1},{4,6},{5,7},{6,4},{7,5},{8,10},{9,11},{10,... | collective-permute-start | bytes 884744 | tf_op jit(solution)/shard_map/ppermute | solution.py:170
  28.9 12.6 %collective-permute-start.2 = (bf16[96,1536]{1,0:T(8,128)(2,1)S(1)}, bf16[96,1536]{1,0:T(8,128)(2,1)S(1)}, u32[]{:S(2)}, u32[]{:S(2)}) collective-permute-start(bf16[96,1536]{1,0:T(8,128)(2,1)S(1)} %get-tuple-element.14), channel_id=1, source_target_pairs={{0,1},{1,0},{2,3},{3,2},{4,5},{5,4},{6,7},{7,6},{8,9},{9,8},{10,11... | collective-permute-start | bytes 884744 | tf_op jit(solution)/shard_map/ppermute | solution.py:170
  30.8 11.4 %collective-permute-start.3 = (bf16[96,1536]{1,0:T(8,128)(2,1)S(1)}, bf16[96,1536]{1,0:T(8,128)(2,1)S(1)}, u32[]{:S(2)}, u32[]{:S(2)}) collective-permute-start(bf16[96,1536]{1,0:T(8,128)(2,1)S(1)} %get-tuple-element.15), channel_id=1, source_target_pairs={{0,3},{1,2},{2,1},{3,0},{4,7},{5,6},{6,5},{7,4},{8,11},{9,10},{10,... | collective-permute-start | bytes 884744 | tf_op jit(solution)/shard_map/ppermute | solution.py:170
  42.2 17.1 %copy-start.3 = (bf16[128,2048]{1,0:T(8,128)(2,1)S(1)}, bf16[128,2048]{1,0:T(8,128)(2,1)}, u32[]{:S(2)}) copy-start(bf16[128,2048]{1,0:T(8,128)(2,1)} %residual.1) | copy-start | bytes 1572868
  42.2 17.1 %copy-start.6 = (s32[128,1]{0,1:T(1,128)S(1)}, s32[128,1]{0,1:T(1,128)}, u32[]{:S(2)}) copy-start(s32[128,1]{0,1:T(1,128)} %param.7) | copy-start | bytes 1540
  43.1 29.4 %all-to-all-start.2 = ((bf16[12,8,1536]{2,1,0:T(8,128)(2,1)}), bf16[12,8,1536]{2,1,0:T(8,128)(2,1)S(1)}, u32[]{:S(2)}, u32[]{:S(2)}) async-start(bf16[12,8,1536]{2,1,0:T(8,128)(2,1)} %fusion), calls=%async_computation.2 | async-start | bytes 589824 | tf_op jit(solution)/shard_map/all_to_all | solution.py:174
  55.8 3.5 %collective-permute-start = (bf16[64,2304]{1,0:T(8,128)(2,1)S(1)}, bf16[64,2304]{1,0:T(8,128)(2,1)S(1)}, u32[]{:S(2)}, u32[]{:S(2)}) collective-permute-start(bf16[64,2304]{1,0:T(8,128)(2,1)S(1)} %slice_bitcast_fusion), channel_id=1, source_target_pairs={{0,48},{48,0},{1,49},{49,1},{2,50},{50,2},{3,51},{51,3},{4,52},{52... | collective-permute-start | bytes 884744 | tf_op jit(solution)/shard_map/ppermute | solution.py:168
